TPU v7x, 128 devices: a whole 4x4x4 slice. The times are simulated.
128 devices in a mesh: along: 32 (over z, y, core), across: 4 (over x).
Axes of the slice: x: 4, y: 4, z: 4, core: 2. Of those that a mesh axis runs over, the one named last changes fastest.
Arguments:
- elevation: float32 [64, 512, 512], P(None, 'along', 'across'), may hold values from -6 to 6
- velocity_pot: float32 [64, 512, 512], P(None, 'along', 'across'), may hold values from -6 to 6
- surface_coef: float32 [512, 512], P('along', 'across'), may hold values from 0.1 to 1
- panel_slot: int32 [512, 512], P('along', 'across'), may hold values from 0 to 262143, as said below
- near_blocks: bfloat16 [1024, 9, 256, 256], P(('along', 'across')), may hold values from -0.125 to 0.125
- near_cols: int32 [1024, 9], P(('along', 'across')), may hold values from 0 to 1023, as said below
- far_v: bfloat16 [16384, 32, 256], P(('along', 'across')), may hold values from -0.375 to 0.375
- far_u: bfloat16 [16384, 32, 256], P(('along', 'across')), may hold values from -0.25 to 0.25
- far_rows: int32 [16384], P(('along', 'across')), may hold values from 0 to 1023, as said below
- far_cols: int32 [16384], P(('along', 'across')), may hold values from 0 to 1023, as said below
Outputs:
- eta_next: float32 [64, 512, 512], P(None, 'along', 'across')
- potential: bfloat16 [64, 512, 512], P(None, 'along', 'across')
Inputs may be any that keep to these rules, and one draw needn't show every extreme that they name: `panel_slot`: A permutation of the positions; cluster c spans positions c * 256 to c * 256 + 255 and belongs to device c // 8 (devices numbered along-major). The panels of each device's tile take exactly 16 positions in each device's range. `near_cols`: entry k = 0 is the row cluster itself; the others are distinct clusters whose index differs from the row's by at most 8 modulo 1024. Pair p's column cluster is owned by the device holding pair p: far_cols[p] // 8 == p // 128. `far_rows`: of the pairs held by one device, at most 2 have row clusters owned by any one device, and in every draw some device receives exactly 2 from every sender; some devices receive none.
All inputs are finite; a program needn't handle non-finite values.
Results may differ from a plain program's by a relative error of at most 0.0058.
Values may be sent and summed in bfloat16 or wider, within the bound.
No kernel may reach another device: no remote copies, remote signals or barrier semaphores. Data moves between devices by JAX's collectives and lax.ppermute only.
A program may use at most 128 MiB of HBM per device.

v0:
```python
import functools

import jax
import jax.numpy as jnp
from jax import lax
from jax.experimental import pallas as pl
from jax.experimental.pallas import tpu as pltpu
from jax.sharding import PartitionSpec as P

CL = 256
BOTH = ("along", "across")
OWNERS = 128
PAIRS = 128
RANK = 32
WAVES = 64
ROWS = 1024
PANELS = 2048
BF16 = jnp.bfloat16
F32 = jnp.float32
VMEM = pl.BlockSpec(memory_space=pltpu.VMEM)
SMEM = pl.BlockSpec(memory_space=pltpu.SMEM)


def call(kernel, out_shape, in_specs, out_specs, scratch=(), limit=48, cost=0):
    return pl.pallas_call(
        kernel,
        out_shape=out_shape,
        in_specs=in_specs,
        out_specs=out_specs,
        scratch_shapes=list(scratch),
        compiler_params=pltpu.CompilerParams(vmem_limit_bytes=limit * 2**20),
        cost_estimate=pl.CostEstimate(flops=0, bytes_accessed=cost, transcendentals=0),
    )


def iota(shape, dim):
    return lax.broadcasted_iota(jnp.int32, shape, dim)


def dot(a, b):
    return jnp.dot(a, b, preferred_element_type=F32)


def dot_nt(a, b):
    return lax.dot_general(a, b, (((1,), (1,)), ((), ())), preferred_element_type=F32)


def bucket_kernel(rows_ref, u_ref, out_ref, pick_ref, count):
    def clear(i, c):
        pick_ref[i] = PAIRS
        pick_ref[OWNERS + i] = PAIRS
        count[i] = 0
        return c

    lax.fori_loop(0, OWNERS, clear, 0, unroll=8)
    out_ref[...] = jnp.zeros_like(out_ref)

    def put(p, c):
        target = rows_ref[p] // 8
        slot = count[target]
        count[target] = slot + 1
        pick_ref[slot * OWNERS + target] = p
        out_ref[target, slot] = u_ref[p]
        return c

    lax.fori_loop(0, PAIRS, put, 0, unroll=4)


def far_bucket(far_rows, far_u):
    return call(
        bucket_kernel,
        (
            jax.ShapeDtypeStruct((OWNERS, 2, RANK, CL), BF16),
            jax.ShapeDtypeStruct((2 * OWNERS,), jnp.int32),
        ),
        [SMEM, VMEM],
        (VMEM, SMEM),
        [pltpu.SMEM((OWNERS,), jnp.int32)],
    )(far_rows, far_u)


def order_kernel(slot_ref, hot_ref, place_ref):
    strict = (iota((128, 128), 0) < iota((128, 128), 1)).astype(BF16)
    weights = jnp.concatenate([strict, jnp.ones((128, 128), BF16)], axis=1)
    seen = jnp.zeros((128, 128), F32)
    for x in range(16):
        slot = slot_ref[x : x + 1, :]
        dest, local = slot >> 11, slot & (PANELS - 1)
        hits = iota((128, 128), 0) == dest
        sums = dot(hits.astype(BF16), weights)
        rank = jnp.sum(jnp.where(hits, sums[:, :128] + seen, 0.0), axis=0, keepdims=True)
        seen = seen + sums[:, 128:]
        rank = rank.astype(jnp.int32)
        row = dest * 8 + (rank & 7)
        lanes = pl.ds(x * 128, 128)
        hot_ref[:, lanes] = (iota((ROWS, 128), 0) == row).astype(F32).astype(BF16)
        place_ref[0:1, lanes] = rank >> 3
        place_ref[1:2, lanes] = local >> 7
        place_ref[2:3, lanes] = local & 127
        place_ref[3:8, lanes] = jnp.zeros((5, 128), jnp.int32)


def sender_order(panel_slot):
    return call(
        order_kernel,
        (
            jax.ShapeDtypeStruct((ROWS, PANELS), BF16),
            jax.ShapeDtypeStruct((8, PANELS), jnp.int32),
        ),
        [VMEM],
        (VMEM, VMEM),
    )(panel_slot)


def payload_kernel(source_ref, hot_ref, place_ref, rows_ref, out_ref, stack):
    stack[...] = jnp.zeros_like(stack)
    for x in range(16):
        lanes = pl.ds(x * 128, 128)
        place = place_ref[:, lanes]
        second = place[0:1] == 1
        values = source_ref[:, x, :]
        stack[0:64, lanes] = jnp.where(second, 0.0, values).astype(BF16)
        stack[64:128, lanes] = jnp.where(second, values, 0.0).astype(BF16)
        high, low = place[1:2].astype(F32), place[2:3].astype(F32)
        notes = [
            jnp.where(second, 0.0, high),
            jnp.where(second, 0.0, low),
            jnp.where(second, high, 0.0),
            jnp.where(second, low, 0.0),
            jnp.zeros((12, 128), F32),
        ]
        stack[128:144, lanes] = jnp.concatenate(notes, axis=0).astype(BF16)
    rows = rows_ref[...].astype(F32)
    own = jnp.concatenate([jnp.zeros((4, 128), F32), rows, jnp.zeros((10, 128), F32)], axis=0)
    stack[128:144, pl.ds(PANELS, 128)] = own.astype(BF16)
    for m in range(0, ROWS, 256):
        left = hot_ref[pl.ds(m, 256), :]
        owner = ((iota((256, 128), 0) + m) >> 3) == iota((256, 128), 1)
        values = dot_nt(left, stack[:, pl.ds(0, PANELS)])
        values += dot_nt(owner.astype(F32).astype(BF16), stack[:, pl.ds(PANELS, 128)])
        out_ref[pl.ds(m, 256), :] = values.astype(BF16)


def source_payload(source, hot, place, rows):
    return call(
        payload_kernel,
        jax.ShapeDtypeStruct((ROWS, 256), BF16),
        [VMEM] * 4,
        VMEM,
        [pltpu.VMEM((256, PANELS + 128), BF16)],
    )(source, hot, place, rows)


def cluster_kernel(
    pick_ref, col_ref, arrived_ref, v_ref, clustered_ref, hot_ref, info_ref, c_ref, left, coeff
):
    for m in range(0, ROWS, 128):
        lanes = pl.ds(m, 128)
        values = arrived_ref[lanes, 0:128].astype(F32).T
        notes = arrived_ref[lanes, 128:256].astype(F32).T
        for half in range(2):
            slot = (notes[2 * half : 2 * half + 1] * 128.0 + notes[2 * half + 1 : 2 * half + 2])
            slot = slot.astype(jnp.int32)
            upper = slot >= 1024
            mine = values[half * 64 : half * 64 + 64]
            at = pl.ds(half * ROWS + m, 128)
            left[0:64, at] = jnp.where(upper, 0.0, mine).astype(BF16)
            left[64:128, at] = jnp.where(upper, mine, 0.0).astype(BF16)
            hot = iota((1024, 128), 0) == (slot & 1023)
            hot_ref[:, at] = hot.astype(F32).astype(BF16)
            info_ref[half : half + 1, lanes] = upper.astype(F32)
        info_ref[2:4, lanes] = notes[4:6]
        info_ref[4:8, lanes] = jnp.zeros((4, 128), F32)
    for q in range(4):
        got = dot_nt(left[...], hot_ref[pl.ds(q * 256, 256), :]).astype(BF16)
        clustered_ref[q] = got[0:64]
        clustered_ref[4 + q] = got[64:128]
    for q in range(4):
        pair = jnp.concatenate([clustered_ref[2 * q], clustered_ref[2 * q + 1]], axis=0)
        for m in range(0, PAIRS, 16):
            rows = v_ref[pl.ds(m, 16)].reshape(16 * RANK, CL)
            coeff[q, pl.ds(m * RANK, 16 * RANK), :] = dot_nt(rows, pair)
    lane = iota((RANK, 128), 1)

    def put(t, c):
        both = []
        for s in range(2):
            p = pick_ref[s * OWNERS + t]
            held = p < PAIRS
            p = jnp.minimum(p, PAIRS - 1)
            col = col_ref[p] & 7
            tile = coeff[col >> 1, pl.ds(pl.multiple_of(p * RANK, RANK), RANK), :]
            tile = jnp.where((col & 1) == s, tile, pltpu.roll(tile, 64, 1))
            both.append(jnp.where(held, tile, 0.0))
        c_ref[t] = jnp.where(lane < 64, both[0], both[1]).astype(BF16)
        return c

    lax.fori_loop(0, OWNERS, put, 0, unroll=4)


def cluster_and_coeff(pick, cols, arrived, far_v):
    return call(
        cluster_kernel,
        (
            jax.ShapeDtypeStruct((8, WAVES, CL), BF16),
            jax.ShapeDtypeStruct((1024, PANELS), BF16),
            jax.ShapeDtypeStruct((8, ROWS), F32),
            jax.ShapeDtypeStruct((OWNERS, RANK, 2 * WAVES), BF16),
        ),
        [SMEM, SMEM, VMEM, VMEM],
        (VMEM,) * 4,
        [pltpu.VMEM((128, PANELS), BF16), pltpu.VMEM((4, PAIRS * RANK, 128), F32)],
    )(pick, cols, arrived, far_v)


def near_kernel(rel_ref, before_ref, own_ref, after_ref, blocks_ref, out_ref, wide):
    c = pl.program_id(0)

    @pl.when(c == 0)
    def _():
        wide[0:8] = before_ref[...]
        wide[8:16] = own_ref[...]
        wide[16:24] = after_ref[...]

    total = jnp.zeros((WAVES, CL), F32)
    for k in range(9):
        total += dot_nt(wide[rel_ref[c * 9 + k]], blocks_ref[0, k])
    out_ref[0] = total


def near_product(relative, before, own, after, near_blocks):
    whole = pl.BlockSpec((8, WAVES, CL), lambda c, r: (0, 0, 0))
    return pl.pallas_call(
        near_kernel,
        out_shape=jax.ShapeDtypeStruct((8, WAVES, CL), F32),
        grid_spec=pltpu.PrefetchScalarGridSpec(
            num_scalar_prefetch=1,
            grid=(8,),
            in_specs=[
                whole,
                whole,
                whole,
                pl.BlockSpec((1, 9, CL, CL), lambda c, r: (c, 0, 0, 0)),
            ],
            out_specs=pl.BlockSpec((1, WAVES, CL), lambda c, r: (c, 0, 0)),
            scratch_shapes=[pltpu.VMEM((24, WAVES, CL), BF16)],
        ),
        compiler_params=pltpu.CompilerParams(vmem_limit_bytes=32 * 2**20),
        cost_estimate=pl.CostEstimate(flops=0, bytes_accessed=0, transcendentals=0),
    )(relative, before, own, after, near_blocks)


def total_kernel(c_ref, u_ref, near_ref, hot_ref, info_ref, out_ref, acc, masked, grid):
    acc[...] = jnp.zeros_like(acc)
    spread = ((iota((128, 512), 0) >> 3) == (iota((128, 512), 1) >> 5)) & (
        (iota((128, 512), 0) & 7) == 0
    )
    spread = spread.astype(F32).astype(BF16)

    def chunk(m, c):
        src = pl.ds(m * 16, 16)
        rows = dot(info_ref[:, pl.ds(pl.multiple_of(m * 128, 128), 128)].astype(BF16), spread)
        turned = c_ref[src].reshape(512, 128).astype(F32).T
        for s in range(2):
            row = rows[2 + s : 3 + s]
            mine = turned[s * 64 : s * 64 + 64]
            for cluster in range(8):
                masked[pl.ds(cluster * 64, 64), :] = jnp.where(
                    row == float(cluster), mine, 0.0
                ).astype(BF16)
            acc[...] += dot(masked[...], u_ref[src, s].reshape(512, CL))
        return c

    lax.fori_loop(0, 8, chunk, 0)
    for cluster in range(8):
        total = near_ref[cluster] + acc[pl.ds(cluster * 64, 64), :]
        grid[pl.ds((cluster >> 2) * 64, 64), pl.ds((cluster & 3) * 256, 256)] = total.astype(BF16)
    for m in range(0, ROWS, 256):
        halves = []
        for half in range(2):
            got = dot(grid[...], hot_ref[:, pl.ds(half * ROWS + m, 256)])
            upper = info_ref[half : half + 1, pl.ds(m, 256)] == 1.0
            halves.append(jnp.where(upper, got[64:128], got[0:64]))
        out_ref[pl.ds(m, 256), :] = jnp.concatenate(halves, axis=0).T.astype(BF16)


def total_home(c_in, u_in, near, hot, info):
    return call(
        total_kernel,
        jax.ShapeDtypeStruct((ROWS, 128), BF16),
        [VMEM] * 5,
        VMEM,
        [
            pltpu.VMEM((512, CL), F32),
            pltpu.VMEM((512, 512), BF16),
            pltpu.VMEM((128, 1024), BF16),
        ],
    )(c_in, u_in, near, hot, info)


def potential_kernel(returned_ref, hot_ref, place_ref, out_ref, turned, wide):
    for m in range(0, ROWS, 128):
        turned[:, pl.ds(m, 128)] = returned_ref[pl.ds(m, 128), :].astype(F32).T.astype(BF16)
    for x in range(0, 16, 2):
        lanes = pl.ds(x * 128, 256)
        got = dot(turned[...], hot_ref[:, lanes])
        got = jnp.where(place_ref[0:1, lanes] == 1, got[64:128], got[0:64])
        wide[:, x, :] = got[:, :128]
        wide[:, x + 1, :] = got[:, 128:]
    out_ref[...] = wide[...].astype(BF16)


def panel_potential(returned, hot, place):
    return call(
        potential_kernel,
        jax.ShapeDtypeStruct((WAVES, 16, 128), BF16),
        [VMEM] * 3,
        VMEM,
        [pltpu.VMEM((128, ROWS), BF16), pltpu.VMEM((WAVES, 16, 128), F32)],
    )(returned, hot, place)


def halo(elevation, velocity_pot):
    n, m = lax.axis_size("along"), lax.axis_size("across")
    down = [(i, i + 1) for i in range(n - 1)]
    up = [(i + 1, i) for i in range(n - 1)]
    right = [(i, i + 1) for i in range(m - 1)]
    left = [(i + 1, i) for i in range(m - 1)]
    both = jnp.stack([elevation, velocity_pot])
    above = lax.ppermute(both[:, :, -2:, :], "along", down)
    below = lax.ppermute(velocity_pot[:, :1, :], "along", up)
    west = lax.ppermute(both[:, :, :, -2:], "across", right)
    east = lax.ppermute(both[:, :, :, :2], "across", left)
    return above, below, west, east


def surface_step(elevation, velocity_pot, coef, above, below, west, east):
    def up_x(f, a):
        g = jnp.concatenate([a, f], axis=1)
        return 0.5 * (3.0 * f - 4.0 * g[:, 1:-1] + g[:, :-2])

    def trans(f, w, e):
        g = jnp.concatenate([w, f, e], axis=2)
        return (g[:, :, :-4] - 8.0 * g[:, :, 1:-3] + 8.0 * g[:, :, 3:-1] - g[:, :, 4:]) / 12.0

    gx = jnp.concatenate([above[1][:, 1:], velocity_pot, below], axis=1)
    gy = jnp.concatenate([west[1][:, :, 1:], velocity_pot, east[1][:, :, :1]], axis=2)
    curv = gx[:, 2:] + gx[:, :-2] + gy[:, :, 2:] + gy[:, :, :-2] - 4.0 * velocity_pot
    eta = (
        elevation
        - 0.4 * up_x(elevation, above[0])
        + 0.3 * trans(elevation, west[0], east[0])
        + coef * curv
    )
    source = (
        velocity_pot
        - 0.4 * up_x(velocity_pot, above[1])
        + 0.3 * trans(velocity_pot, west[1], east[1])
        - 0.5 * eta
    )
    return eta, source


def exchange(x):
    return lax.all_to_all(x, BOTH, split_axis=0, concat_axis=0, tiled=True)


def body(
    elevation,
    velocity_pot,
    surface_coef,
    panel_slot,
    near_blocks,
    near_cols,
    far_v,
    far_u,
    far_rows,
    far_cols,
):
    per_owner, clusters = 8, 1024
    me = lax.axis_index(BOTH)

    u_out, pick = far_bucket(far_rows, far_u)
    u_in = exchange(u_out)

    padded_rows = jnp.concatenate([far_rows % 8, jnp.full((1,), 8, jnp.int32)])
    slot_rows = padded_rows[pick].reshape(2, OWNERS)
    above, below, west, east = halo(elevation, velocity_pot)
    hot, place = sender_order(panel_slot)
    eta, source = surface_step(elevation, velocity_pot, surface_coef, above, below, west, east)
    payload = source_payload(source, hot, place, slot_rows).reshape(OWNERS, 8, 256)
    payload, u_in = lax.optimization_barrier((payload, u_in))
    arrived = exchange(payload).reshape(ROWS, 256)

    clustered, unhot, info, c_out = cluster_and_coeff(pick, far_cols, arrived, far_v)
    c_in = exchange(c_out)

    ring = [(i, (i + 1) % OWNERS) for i in range(OWNERS)]
    back = [(j, i) for i, j in ring]
    before = lax.ppermute(clustered, BOTH, ring)
    after = lax.ppermute(clustered, BOTH, back)
    relative = (near_cols - (me * per_owner - per_owner)) % clusters
    near = near_product(relative.reshape(72), before, clustered, after, near_blocks)

    home = total_home(c_in, u_in, near, unhot, info).reshape(OWNERS, 8, 128)
    returned = exchange(home).reshape(ROWS, 128)
    potential = panel_potential(returned, hot, place)
    return (eta, potential)


def solution(mesh):
    in_specs = (
        P(None, "along", "across"),
        P(None, "along", "across"),
        P("along", "across"),
        P("along", "across"),
        P(BOTH, None, None, None),
        P(BOTH, None),
        P(BOTH, None, None),
        P(BOTH, None, None),
        P(BOTH),
        P(BOTH),
    )
    out_specs = (P(None, "along", "across"), P(None, "along", "across"))
    return jax.shard_map(body, mesh=mesh, in_specs=in_specs, out_specs=out_specs, check_vma=False)
```

profile of v0, /device:TPU:1, one launch (start us, length us, event | category | flops | bytes accessed | tf_op | source)
XLA Modules:
  0.0 170.4 jit_solution(11943429724668090763)
XLA Ops:
  0.6 1.6 copy-done.4
  2.2 0.7 copy-done.7
  2.9 4.3 %shard_map.113 = (bf16[128,2,32,256]{3,2,1,0:T(8,128)(2,1)}, s32[256]{0:T(256)S(1)}) custom-call(s32[128]{0:T(128)S(1)} %copy-done.7, bf16[128,32,256]{2,1,0:T(8,128)(2,1)S(1)} %copy-done.4), custom_call_target="tpu_custom_call" | custom-call | tf_op jit(solution)/shard_map/pallas_call | solution.py:70
  7.2 0.0 copy-start.10
  7.2 0.0 copy-start.11
  7.3 12.0 %all-to-all-start = ((bf16[128,2,32,256]{3,2,1,0:T(8,128)(2,1)}), bf16[128,2,32,256]{3,2,1,0:T(8,128)(2,1)}, u32[]{:S(2)}, u32[]{:S(2)}) async-start(bf16[128,2,32,256]{3,2,1,0:T(8,128)(2,1)} %get-tuple-element.15), calls=%async_computation | async-start | bytes 8388608 | tf_op jit(solution)/shard_map/all_to_all | solution.py:365
  19.2 0.0 copy-start.8
  19.2 0.0 copy-start.6
  19.3 0.1 pad_maximum_fusion.11
  19.3 3.5 %collective-permute-start = (f32[2,64,2,128]{3,2,1,0:T(2,128)S(1)}, f32[2,64,2,128]{3,2,1,0:T(2,128)S(1)}, u32[]{:S(2)}, u32[]{:S(2)}) collective-permute-start(f32[2,64,2,128]{3,2,1,0:T(2,128)S(1)} %pad_maximum_fusion.11), channel_id=1, source_target_pairs={{0,4},{4,8},{8,12},{12,16},{16,20},{20,24},{24,28},{28,32},{32,36}... | collective-permute-start | bytes 393224 | tf_op jit(solution)/shard_map/ppermute | solution.py:330
  22.9 0.3 slice_maximum_fusion
  23.2 0.5 copy.14
  23.7 1.3 collective-permute-start.2
  25.0 0.5 copy.12
  25.4 4.0 %collective-permute-start.1 = (f32[2,64,16,2]{1,2,3,0:T(8,128)S(1)}, f32[2,64,16,2]{1,2,3,0:T(8,128)S(1)}, u32[]{:S(2)}, u32[]{:S(2)}) collective-permute-start(f32[2,64,16,2]{1,2,3,0:T(8,128)S(1)} %copy.12), channel_id=1, source_target_pairs={{0,1},{1,2},{2,3},{4,5},{5,6},{6,7},{8,9},{9,10},{10,11},{12,13},{... | collective-permute-start | bytes 49160 | tf_op jit(solution)/shard_map/ppermute | solution.py:332
  29.4 0.6 slice.114
  30.1 1.9 %collective-permute-start.3 = (f32[64,1,128]{2,1,0:T(1,128)}, f32[64,1,128]{2,1,0:T(1,128)S(1)}, u32[]{:S(2)}, u32[]{:S(2)}) collective-permute-start(f32[64,1,128]{2,1,0:T(1,128)} %slice.114), channel_id=1, source_target_pairs={{4,0},{8,4},{12,8},{16,12},{20,16},{24,20},{28,24},{32,28},{36,32}... | collective-permute-start | bytes 98312 | tf_op jit(solution)/shard_map/ppermute | solution.py:331
  32.0 0.0 copy-done.8
  32.1 3.0 %shard_map.114 = (bf16[1024,2048]{1,0:T(8,128)(2,1)S(1)}, s32[8,2048]{1,0:T(8,128)S(1)}) custom-call(s32[16,128]{1,0:T(8,128)S(1)} %copy-done.6), custom_call_target="tpu_custom_call" | custom-call | tf_op jit(solution)/shard_map/pallas_call | solution.py:104
  35.1 2.0 %copy-done = bf16[1024,2048]{1,0:T(8,128)(2,1)} copy-done((bf16[1024,2048]{1,0:T(8,128)(2,1)}, bf16[1024,2048]{1,0:T(8,128)(2,1)S(1)}, u32[]{:S(2)}) %copy-start) | copy-done | bytes 4194328
  37.0 1.9 %gather_fusion = s32[256]{0:T(256)S(1)} fusion(s32[129]{0:T(256)S(1)} %pad_add_fusion, s32[1024]{0:T(1024)S(1)} %pad_clamp_fusion), kind=kCustom, calls=%fused_computation | custom fusion | bytes 3072 | tf_op jit(solution)/shard_map/gather | solution.py:387
  39.0 27.0 %collective-permute-done.2 = f32[2,64,16,2]{1,2,3,0:T(8,128)S(1)} collective-permute-done((f32[2,64,16,2]{1,2,3,0:T(8,128)S(1)}, f32[2,64,16,2]{1,2,3,0:T(8,128)S(1)}, u32[]{:S(2)}, u32[]{:S(2)}) %collective-permute-start.2) | collective-permute-done | bytes 16416 | tf_op jit(solution)/shard_map/ppermute | solution.py:333
  66.0 0.3 copy.20
  66.3 0.0 collective-permute-done.1
  66.4 0.3 copy.21
  66.7 0.2 slice.149
  66.9 0.3 copy.19
  67.2 1.1 copy.18
  68.4 0.0 collective-permute-done
  68.4 0.0 collective-permute-done.3
  68.4 4.3 %fusion.7 = (f32[64,16,128]{2,1,0:T(8,128)S(1)}, f32[64,16,128]{2,1,0:T(8,128)}) fusion(f32[64,16,128]{2,1,0:T(8,128)S(1)} %copy-done.10, f32[64,2,128]{2,1,0:T(2,128)S(1)} %get-tuple-element.27, f32[64,16,2]{2,1,0:T(8,128)S(1)} %bitcast.27, f32[64,16,2]{2,1,0:T(8,128)S(1)} %bitcast.24, f32[64,16,1]{2,1,0:T(8,128)S(1)} %slice.149, ...), kind=kLoop, calls=%fused_computation.22 | loop fusion | flops 6684672 | bytes 2342912 | tf_op jit(solution)/shard_map/sub | solution.py:356
  72.7 1.6 shard_map.115
  74.3 0.0 copy-start.12
  74.3 0.0 all-to-all-done.u_ref
  74.3 23.5 %all_to_all.20 = bf16[128,8,256]{2,1,0:T(8,128)(2,1)S(1)} all-to-all(bf16[128,8,256]{2,1,0:T(8,128)(2,1)S(1)} %bitcast.16), channel_id=1, replica_groups=mesh['along'=32,'across'=4] {'along','across'}, dimensions={0} | all-to-all | bytes 1048576 | tf_op jit(solution)/shard_map/all_to_all | solution.py:365
  97.8 10.3 %shard_map.116 = (bf16[8,64,256]{2,1,0:T(8,128)(2,1)S(1)}, bf16[1024,2048]{1,0:T(8,128)(2,1)}, f32[8,1024]{1,0:T(8,128)S(1)}, bf16[128,32,128]{2,1,0:T(8,128)(2,1)}) custom-call(s32[256]{0:T(256)S(1)} %get-tuple-element.12.pick_ref, s32[128]{0:T(128)S(1)} %copy-done.9, bf16[1024,256]{1,0:T(8,128)(2,1)S(1)} %bitcast.17, bf16[128,32,256]{2,1,0:T(8,128)(2,1)S(1)} %copy-done.5), custom_call_target="tpu_custom_call" | custom-call | tf_op jit(solution)/shard_map/pallas_call | solution.py:202
  108.1 3.8 %all-to-all-start.2 = ((bf16[128,32,128]{2,1,0:T(8,128)(2,1)}), bf16[128,32,128]{2,1,0:T(8,128)(2,1)S(1)}, u32[]{:S(2)}, u32[]{:S(2)}) async-start(bf16[128,32,128]{2,1,0:T(8,128)(2,1)} %get-tuple-element.17), calls=%async_computation.2 | async-start | bytes 2097152 | tf_op jit(solution)/shard_map/all_to_all | solution.py:365
  111.9 1.5 collective-permute-start.4
  113.4 1.6 collective-permute-start.5
  115.0 0.1 reshape.26.rel_ref
  115.0 16.9 %collective-permute-done.4.before_ref = bf16[8,64,256]{2,1,0:T(8,128)(2,1)S(1)} collective-permute-done((bf16[8,64,256]{2,1,0:T(8,128)(2,1)S(1)}, bf16[8,64,256]{2,1,0:T(8,128)(2,1)S(1)}, u32[]{:S(2)}, u32[]{:S(2)}) %collective-permute-start.4) | collective-permute-done | bytes 262176 | tf_op jit(solution)/shard_map/ppermute | solution.py:400
  132.0 0.0 collective-permute-done.5.after_ref
  132.0 3.7 %copy-done.3 = bf16[8,9,256,256]{3,2,1,0:T(8,128)(2,1)S(1)} copy-done((bf16[8,9,256,256]{3,2,1,0:T(8,128)(2,1)S(1)}, bf16[8,9,256,256]{3,2,1,0:T(8,128)(2,1)}, u32[]{:S(2)}) %copy-start.3) | copy-done | bytes 9437208
  135.7 4.6 %shard_map.117.near_ref = f32[8,64,256]{2,1,0:T(8,128)S(1)} custom-call(s32[72]{0:T(128)S(1)} %reshape.26.rel_ref, bf16[8,64,256]{2,1,0:T(8,128)(2,1)S(1)} %collective-permute-done.4.before_ref, bf16[8,64,256]{2,1,0:T(8,128)(2,1)S(1)} %get-tuple-element.19.own_ref, bf16[8,64,256]{2,1,0:T(8,128)(2,1)S(1)} %collective-permute-done.5.after_ref, ...), custom_call_target="tpu_custom_call" | custom-call | tf_op jit(solution)/shard_map/pallas_call | solution.py:233
  140.3 0.0 all-to-all-done.2.c_ref
  140.3 8.9 %shard_map.118 = bf16[1024,128]{1,0:T(8,128)(2,1)S(1)} custom-call(bf16[128,32,128]{2,1,0:T(8,128)(2,1)S(1)} %all-to-all-done.2.c_ref, bf16[128,2,32,256]{3,2,1,0:T(8,128)(2,1)} %all-to-all-done.u_ref, f32[8,64,256]{2,1,0:T(8,128)S(1)} %shard_map.117.near_ref, bf16[1024,2048]{1,0:T(8,128)(2,1)} %get-tuple-element.20.hot_ref, ...), custom_call_target="tpu_custom_call" | custom-call | tf_op jit(solution)/shard_map/pallas_call | solution.py:288
  149.2 19.4 %all_to_all.21 = bf16[128,8,128]{2,1,0:T(8,128)(2,1)S(1)} all-to-all(bf16[128,8,128]{2,1,0:T(8,128)(2,1)S(1)} %bitcast.18), channel_id=1, replica_groups=mesh['along'=32,'across'=4] {'along','across'}, dimensions={0} | all-to-all | bytes 524288 | tf_op jit(solution)/shard_map/all_to_all | solution.py:365
  168.6 1.8 %shard_map.119 = bf16[64,16,128]{2,1,0:T(8,128)(2,1)} custom-call(bf16[1024,128]{1,0:T(8,128)(2,1)S(1)} %bitcast.19, bf16[1024,2048]{1,0:T(8,128)(2,1)S(1)} %copy-done.2, s32[8,2048]{1,0:T(8,128)S(1)} %get-tuple-element.14.place_ref), custom_call_target="tpu_custom_call" | custom-call | tf_op jit(solution)/shard_map/pallas_call | solution.py:314
  (25 shorter events, 0.1 us)
Async XLA Ops:
  0.6 1.6 copy-start.4
  2.2 0.7 copy-start.7
  7.2 12.0 %copy-start.10 = (f32[64,16,128]{2,1,0:T(8,128)S(1)}, f32[64,16,128]{2,1,0:T(8,128)}, u32[]{:S(2)}) copy-start(f32[64,16,128]{2,1,0:T(8,128)} %param.11) | copy-start | bytes 1572868
  7.2 12.0 %copy-start.11 = (f32[64,16,128]{2,1,0:T(8,128)S(1)}, f32[64,16,128]{2,1,0:T(8,128)}, u32[]{:S(2)}) copy-start(f32[64,16,128]{2,1,0:T(8,128)} %param.10) | copy-start | bytes 1572868
  7.3 67.0 %all-to-all-start = ((bf16[128,2,32,256]{3,2,1,0:T(8,128)(2,1)}), bf16[128,2,32,256]{3,2,1,0:T(8,128)(2,1)}, u32[]{:S(2)}, u32[]{:S(2)}) async-start(bf16[128,2,32,256]{3,2,1,0:T(8,128)(2,1)} %get-tuple-element.15), calls=%async_computation | async-start | bytes 8388608 | tf_op jit(solution)/shard_map/all_to_all | solution.py:365
  19.2 12.8 %copy-start.8 = (s32[128]{0:T(128)S(1)}, s32[128]{0:T(128)}, u32[]{:S(2)}) copy-start(s32[128]{0:T(128)} %rows_ref.1) | copy-start | bytes 1540
  19.2 12.8 %copy-start.6 = (s32[16,128]{1,0:T(8,128)S(1)}, s32[16,128]{1,0:T(8,128)}, u32[]{:S(2)}) copy-start(s32[16,128]{1,0:T(8,128)} %slot_ref.1) | copy-start | bytes 24580
  19.3 49.0 %collective-permute-start = (f32[2,64,2,128]{3,2,1,0:T(2,128)S(1)}, f32[2,64,2,128]{3,2,1,0:T(2,128)S(1)}, u32[]{:S(2)}, u32[]{:S(2)}) collective-permute-start(f32[2,64,2,128]{3,2,1,0:T(2,128)S(1)} %pad_maximum_fusion.11), channel_id=1, source_target_pairs={{0,4},{4,8},{8,12},{12,16},{16,20},{20,24},{24,28},{28,32},{32,36}... | collective-permute-start | bytes 393224 | tf_op jit(solution)/shard_map/ppermute | solution.py:330
  23.7 42.3 %collective-permute-start.2 = (f32[2,64,16,2]{1,2,3,0:T(8,128)S(1)}, f32[2,64,16,2]{1,2,3,0:T(8,128)S(1)}, u32[]{:S(2)}, u32[]{:S(2)}) collective-permute-start(f32[2,64,16,2]{1,2,3,0:T(8,128)S(1)} %copy.14), channel_id=1, source_target_pairs={{1,0},{2,1},{3,2},{5,4},{6,5},{7,6},{9,8},{10,9},{11,10},{13,12},{... | collective-permute-start | bytes 49160 | tf_op jit(solution)/shard_map/ppermute | solution.py:333
  25.4 40.9 %collective-permute-start.1 = (f32[2,64,16,2]{1,2,3,0:T(8,128)S(1)}, f32[2,64,16,2]{1,2,3,0:T(8,128)S(1)}, u32[]{:S(2)}, u32[]{:S(2)}) collective-permute-start(f32[2,64,16,2]{1,2,3,0:T(8,128)S(1)} %copy.12), channel_id=1, source_target_pairs={{0,1},{1,2},{2,3},{4,5},{5,6},{6,7},{8,9},{9,10},{10,11},{12,13},{... | collective-permute-start | bytes 49160 | tf_op jit(solution)/shard_map/ppermute | solution.py:332
  30.1 38.4 %collective-permute-start.3 = (f32[64,1,128]{2,1,0:T(1,128)}, f32[64,1,128]{2,1,0:T(1,128)S(1)}, u32[]{:S(2)}, u32[]{:S(2)}) collective-permute-start(f32[64,1,128]{2,1,0:T(1,128)} %slice.114), channel_id=1, source_target_pairs={{4,0},{8,4},{12,8},{16,12},{20,16},{24,20},{28,24},{32,28},{36,32}... | collective-permute-start | bytes 98312 | tf_op jit(solution)/shard_map/ppermute | solution.py:331
  35.1 2.0 %copy-start = (bf16[1024,2048]{1,0:T(8,128)(2,1)}, bf16[1024,2048]{1,0:T(8,128)(2,1)S(1)}, u32[]{:S(2)}) copy-start(bf16[1024,2048]{1,0:T(8,128)(2,1)S(1)} %get-tuple-element.13.hot_ref) | copy-start | bytes 12582916
  68.4 4.3 %copy-start.1 = (bf16[1024,2048]{1,0:T(8,128)(2,1)S(1)}, bf16[1024,2048]{1,0:T(8,128)(2,1)}, u32[]{:S(2)}) copy-start(bf16[1024,2048]{1,0:T(8,128)(2,1)} %copy-done) | copy-start | bytes 12582916
  72.7 25.1 %copy-start.5 = (bf16[128,32,256]{2,1,0:T(8,128)(2,1)S(1)}, bf16[128,32,256]{2,1,0:T(8,128)(2,1)}, u32[]{:S(2)}) copy-start(bf16[128,32,256]{2,1,0:T(8,128)(2,1)} %v_ref.1) | copy-start | bytes 6291460
  72.7 25.1 %copy-start.9 = (s32[128]{0:T(128)S(1)}, s32[128]{0:T(128)}, u32[]{:S(2)}) copy-start(s32[128]{0:T(128)} %col_ref.1) | copy-start | bytes 1540
  74.3 40.7 %copy-start.12 = (s32[8,9]{1,0:T(8,128)S(1)}, s32[8,9]{1,0:T(8,128)}, u32[]{:S(2)}) copy-start(s32[8,9]{1,0:T(8,128)} %param.15) | copy-start | bytes 868
  108.1 32.2 %all-to-all-start.2 = ((bf16[128,32,128]{2,1,0:T(8,128)(2,1)}), bf16[128,32,128]{2,1,0:T(8,128)(2,1)S(1)}, u32[]{:S(2)}, u32[]{:S(2)}) async-start(bf16[128,32,128]{2,1,0:T(8,128)(2,1)} %get-tuple-element.17), calls=%async_computation.2 | async-start | bytes 2097152 | tf_op jit(solution)/shard_map/all_to_all | solution.py:365
  111.9 20.1 %collective-permute-start.4 = (bf16[8,64,256]{2,1,0:T(8,128)(2,1)S(1)}, bf16[8,64,256]{2,1,0:T(8,128)(2,1)S(1)}, u32[]{:S(2)}, u32[]{:S(2)}) collective-permute-start(bf16[8,64,256]{2,1,0:T(8,128)(2,1)S(1)} %get-tuple-element.19.own_ref), channel_id=1, source_target_pairs={{0,1},{1,2},{2,3},{3,4},{4,5},{5,6},{6,7},{7,8},{8,9},{9,10},{10,1... | collective-permute-start | bytes 786440 | tf_op jit(solution)/shard_map/ppermute | solution.py:400
  113.4 18.6 %collective-permute-start.5 = (bf16[8,64,256]{2,1,0:T(8,128)(2,1)S(1)}, bf16[8,64,256]{2,1,0:T(8,128)(2,1)S(1)}, u32[]{:S(2)}, u32[]{:S(2)}) collective-permute-start(bf16[8,64,256]{2,1,0:T(8,128)(2,1)S(1)} %get-tuple-element.19.own_ref), channel_id=1, source_target_pairs={{1,0},{2,1},{3,2},{4,3},{5,4},{6,5},{7,6},{8,7},{9,8},{10,9},{11,1... | collective-permute-start | bytes 786440 | tf_op jit(solution)/shard_map/ppermute | solution.py:401
  132.0 3.7 %copy-start.3 = (bf16[8,9,256,256]{3,2,1,0:T(8,128)(2,1)S(1)}, bf16[8,9,256,256]{3,2,1,0:T(8,128)(2,1)}, u32[]{:S(2)}) copy-start(bf16[8,9,256,256]{3,2,1,0:T(8,128)(2,1)} %blocks_ref.1) | copy-start | bytes 28311556
  140.3 28.3 %copy-start.2 = (bf16[1024,2048]{1,0:T(8,128)(2,1)S(1)}, bf16[1024,2048]{1,0:T(8,128)(2,1)}, u32[]{:S(2)}) copy-start(bf16[1024,2048]{1,0:T(8,128)(2,1)} %copy-done) | copy-start | bytes 12582916
where the time goes:
time: 171 us; the launch traced here: 170 us
  waiting for transfers between devices  44 us (26%)
  blocking collectives  42.9 us (25%)
  Pallas kernels  34.5 us (20%)
  starting transfers between devices  29.5 us (17%)
  local copies, waits for them, and re-layouts  13.8 us (8%)
  other arithmetic  4.69 us (3%)
    all_to_all x2, blocking collectives, exchange(): return lax.all_to_all(x, BOTH, split_axis=0, concat_axis=0, tiled=True)  42.9 us
    ppermute x1, waiting for transfers between devices, halo(): east = lax.ppermute(both[:, :, :, :2], 'across', left)  27 us
    ppermute x1, waiting for transfers between devices, body(): before = lax.ppermute(clustered, BOTH, ring)  16.9 us
    all_to_all x2, starting transfers between devices, exchange(): return lax.all_to_all(x, BOTH, split_axis=0, concat_axis=0, tiled=True)  15.8 us
    pallas_call x1, Pallas kernels, cluster_and_coeff(): call(cluster_kernel, (jax.ShapeDtypeStruct((8, WAVES, CL), BF16), jax.Sha...  10.3 us
    unnamed x30, local copies, waits for them, and re-layouts  10 us
    pallas_call x1, Pallas kernels, total_home(): call(total_kernel, jax.ShapeDtypeStruct((ROWS, 128), BF16), [VMEM] * 5, V...  8.89 us
    pallas_call x1, Pallas kernels, near_product(): pl.pallas_call(near_kernel, out_shape=jax.ShapeDtypeStruct((8, WAVES, CL)...  4.6 us
  transfers between devices with their start and end apart: 8, of which 2 were waited for; matrix products, arithmetic and copies ran while one was open for 6% of the time, Pallas kernels for 5%

commit v1 on v0

v1 whole, which is shorter than its diff:
```python
import jax
import jax.numpy as jnp
from jax import lax
from jax.experimental import pallas as pl
from jax.experimental.pallas import tpu as pltpu
from jax.sharding import PartitionSpec as P

CL = 256
BOTH = ("along", "across")
OWNERS = 128
PAIRS = 128
RANK = 32
WAVES = 64
ROWS = 1024
PANELS = 2048
BF16 = jnp.bfloat16
F32 = jnp.float32
WIDE = 56
VMEM = pl.BlockSpec(memory_space=pltpu.VMEM)
SMEM = pl.BlockSpec(memory_space=pltpu.SMEM)
HBM = pl.BlockSpec(memory_space=pltpu.HBM)


def call(kernel, out_shape, in_specs, out_specs, scratch=(), limit=4, cost=0):
    return pl.pallas_call(
        kernel,
        out_shape=out_shape,
        in_specs=in_specs,
        out_specs=out_specs,
        scratch_shapes=list(scratch),
        compiler_params=pltpu.CompilerParams(vmem_limit_bytes=limit * 2**20),
        cost_estimate=pl.CostEstimate(flops=0, bytes_accessed=cost, transcendentals=0),
    )


def hot_block(count, row):
    index = iota((count, row.shape[1]), 0).astype(jnp.int16)
    hit = index == row.astype(jnp.int16)
    return jnp.where(hit, jnp.ones((), BF16), jnp.zeros((), BF16))


def iota(shape, dim):
    return lax.broadcasted_iota(jnp.int32, shape, dim)


def dot(a, b):
    return jnp.dot(a, b, preferred_element_type=F32)


def dot_nt(a, b):
    return lax.dot_general(a, b, (((1,), (1,)), ((), ())), preferred_element_type=F32)


def bucket_kernel(table_ref, u_hbm, out_hbm, values, packed, sems):
    load([(u_hbm, values)], sems)

    def put(t, c):
        for s in range(2):
            p = table_ref[s * OWNERS + t]
            mine = values[jnp.minimum(p, PAIRS - 1)]
            packed[t, pl.ds(s * RANK, RANK), :] = jnp.where(p < PAIRS, mine, jnp.zeros_like(mine))
        return c

    lax.fori_loop(0, OWNERS, put, 0, unroll=4)
    load([(packed, out_hbm.at[:, 0:64, :])], sems)


def far_bucket(table, far_u):
    return call(
        bucket_kernel,
        jax.ShapeDtypeStruct((OWNERS, 80, CL), BF16),
        [SMEM, HBM],
        HBM,
        [
            pltpu.VMEM((PAIRS, RANK, CL), BF16),
            pltpu.VMEM((OWNERS, 2 * RANK, CL), BF16),
            pltpu.SemaphoreType.DMA((1,)),
        ],
        limit=WIDE,
        cost=9 * 2**20,
    )(table, far_u)


def load(pairs, sems):
    copies = [pltpu.make_async_copy(a, b, sems.at[i]) for i, (a, b) in enumerate(pairs)]
    for copy in copies:
        copy.start()
    for copy in copies:
        copy.wait()


def tracks(hbm, ref):
    return [(hbm.at[:, x, :], ref.at[x]) for x in range(16)]


def pack_kernel(
    elevation_hbm, phi_hbm, down_ref, up_ref, right_ref, left_ref, elevation, phi, sems
):
    load(tracks(elevation_hbm, elevation) + tracks(phi_hbm, phi), sems)
    lane = iota((WAVES, 128), 1)
    right = jnp.zeros((WAVES, 128), F32)
    left = jnp.zeros((WAVES, 128), F32)
    for k, ref in enumerate((elevation, phi)):
        for x in range(16):
            values = ref[x]
            if x >= 14:
                down_ref[2 * k + x - 14] = values
            if x == 0 and k == 1:
                up_ref[...] = values
            at = 64 * k + 2 * x
            here = (lane >> 1) == at // 2
            right = jnp.where(here, pltpu.roll(values, (at + 2) % 128, 1), right)
            left = jnp.where(here, pltpu.roll(values, at, 1) if at else values, left)
    right_ref[...] = right
    left_ref[...] = left


def pack_edges(elevation, velocity_pot):
    side = jax.ShapeDtypeStruct((WAVES, 128), F32)
    track = pltpu.VMEM((16, WAVES, 128), F32)
    return call(
        pack_kernel,
        (jax.ShapeDtypeStruct((4, WAVES, 128), F32), side, side, side),
        [HBM, HBM],
        (VMEM,) * 4,
        [track, track, pltpu.SemaphoreType.DMA((32,))],
        limit=WIDE,
    )(elevation, velocity_pot)


def surface_kernel(
    keep_ref,
    elevation_hbm,
    phi_hbm,
    coef_hbm,
    slot_hbm,
    rows_hbm,
    cols_hbm,
    above_ref,
    below_ref,
    west_ref,
    east_ref,
    eta_hbm,
    out_hbm,
    place_ref,
    table_ref,
    elevation,
    phi,
    coef,
    slots,
    far,
    hot,
    eta_tracks,
    stack,
    out,
    sems,
    field_sems,
    eta_sems,
    out_sems,
):
    fields = tracks(elevation_hbm, elevation) + tracks(phi_hbm, phi)
    fields = [pltpu.make_async_copy(a, b, field_sems.at[i]) for i, (a, b) in enumerate(fields)]
    small = [
        (slot_hbm, slots),
        (rows_hbm, far.at[0:1]),
        (cols_hbm, far.at[1:2]),
        (coef_hbm, coef),
    ]
    small = [pltpu.make_async_copy(a, b, sems.at[i]) for i, (a, b) in enumerate(small)]
    for copy in small + fields:
        copy.start()
    for copy in small:
        copy.wait()

    up = iota((128, 128), 0) < iota((128, 128), 1)
    weights = jnp.concatenate([up.astype(F32), jnp.ones((128, 128), F32)], axis=1).astype(BF16)
    seen = jnp.zeros((128, 128), F32)
    for x in range(16):
        slot = slots[x : x + 1, :]
        dest, local = slot >> 11, slot & (PANELS - 1)
        hits = iota((128, 128), 0) == dest
        sums = dot(hits.astype(F32).astype(BF16), weights)
        rank = jnp.sum(jnp.where(hits, sums[:, :128] + seen, 0.0), axis=0, keepdims=True)
        seen = seen + sums[:, 128:]
        rank = rank.astype(jnp.int32)
        row = dest * 8 + (rank & 7)
        lanes = pl.ds(x * 128, 128)
        hot[:, lanes] = hot_block(ROWS, row)
        place_ref[0:1, lanes] = rank >> 3
        place_ref[1:2, lanes] = local >> 7
        place_ref[2:3, lanes] = local & 127
        place_ref[3:4, lanes] = row
        place_ref[4:8, lanes] = jnp.zeros((4, 128), jnp.int32)

    turned = [
        jnp.broadcast_to(far[k : k + 1, :].astype(F32), (128, 128)).T.astype(jnp.int32)
        for k in range(2)
    ]
    hits = (turned[0] >> 3) == iota((128, 128), 1)
    down = (iota((128, 128), 0) > iota((128, 128), 1)).astype(F32).astype(BF16)
    rank = dot(down, hits.astype(F32).astype(BF16))
    values = (iota((128, 128), 0) - PAIRS, (turned[0] & 7) - 8, turned[1] & 7)
    for k, (value, base) in enumerate(zip(values, (PAIRS, 8, 0))):
        for s in range(2):
            chosen = hits & (rank == float(s))
            found = jnp.sum(jnp.where(chosen, value.astype(F32), 0.0), axis=0, keepdims=True)
            table_ref[2 * k + s : 2 * k + s + 1, :] = found.astype(jnp.int32) + base
    table_ref[6:8, :] = jnp.zeros((2, 128), jnp.int32)

    for copy in fields:
        copy.wait()
    lane = iota((WAVES, 128), 1)
    west, east = west_ref[...] * keep_ref[2], east_ref[...] * keep_ref[3]
    above = [above_ref[k] * keep_ref[0] for k in range(4)]
    below = below_ref[...] * keep_ref[1]

    def views(f, x, k, ref):
        x1 = ref[x - 1] if x >= 1 else above[2 * k + 1]
        x2 = ref[x - 2] if x >= 2 else above[2 * k + x]
        at = 64 * k + 2 * x
        left = pltpu.roll(west, 128 - at, 1) if at else west
        right = pltpu.roll(east, 126 - at, 1)
        w2 = jnp.where(lane < 2, left, pltpu.roll(f, 2, 1))
        w1 = jnp.where(lane < 1, pltpu.roll(left, 127, 1), pltpu.roll(f, 1, 1))
        e2 = jnp.where(lane >= 126, right, pltpu.roll(f, 126, 1))
        e1 = jnp.where(lane >= 127, pltpu.roll(right, 1, 1), pltpu.roll(f, 127, 1))
        up = 0.5 * (3.0 * f - 4.0 * x1 + x2)
        across = (w2 - 8.0 * w1 + 8.0 * e1 - e2) * (1.0 / 12.0)
        return x1, w1, e1, up, across

    stack[128:256, :] = jnp.zeros((128, PANELS + 128), BF16)
    stack[0:128, pl.ds(PANELS, 128)] = jnp.zeros((128, 128), BF16)
    stores = []
    for x in range(16):
        e, p = elevation[x], phi[x]
        _, _, _, up, across = views(e, x, 0, elevation)
        p1, pw, pe, phi_up, phi_across = views(p, x, 1, phi)
        next_row = phi[x + 1] if x < 15 else below
        curvature = next_row + p1 + pe + pw - 4.0 * p
        eta = e - 0.4 * up + 0.3 * across + coef[x : x + 1, :] * curvature
        eta_tracks[x] = eta
        stores.append(pltpu.make_async_copy(eta_tracks.at[x], eta_hbm.at[:, x, :], eta_sems.at[x]))
        stores[x].start()
        values = p - 0.4 * phi_up + 0.3 * phi_across - 0.5 * eta
        lanes = pl.ds(x * 128, 128)
        place = place_ref[:, lanes]
        second = place[0:1] == 1
        stack[0:64, lanes] = jnp.where(second, 0.0, values).astype(BF16)
        stack[64:128, lanes] = jnp.where(second, values, 0.0).astype(BF16)
        high, low = place[1:2].astype(F32), place[2:3].astype(F32)
        notes = [
            jnp.where(second, 0.0, high),
            jnp.where(second, 0.0, low),
            jnp.where(second, high, 0.0),
            jnp.where(second, low, 0.0),
            jnp.zeros((12, 128), F32),
        ]
        stack[128:144, lanes] = jnp.concatenate(notes, axis=0).astype(BF16)
    rows = table_ref[2:4, :].astype(F32)
    own = jnp.concatenate([jnp.zeros((4, 128), F32), rows, jnp.zeros((10, 128), F32)], axis=0)
    stack[128:144, pl.ds(PANELS, 128)] = own.astype(BF16)
    for m in range(0, ROWS, 256):
        at = pl.ds(m, 256)
        owner = ((iota((256, 128), 0) + m) >> 3) == iota((256, 128), 1)
        values = dot_nt(hot[at, :], stack[:, pl.ds(0, PANELS)])
        values += dot_nt(owner.astype(F32).astype(BF16), stack[:, pl.ds(PANELS, 128)])
        out[at, :] = values.astype(BF16)
        stores.append(pltpu.make_async_copy(out.at[at], out_hbm.at[at], out_sems.at[m // 256]))
        stores[-1].start()
    for copy in stores:
        copy.wait()


def surface_payload(keep, elevation, velocity_pot, coef, slots, rows, cols, halo):
    track = pltpu.VMEM((16, WAVES, 128), F32)
    return call(
        surface_kernel,
        (
            jax.ShapeDtypeStruct((WAVES, 16, 128), F32),
            jax.ShapeDtypeStruct((ROWS, 256), BF16),
            jax.ShapeDtypeStruct((8, PANELS), jnp.int32),
            jax.ShapeDtypeStruct((8, 128), jnp.int32),
        ),
        [SMEM] + [HBM] * 6 + [VMEM] * 4,
        (HBM, HBM, VMEM, VMEM),
        [
            track,
            track,
            pltpu.VMEM((16, 128), F32),
            pltpu.VMEM((16, 128), jnp.int32),
            pltpu.VMEM((2, 128), jnp.int32),
            pltpu.VMEM((ROWS, PANELS), BF16),
            track,
            pltpu.VMEM((256, PANELS + 128), BF16),
            pltpu.VMEM((ROWS, 256), BF16),
            pltpu.SemaphoreType.DMA((4,)),
            pltpu.SemaphoreType.DMA((32,)),
            pltpu.SemaphoreType.DMA((16,)),
            pltpu.SemaphoreType.DMA((4,)),
        ],
        limit=WIDE,
    )(
        keep,
        elevation,
        velocity_pot,
        coef,
        slots,
        rows.reshape(1, PAIRS),
        cols.reshape(1, PAIRS),
        *halo,
    )


def cluster_kernel(arrived_ref, clustered_ref, info_ref, hot, right):
    lane = iota((128, 128), 1)
    for m in range(0, ROWS, 128):
        lanes = pl.ds(m, 128)
        values = arrived_ref[lanes, 0:128].astype(F32)
        tail = arrived_ref[lanes, 128:256].astype(F32)
        notes = tail.T
        swapped = pltpu.roll(values, 64, 1)
        for half in range(2):
            slot = notes[2 * half : 2 * half + 1] * 128.0 + notes[2 * half + 1 : 2 * half + 2]
            info_ref[half : half + 1, lanes] = slot
            at = half * ROWS + m
            place = slot.astype(jnp.int32) & 1023
            hot[:, pl.ds(at, 128)] = hot_block(1024, place)
            both = jnp.where((lane < 64) == (half == 0), values, swapped)
            upper = tail[:, 2 * half : 2 * half + 1] >= 8.0
            right[pl.ds(at, 128), :] = jnp.where(upper == (lane >= 64), both, 0.0).astype(BF16)
        info_ref[2:4, lanes] = notes[4:6]
        info_ref[4:8, lanes] = jnp.zeros((4, 128), F32)
    for m in range(0, 1024, 256):
        clustered_ref[pl.ds(m, 256), :] = dot(hot[pl.ds(m, 256), :], right[...]).astype(BF16)


def to_clusters(arrived):
    return call(
        cluster_kernel,
        (
            jax.ShapeDtypeStruct((1024, 128), BF16),
            jax.ShapeDtypeStruct((8, ROWS), F32),
        ),
        [VMEM],
        (VMEM,) * 2,
        [pltpu.VMEM((1024, PANELS), BF16), pltpu.VMEM((PANELS, 128), BF16)],
        limit=8,
    )(arrived)


def coeff_kernel(table_ref, clustered_ref, v_hbm, big_hbm, out_hbm, basis, coeff, packed, sems):
    del big_hbm
    parts = [
        pltpu.make_async_copy(v_hbm.at[pl.ds(m, 32)], basis.at[pl.ds(m, 32)], sems.at[m // 32])
        for m in range(0, PAIRS, 32)
    ]
    for copy in parts:
        copy.start()
    weights = [clustered_ref[pl.ds(q * 256, 256), :] for q in range(4)]
    weights = [jnp.concatenate(weights[q : q + 2], axis=1) for q in (0, 2)]
    for q in range(4):
        coeff[q, pl.ds(PAIRS * RANK, RANK), :] = jnp.zeros((RANK, 128), F32)
    for m in range(0, PAIRS, 16):
        if m % 32 == 0:
            parts[m // 32].wait()
        rows = basis[pl.ds(m, 16)].reshape(16 * RANK, CL)
        at = pl.ds(m * RANK, 16 * RANK)
        for q in range(2):
            got = dot(rows, weights[q])
            coeff[2 * q, at, :] = got[:, :128]
            coeff[2 * q + 1, at, :] = got[:, 128:]
    lane = iota((RANK, 128), 1)

    def put(t, c):
        both = []
        for s in range(2):
            p = table_ref[s * OWNERS + t]
            col = table_ref[(4 + s) * OWNERS + t]
            tile = coeff[col & 3, pl.ds(pl.multiple_of(p * RANK, RANK), RANK), :]
            both.append(pltpu.roll(tile, ((col >> 2) ^ s) * 64, 1))
        both = jnp.where(lane < 64, both[0], both[1])
        packed[t, :, 0:128] = both[0:16].astype(BF16)
        packed[t, :, 128:256] = both[16:32].astype(BF16)
        return c

    lax.fori_loop(0, OWNERS, put, 0, unroll=8)
    load([(packed, out_hbm.at[:, 64:80, :])], sems)


def add_coeff(table, clustered, far_v, big):
    return pl.pallas_call(
        coeff_kernel,
        out_shape=jax.ShapeDtypeStruct((OWNERS, 80, CL), BF16),
        in_specs=[SMEM, VMEM, HBM, HBM],
        out_specs=HBM,
        scratch_shapes=[
            pltpu.VMEM((PAIRS, RANK, CL), BF16),
            pltpu.VMEM((4, PAIRS * RANK + RANK, 128), F32),
            pltpu.VMEM((OWNERS, 16, CL), BF16),
            pltpu.SemaphoreType.DMA((4,)),
        ],
        input_output_aliases={3: 0},
        compiler_params=pltpu.CompilerParams(vmem_limit_bytes=WIDE * 2**20),
        cost_estimate=pl.CostEstimate(flops=0, bytes_accessed=0, transcendentals=0),
    )(table, clustered, far_v, big)


def near_kernel(
    rel_ref,
    before_ref,
    own_ref,
    after_ref,
    info_ref,
    place_ref,
    blocks_ref,
    out_ref,
    unhot_hbm,
    hot_hbm,
    wide,
    unhot,
    hot,
    sems,
):
    c = pl.program_id(0)

    @pl.when(c == 0)
    def _():
        for k, ref in enumerate((before_ref, own_ref, after_ref)):
            for q in range(4):
                turned = ref[pl.ds(q * 256, 256), :].astype(F32).T.astype(BF16)
                wide[8 * k + q] = turned[0:64]
                wide[8 * k + 4 + q] = turned[64:128]

    lanes = pl.ds(pl.multiple_of(c * 256, 256), 256)
    info = info_ref[:, pl.ds(pl.multiple_of(lax.rem(c, 4) * 256, 256), 256)]
    slot = jnp.where(c < 4, info[0:1], info[1:2]).astype(jnp.int32)
    unhot[:, lanes] = hot_block(1024, slot & 1023)
    hot[:, lanes] = hot_block(ROWS, place_ref[3:4, lanes])
    total = jnp.zeros((WAVES, CL), F32)
    for k in range(9):
        total += dot_nt(wide[rel_ref[c * 9 + k]], blocks_ref[0, k])
    out_ref[0] = total

    @pl.when(c == 7)
    def _():
        load([(unhot, unhot_hbm), (hot, hot_hbm)], sems)


def near_product(relative, before, own, after, info, place, near_blocks):
    matrix = jax.ShapeDtypeStruct((1024, PANELS), BF16)
    return pl.pallas_call(
        near_kernel,
        out_shape=(jax.ShapeDtypeStruct((8, WAVES, CL), F32), matrix, matrix),
        grid_spec=pltpu.PrefetchScalarGridSpec(
            num_scalar_prefetch=1,
            grid=(8,),
            in_specs=[VMEM] * 5 + [pl.BlockSpec((1, 9, CL, CL), lambda c, r: (c, 0, 0, 0))],
            out_specs=(pl.BlockSpec((1, WAVES, CL), lambda c, r: (c, 0, 0)), HBM, HBM),
            scratch_shapes=[
                pltpu.VMEM((24, WAVES, CL), BF16),
                pltpu.VMEM((1024, PANELS), BF16),
                pltpu.VMEM((1024, PANELS), BF16),
                pltpu.SemaphoreType.DMA((2,)),
            ],
        ),
        compiler_params=pltpu.CompilerParams(vmem_limit_bytes=WIDE * 2**20),
        cost_estimate=pl.CostEstimate(flops=0, bytes_accessed=12 * 2**20, transcendentals=0),
    )(relative, before, own, after, info, place, near_blocks)


def total_kernel(
    big_hbm, near_ref, hot_hbm, info_ref, out_hbm, big, hot, acc, masked, grid, out, sems, hot_sems, out_sems
):
    pieces = [
        pltpu.make_async_copy(big_hbm.at[pl.ds(m * 16, 16)], big.at[pl.ds(m * 16, 16)], sems.at[m])
        for m in range(8)
    ]
    for piece in pieces:
        piece.start()
    hot_copy = pltpu.make_async_copy(hot_hbm, hot, hot_sems.at[0])
    hot_copy.start()
    spread = ((iota((128, 256), 0) >> 3) == (iota((128, 256), 1) >> 4)) & (
        (iota((128, 256), 0) & 7) == 0
    )
    spread = spread.astype(F32).astype(BF16)
    for m in range(8):
        pieces[m].wait()
        src = pl.ds(m * 16, 16)
        slot = m % 2
        rows = dot(info_ref[:, pl.ds(m * 128, 128)].astype(BF16), spread)
        bases = []
        for part in range(2):
            mine = big[src, 64:80, pl.ds(part * 128, 128)].reshape(256, 128)
            turned = mine.astype(F32).T.astype(BF16)
            for s in range(2):
                at = pl.ds((2 * part + s) * 256, 256)
                for cluster in range(8):
                    hit = (rows[2 + s : 3 + s] == float(cluster)).astype(F32).astype(BF16)
                    masked[slot, pl.ds(cluster * 64, 64), at] = turned[s * 64 : s * 64 + 64] * hit
                bases.append(big[src, pl.ds(s * RANK + part * 16, 16), :].reshape(256, CL))
        product = dot(masked[slot], jnp.concatenate(bases, axis=0))
        if m == 0:
            acc[...] = product
        else:
            acc[...] += product
    for cluster in range(8):
        total = near_ref[cluster] + acc[pl.ds(cluster * 64, 64), :]
        grid[pl.ds((cluster >> 2) * 64, 64), pl.ds((cluster & 3) * 256, 256)] = total.astype(BF16)
    hot_copy.wait()
    stores = []
    for m in range(0, ROWS, 256):
        at = pl.ds(m, 256)
        halves = []
        for half in range(2):
            got = dot(grid[...], hot[:, pl.ds(half * ROWS + m, 256)])
            upper = info_ref[half : half + 1, at] >= 1024.0
            halves.append(jnp.where(upper, got[64:128], got[0:64]))
        out[at, :] = jnp.concatenate(halves, axis=0).T.astype(BF16)
        stores.append(pltpu.make_async_copy(out.at[at], out_hbm.at[at], out_sems.at[m // 256]))
        stores[-1].start()
    for copy in stores:
        copy.wait()


def total_home(big, near, hot, info):
    return call(
        total_kernel,
        jax.ShapeDtypeStruct((ROWS, 128), BF16),
        [HBM, VMEM, HBM, VMEM],
        HBM,
        [
            pltpu.VMEM((OWNERS, 80, CL), BF16),
            pltpu.VMEM((1024, PANELS), BF16),
            pltpu.VMEM((512, CL), F32),
            pltpu.VMEM((2, 512, 1024), BF16),
            pltpu.VMEM((128, 1024), BF16),
            pltpu.VMEM((ROWS, 128), BF16),
            pltpu.SemaphoreType.DMA((8,)),
            pltpu.SemaphoreType.DMA((1,)),
            pltpu.SemaphoreType.DMA((4,)),
        ],
        limit=WIDE,
    )(big, near, hot, info)


def potential_kernel(returned_ref, hot_ref, place_ref, out_ref, turned, wide):
    for m in range(0, ROWS, 128):
        turned[:, pl.ds(m, 128)] = returned_ref[pl.ds(m, 128), :].astype(F32).T.astype(BF16)
    for x in range(0, 16, 2):
        lanes = pl.ds(x * 128, 256)
        got = dot(turned[...], hot_ref[:, lanes])
        got = jnp.where(place_ref[0:1, lanes] == 1, got[64:128], got[0:64])
        wide[:, x, :] = got[:, :128]
        wide[:, x + 1, :] = got[:, 128:]
    out_ref[...] = wide[...].astype(BF16)


def panel_potential(returned, hot, place):
    return call(
        potential_kernel,
        jax.ShapeDtypeStruct((WAVES, 16, 128), BF16),
        [VMEM] * 3,
        VMEM,
        [pltpu.VMEM((128, ROWS), BF16), pltpu.VMEM((WAVES, 16, 128), F32)],
    )(returned, hot, place)


def exchange(x):
    return lax.all_to_all(x, BOTH, split_axis=0, concat_axis=0, tiled=True)


def ring(axis, step):
    size = lax.axis_size(axis)
    return [(i, (i + step) % size) for i in range(size)]


def body(
    elevation,
    velocity_pot,
    surface_coef,
    panel_slot,
    near_blocks,
    near_cols,
    far_v,
    far_u,
    far_rows,
    far_cols,
):
    per_owner, clusters = 8, 1024
    me = lax.axis_index(BOTH)
    row, col = lax.axis_index("along"), lax.axis_index("across")
    keep = jnp.stack(
        [row > 0, row < lax.axis_size("along") - 1, col > 0, col < lax.axis_size("across") - 1]
    ).astype(F32)

    down, up, right, left = pack_edges(elevation, velocity_pot)
    above = lax.ppermute(down, "along", ring("along", 1))
    below = lax.ppermute(up, "along", ring("along", -1))
    west = lax.ppermute(right, "across", ring("across", 1))
    east = lax.ppermute(left, "across", ring("across", -1))
    eta, payload, place, table = surface_payload(
        keep,
        elevation,
        velocity_pot,
        surface_coef,
        panel_slot,
        far_rows,
        far_cols,
        (above, below, west, east),
    )
    table = table.reshape(8 * 128)
    arrived = exchange(payload.reshape(OWNERS, 8, 256)).reshape(ROWS, 256)
    big = far_bucket(table, far_u)
    arrived, big = lax.optimization_barrier((arrived, big))

    clustered, info = to_clusters(arrived)
    before = lax.ppermute(clustered, BOTH, ring(BOTH, 1))
    after = lax.ppermute(clustered, BOTH, ring(BOTH, -1))
    big = add_coeff(table, clustered, far_v, big)
    before, after, big = lax.optimization_barrier((before, after, big))
    big = exchange(big)

    relative = (near_cols - (me * per_owner - per_owner)) % clusters
    near, unhot, hot = near_product(
        relative.reshape(72), before, clustered, after, info, place, near_blocks
    )

    home = total_home(big, near, unhot, info).reshape(OWNERS, 8, 128)
    returned = exchange(home).reshape(ROWS, 128)
    potential = panel_potential(returned, hot, place)
    return (eta, potential)


def solution(mesh):
    in_specs = (
        P(None, "along", "across"),
        P(None, "along", "across"),
        P("along", "across"),
        P("along", "across"),
        P(BOTH, None, None, None),
        P(BOTH, None),
        P(BOTH, None, None),
        P(BOTH, None, None),
        P(BOTH),
        P(BOTH),
    )
    out_specs = (P(None, "along", "across"), P(None, "along", "across"))
    return jax.shard_map(body, mesh=mesh, in_specs=in_specs, out_specs=out_specs, check_vma=False)
```

time: 171 us -> 161 us (0.942)
  blocking collectives: 42.9 us -> 16 us
  waiting for transfers between devices: 44 us -> 63.3 us
  Pallas kernels: 34.5 us -> 52 us
  local copies, waits for them, and re-layouts: 13.8 us -> 2.58 us
  starting transfers between devices: 29.5 us -> 25.2 us
  other arithmetic: 4.69 us -> 0.68 us
    all_to_all x2, waiting for transfers between devices: 0.02 us -> 59.4 us  [exchange(): return lax.all_to_all(x, BOTH, split_axis=0, concat_axis=0, tiled=True)]
    ppermute x6, waiting for transfers between devices: 44 us -> 3.97 us  [the longest x1 3.13 us: body(): before = lax.ppermute(clustered, BOTH, ring(BOTH, 1))]
    all_to_all x2 -> x1, blocking collectives: 42.9 us -> 16 us  [exchange(): return lax.all_to_all(x, BOTH, split_axis=0, concat_axis=0, tiled=True)]
    pallas_call x6 -> x7, Pallas kernels: 32.7 us -> 50.2 us  [the longest x1 13.7 us: near_product(): pl.pallas_call(near_kernel, out_shape=(jax.ShapeDtypeStruct((8, WAVES, CL...]
    unnamed x30 -> x22, local copies, waits for them, and re-layouts: 10 us -> 1.98 us
    ppermute x6, starting transfers between devices: 13.8 us -> 6.9 us  [the longest x1 2.76 us: body(): above = lax.ppermute(down, 'along', ring('along', 1))]
    sub x1 -> x0, other arithmetic: 4.25 us -> none  [surface_step(): velocity_pot - 0.4 * up_x(velocity_pot, above[1])]
    all_to_all x2, starting transfers between devices: 15.8 us -> 18.3 us  [exchange(): return lax.all_to_all(x, BOTH, split_axis=0, concat_axis=0, tiled=True)]
  transfers between devices with their start and end apart: 8 -> 8, of which waited for: 2 -> 5; matrix products, arithmetic and copies ran while one was open for 6% -> 1% of each run, Pallas kernels for 5% -> 16%
where the time goes in v1:
time: 161 us
  waiting for transfers between devices  63.3 us (39%)
  Pallas kernels  52 us (32%)
  starting transfers between devices  25.2 us (16%)
  blocking collectives  16 us (10%)
  local copies, waits for them, and re-layouts  2.58 us (2%)
    all_to_all x2, waiting for transfers between devices, exchange(): return lax.all_to_all(x, BOTH, split_axis=0, concat_axis=0, tiled=True)  59.4 us
    all_to_all x2, starting transfers between devices, exchange(): return lax.all_to_all(x, BOTH, split_axis=0, concat_axis=0, tiled=True)  18.3 us
    all_to_all x1, blocking collectives, exchange(): return lax.all_to_all(x, BOTH, split_axis=0, concat_axis=0, tiled=True)  16 us
    pallas_call x1, Pallas kernels, near_product(): pl.pallas_call(near_kernel, out_shape=(jax.ShapeDtypeStruct((8, WAVES, CL...  13.7 us
    pallas_call x1, Pallas kernels, total_home(): call(total_kernel, jax.ShapeDtypeStruct((ROWS, 128), BF16), [HBM, VMEM, H...  10.2 us
    pallas_call x1, Pallas kernels, surface_payload(): call(surface_kernel, (jax.ShapeDtypeStruct((WAVES, 16, 128), F32), jax.Sh...  9.78 us
    pallas_call x1, Pallas kernels, add_coeff(): pl.pallas_call(coeff_kernel, out_shape=jax.ShapeDtypeStruct((OWNERS, 80,...  6.75 us
    pallas_call x1, Pallas kernels, far_bucket(): call(bucket_kernel, jax.ShapeDtypeStruct((OWNERS, 80, CL), BF16), [SMEM,...  5.22 us
  transfers between devices with their start and end apart: 8, of which 5 were waited for; matrix products, arithmetic and copies ran while one was open for 1% of the time, Pallas kernels for 16%

profile of v1, /device:TPU:1, one launch (start us, length us, event | category | flops | bytes accessed | tf_op | source)
XLA Modules:
  0.0 160.5 jit_solution(12105861941635286166)
XLA Ops:
  0.6 2.8 %shard_map.113 = (f32[4,64,128]{2,1,0:T(8,128)}, f32[64,128]{1,0:T(8,128)}, f32[64,128]{1,0:T(8,128)}, f32[64,128]{1,0:T(8,128)}) custom-call(f32[64,16,128]{2,1,0:T(8,128)} %elevation_hbm.3, f32[64,16,128]{2,1,0:T(8,128)} %phi_hbm.3), custom_call_target="tpu_custom_call" | custom-call | tf_op jit(solution)/shard_map/pallas_call | solution.py:121
  3.4 2.8 %collective-permute-start = (f32[4,64,128]{2,1,0:T(8,128)}, f32[4,64,128]{2,1,0:T(8,128)S(1)}, u32[]{:S(2)}, u32[]{:S(2)}) collective-permute-start(f32[4,64,128]{2,1,0:T(8,128)} %get-tuple-element.20), channel_id=1, source_target_pairs={{0,4},{4,8},{8,12},{12,16},{16,20},{20,24},{24,28},{28,32},{32,36}... | collective-permute-start | bytes 393224 | tf_op jit(solution)/shard_map/ppermute | solution.py:597
  6.2 0.0 collective-permute-start.1
  6.2 1.2 collective-permute-start.2
  7.4 1.5 collective-permute-start.3
  8.9 0.7 add_convert_fusion.keep_ref
  9.5 0.2 collective-permute-done.1.below_ref
  9.7 0.0 copy-start.7
  9.7 0.6 collective-permute-done.2.west_ref
  10.4 0.0 copy-start.8
  10.4 0.0 collective-permute-done.3.east_ref
  10.4 0.0 copy-start.9
  10.4 0.0 collective-permute-done.above_ref
  10.4 0.0 copy-start.6
  10.4 0.0 copy-done.7
  10.4 0.6 copy-done.8
  11.0 0.0 copy-done.9
  11.0 0.0 copy-done.6
  11.1 9.8 %shard_map.114 = (f32[64,16,128]{2,1,0:T(8,128)}, bf16[1024,256]{1,0:T(8,128)(2,1)}, s32[8,2048]{1,0:T(8,128)}, s32[8,128]{1,0:T(8,128)}) custom-call(f32[4]{0:T(128)} %add_convert_fusion.keep_ref, f32[64,16,128]{2,1,0:T(8,128)} %elevation_hbm.3, f32[64,16,128]{2,1,0:T(8,128)} %phi_hbm.3, f32[16,128]{1,0:T(8,128)} %coef_hbm.1, s32[16,128]{1,0:T(8,128)} %slot_hbm.1, ...), custom_call_target="tpu_custom_call" | custom-call | tf_op jit(solution)/shard_map/pallas_call | solution.py:276
  20.9 11.9 %all-to-all-start = ((bf16[128,8,256]{2,1,0:T(8,128)(2,1)}), bf16[128,8,256]{2,1,0:T(8,128)(2,1)S(1)}, u32[]{:S(2)}, u32[]{:S(2)}) async-start(bf16[128,8,256]{2,1,0:T(8,128)(2,1)} %bitcast.14), calls=%async_computation | async-start | bytes 1048576 | tf_op jit(solution)/shard_map/all_to_all | solution.py:569
  32.8 5.2 %shard_map.115.big_hbm = bf16[128,80,256]{2,1,0:T(8,128)(2,1)} custom-call(s32[1024]{0:T(1024)} %bitcast.15, bf16[128,32,256]{2,1,0:T(8,128)(2,1)} %u_hbm.1), custom_call_target="tpu_custom_call" | custom-call | bytes 9437184 | tf_op jit(solution)/shard_map/pallas_call | solution.py:69
  38.0 8.7 %all-to-all-done = bf16[128,8,256]{2,1,0:T(8,128)(2,1)S(1)} async-done(((bf16[128,8,256]{2,1,0:T(8,128)(2,1)}), bf16[128,8,256]{2,1,0:T(8,128)(2,1)S(1)}, u32[]{:S(2)}, u32[]{:S(2)}) %all-to-all-start) | async-done | bytes 524320 | tf_op jit(solution)/shard_map/all_to_all | solution.py:569
  46.7 1.7 %shard_map.116 = (bf16[1024,128]{1,0:T(8,128)(2,1)S(1)}, f32[8,1024]{1,0:T(8,128)S(1)}) custom-call(bf16[1024,256]{1,0:T(8,128)(2,1)S(1)} %bitcast.11), custom_call_target="tpu_custom_call" | custom-call | tf_op jit(solution)/shard_map/pallas_call | solution.py:338
  48.5 0.0 copy-start.3
  48.5 0.6 copy-done.3
  49.1 0.0 copy-start.1
  49.1 1.4 collective-permute-start.5
  50.5 0.1 collective-permute-start.4
  50.6 0.0 copy-done.1
  50.6 6.8 %shard_map.117 = bf16[128,80,256]{2,1,0:T(8,128)(2,1)} custom-call(s32[1024]{0:T(1024)} %bitcast.16, bf16[1024,128]{1,0:T(8,128)(2,1)} %copy-done.1, bf16[128,32,256]{2,1,0:T(8,128)(2,1)} %v_hbm.1, bf16[128,80,256]{2,1,0:T(8,128)(2,1)} %shard_map.115.big_hbm), custom_call_target="tpu_custom_call", output_to_operand_aliasing={{}: (3, {})} | custom-call | tf_op jit(solution)/shard_map/pallas_call | solution.py:391
  57.3 0.0 copy-start.10
  57.3 0.0 collective-permute-done.5.after_ref
  57.4 0.0 copy-start.4
  57.4 3.1 %collective-permute-done.4.before_ref = bf16[1024,128]{1,0:T(8,128)(2,1)S(1)} collective-permute-done((bf16[1024,128]{1,0:T(8,128)(2,1)S(1)}, bf16[1024,128]{1,0:T(8,128)(2,1)S(1)}, u32[]{:S(2)}, u32[]{:S(2)}) %collective-permute-start.4) | collective-permute-done | bytes 262176 | tf_op jit(solution)/shard_map/ppermute | solution.py:617
  60.5 0.0 copy-start.5
  60.5 0.0 copy-done.4
  60.5 0.7 copy-done.5
  61.2 6.4 %all-to-all-start.1 = ((bf16[128,80,256]{2,1,0:T(8,128)(2,1)}), bf16[128,80,256]{2,1,0:T(8,128)(2,1)}, u32[]{:S(2)}, u32[]{:S(2)}) async-start(bf16[128,80,256]{2,1,0:T(8,128)(2,1)} %shard_map.117), calls=%async_computation.1 | async-start | bytes 10485760 | tf_op jit(solution)/shard_map/all_to_all | solution.py:569
  67.6 0.0 copy-done.10
  67.7 0.6 reshape.33.rel_ref
  68.2 13.7 %shard_map.118 = (f32[8,64,256]{2,1,0:T(8,128)}, bf16[1024,2048]{1,0:T(8,128)(2,1)}, bf16[1024,2048]{1,0:T(8,128)(2,1)}) custom-call(s32[72]{0:T(128)} %reshape.33.rel_ref, bf16[1024,128]{1,0:T(8,128)(2,1)} %copy-done.5, bf16[1024,128]{1,0:T(8,128)(2,1)} %copy-done.1, bf16[1024,128]{1,0:T(8,128)(2,1)} %copy-done.4, f32[8,1024]{1,0:T(8,128)} %copy-done.3, ...), custom_call_target="tpu_custom_call" | custom-call | bytes 12582912 | tf_op jit(solution)/shard_map/pallas_call | solution.py:451
  81.9 50.6 %all-to-all-done.1.big_hbm = bf16[128,80,256]{2,1,0:T(8,128)(2,1)} async-done(((bf16[128,80,256]{2,1,0:T(8,128)(2,1)}), bf16[128,80,256]{2,1,0:T(8,128)(2,1)}, u32[]{:S(2)}, u32[]{:S(2)}) %all-to-all-start.1) | async-done | bytes 5242912 | tf_op jit(solution)/shard_map/all_to_all | solution.py:569
  132.5 0.0 copy-start
  132.6 10.2 %shard_map.119 = bf16[1024,128]{1,0:T(8,128)(2,1)} custom-call(bf16[128,80,256]{2,1,0:T(8,128)(2,1)} %all-to-all-done.1.big_hbm, f32[8,64,256]{2,1,0:T(8,128)} %get-tuple-element.35.near_ref, bf16[1024,2048]{1,0:T(8,128)(2,1)} %get-tuple-element.36.hot_hbm, f32[8,1024]{1,0:T(8,128)} %copy-done.3), custom_call_target="tpu_custom_call" | custom-call | tf_op jit(solution)/shard_map/pallas_call | solution.py:526
  142.8 16.0 %all_to_all.15 = bf16[128,8,128]{2,1,0:T(8,128)(2,1)S(1)} all-to-all(bf16[128,8,128]{2,1,0:T(8,128)(2,1)} %bitcast.13), channel_id=1, replica_groups=mesh['along'=32,'across'=4] {'along','across'}, dimensions={0} | all-to-all | bytes 524288 | tf_op jit(solution)/shard_map/all_to_all | solution.py:569
  158.7 0.0 copy-done
  158.8 0.0 copy-done.2
  158.8 1.8 %shard_map.120 = bf16[64,16,128]{2,1,0:T(8,128)(2,1)} custom-call(bf16[1024,128]{1,0:T(8,128)(2,1)S(1)} %bitcast.12, bf16[1024,2048]{1,0:T(8,128)(2,1)S(1)} %copy-done, s32[8,2048]{1,0:T(8,128)S(1)} %copy-done.2), custom_call_target="tpu_custom_call" | custom-call | tf_op jit(solution)/shard_map/pallas_call | solution.py:559
  (2 shorter events, 0.0 us)
Async XLA Ops:
  3.4 7.0 %collective-permute-start = (f32[4,64,128]{2,1,0:T(8,128)}, f32[4,64,128]{2,1,0:T(8,128)S(1)}, u32[]{:S(2)}, u32[]{:S(2)}) collective-permute-start(f32[4,64,128]{2,1,0:T(8,128)} %get-tuple-element.20), channel_id=1, source_target_pairs={{0,4},{4,8},{8,12},{12,16},{16,20},{20,24},{24,28},{28,32},{32,36}... | collective-permute-start | bytes 393224 | tf_op jit(solution)/shard_map/ppermute | solution.py:597
  6.2 3.6 %collective-permute-start.1 = (f32[64,128]{1,0:T(8,128)}, f32[64,128]{1,0:T(8,128)S(1)}, u32[]{:S(2)}, u32[]{:S(2)}) collective-permute-start(f32[64,128]{1,0:T(8,128)} %get-tuple-element.21), channel_id=1, source_target_pairs={{0,124},{4,0},{8,4},{12,8},{16,12},{20,16},{24,20},{28,24},{32,28}... | collective-permute-start | bytes 98312 | tf_op jit(solution)/shard_map/ppermute | solution.py:598
  6.2 4.2 %collective-permute-start.2 = (f32[64,128]{1,0:T(8,128)}, f32[64,128]{1,0:T(8,128)S(1)}, u32[]{:S(2)}, u32[]{:S(2)}) collective-permute-start(f32[64,128]{1,0:T(8,128)} %get-tuple-element.22), channel_id=1, source_target_pairs={{0,1},{1,2},{2,3},{3,0},{4,5},{5,6},{6,7},{7,4},{8,9},{9,10},{10,1... | collective-permute-start | bytes 98312 | tf_op jit(solution)/shard_map/ppermute | solution.py:599
  7.4 3.0 %collective-permute-start.3 = (f32[64,128]{1,0:T(8,128)}, f32[64,128]{1,0:T(8,128)S(1)}, u32[]{:S(2)}, u32[]{:S(2)}) collective-permute-start(f32[64,128]{1,0:T(8,128)} %get-tuple-element.23), channel_id=1, source_target_pairs={{0,3},{1,0},{2,1},{3,2},{4,7},{5,4},{6,5},{7,6},{8,11},{9,8},{10,9... | collective-permute-start | bytes 98312 | tf_op jit(solution)/shard_map/ppermute | solution.py:600
  9.7 0.7 copy-start.7
  10.4 0.6 copy-start.8
  10.4 0.6 copy-start.9
  10.4 0.7 copy-start.6
  20.9 25.9 %all-to-all-start = ((bf16[128,8,256]{2,1,0:T(8,128)(2,1)}), bf16[128,8,256]{2,1,0:T(8,128)(2,1)S(1)}, u32[]{:S(2)}, u32[]{:S(2)}) async-start(bf16[128,8,256]{2,1,0:T(8,128)(2,1)} %bitcast.14), calls=%async_computation | async-start | bytes 1048576 | tf_op jit(solution)/shard_map/all_to_all | solution.py:569
  48.5 0.6 copy-start.3
  49.1 1.5 copy-start.1
  49.1 8.2 %collective-permute-start.5 = (bf16[1024,128]{1,0:T(8,128)(2,1)S(1)}, bf16[1024,128]{1,0:T(8,128)(2,1)S(1)}, u32[]{:S(2)}, u32[]{:S(2)}) collective-permute-start(bf16[1024,128]{1,0:T(8,128)(2,1)S(1)} %get-tuple-element.28.clustered_ref.own_ref), channel_id=1, source_target_pairs={{0,127},{1,0},{2,1},{3,2},{4,3},{5,4},{6,5},{7,6},{8,7},{9,8},{10,... | collective-permute-start | bytes 786440 | tf_op jit(solution)/shard_map/ppermute | solution.py:618
  50.5 10.0 %collective-permute-start.4 = (bf16[1024,128]{1,0:T(8,128)(2,1)S(1)}, bf16[1024,128]{1,0:T(8,128)(2,1)S(1)}, u32[]{:S(2)}, u32[]{:S(2)}) collective-permute-start(bf16[1024,128]{1,0:T(8,128)(2,1)S(1)} %get-tuple-element.28.clustered_ref.own_ref), channel_id=1, source_target_pairs={{0,1},{1,2},{2,3},{3,4},{4,5},{5,6},{6,7},{7,8},{8,9},{9,10},{10,1... | collective-permute-start | bytes 786440 | tf_op jit(solution)/shard_map/ppermute | solution.py:617
  57.3 10.3 %copy-start.10 = (s32[8,9]{1,0:T(8,128)S(1)}, s32[8,9]{1,0:T(8,128)}, u32[]{:S(2)}) copy-start(s32[8,9]{1,0:T(8,128)} %param.15) | copy-start | bytes 868
  57.4 3.1 %copy-start.4 = (bf16[1024,128]{1,0:T(8,128)(2,1)}, bf16[1024,128]{1,0:T(8,128)(2,1)S(1)}, u32[]{:S(2)}) copy-start(bf16[1024,128]{1,0:T(8,128)(2,1)S(1)} %collective-permute-done.5.after_ref) | copy-start | bytes 786436
  60.5 0.7 copy-start.5
  61.2 71.3 %all-to-all-start.1 = ((bf16[128,80,256]{2,1,0:T(8,128)(2,1)}), bf16[128,80,256]{2,1,0:T(8,128)(2,1)}, u32[]{:S(2)}, u32[]{:S(2)}) async-start(bf16[128,80,256]{2,1,0:T(8,128)(2,1)} %shard_map.117), calls=%async_computation.1 | async-start | bytes 10485760 | tf_op jit(solution)/shard_map/all_to_all | solution.py:569
  132.5 26.2 %copy-start = (bf16[1024,2048]{1,0:T(8,128)(2,1)S(1)}, bf16[1024,2048]{1,0:T(8,128)(2,1)}, u32[]{:S(2)}) copy-start(bf16[1024,2048]{1,0:T(8,128)(2,1)} %get-tuple-element.37.hot_ref) | copy-start | bytes 12582916
  132.5 26.2 %copy-start.2 = (s32[8,2048]{1,0:T(8,128)S(1)}, s32[8,2048]{1,0:T(8,128)}, u32[]{:S(2)}) copy-start(s32[8,2048]{1,0:T(8,128)} %get-tuple-element.34.place_ref) | copy-start | bytes 196612

commit v2 on v1

--- a/solution.py
+++ b/solution.py
@@ -16,6 +16,8 @@
 BF16 = jnp.bfloat16
 F32 = jnp.float32
 WIDE = 56
+PACK = 56
+TIGHT = 52
 VMEM = pl.BlockSpec(memory_space=pltpu.VMEM)
 SMEM = pl.BlockSpec(memory_space=pltpu.SMEM)
 HBM = pl.BlockSpec(memory_space=pltpu.HBM)
@@ -76,7 +78,7 @@
             pltpu.VMEM((OWNERS, 2 * RANK, CL), BF16),
             pltpu.SemaphoreType.DMA((1,)),
         ],
-        limit=WIDE,
+        limit=TIGHT,
         cost=9 * 2**20,
     )(table, far_u)
 
@@ -89,94 +91,94 @@
         copy.wait()
 
 
-def tracks(hbm, ref):
-    return [(hbm.at[:, x, :], ref.at[x]) for x in range(16)]
-
-
 def pack_kernel(
-    elevation_hbm, phi_hbm, down_ref, up_ref, right_ref, left_ref, elevation, phi, sems
+    elevation_hbm,
+    phi_hbm,
+    slot_hbm,
+    rows_hbm,
+    cols_hbm,
+    coef_hbm,
+    elevation_ref,
+    phi_ref,
+    plan_ref,
+    along_a,
+    along_b,
+    across_a,
+    across_b,
+    ints,
+    sems,
+    field_sems,
 ):
-    load(tracks(elevation_hbm, elevation) + tracks(phi_hbm, phi), sems)
+    small = [
+        (slot_hbm, ints.at[0:16]),
+        (rows_hbm, ints.at[16:17]),
+        (cols_hbm, ints.at[17:18]),
+        (coef_hbm, plan_ref.at[24:40]),
+    ]
+    small = [pltpu.make_async_copy(a, b, sems.at[i]) for i, (a, b) in enumerate(small)]
+    fields = []
+    for x in range(16):
+        fields.append((elevation_hbm.at[:, x, :], elevation_ref.at[x]))
+        fields.append((phi_hbm.at[:, x, :], phi_ref.at[x]))
+    fields = [pltpu.make_async_copy(a, b, field_sems.at[i]) for i, (a, b) in enumerate(fields)]
+    for copy in fields + small:
+        copy.start()
+    for copy in small:
+        copy.wait()
+    plan_ref[0:24, :] = ints[...].astype(F32)
+    even_row = lax.rem(lax.axis_index("along"), 2) == 0
+    even_col = lax.rem(lax.axis_index("across"), 2) == 0
+    for copy in fields:
+        copy.wait()
     lane = iota((WAVES, 128), 1)
     right = jnp.zeros((WAVES, 128), F32)
     left = jnp.zeros((WAVES, 128), F32)
-    for k, ref in enumerate((elevation, phi)):
+    for k, ref in enumerate((elevation_ref, phi_ref)):
         for x in range(16):
             values = ref[x]
-            if x >= 14:
-                down_ref[2 * k + x - 14] = values
-            if x == 0 and k == 1:
-                up_ref[...] = values
             at = 64 * k + 2 * x
             here = (lane >> 1) == at // 2
             right = jnp.where(here, pltpu.roll(values, (at + 2) % 128, 1), right)
             left = jnp.where(here, pltpu.roll(values, at, 1) if at else values, left)
-    right_ref[...] = right
-    left_ref[...] = left
-
-
-def pack_edges(elevation, velocity_pot):
+    across_a[...] = jnp.where(even_col, right, left)
+    across_b[...] = jnp.where(even_col, left, right)
+    upward = phi_ref[0]
+    for k, downward in enumerate((elevation_ref[14], elevation_ref[15], phi_ref[14], phi_ref[15])):
+        along_a[k] = jnp.where(even_row, downward, upward)
+        along_b[k] = jnp.where(even_row, upward, downward)
+
+
+def pack_edges(elevation, velocity_pot, panel_slot, far_rows, far_cols, coef):
     side = jax.ShapeDtypeStruct((WAVES, 128), F32)
-    track = pltpu.VMEM((16, WAVES, 128), F32)
+    rows = jax.ShapeDtypeStruct((4, WAVES, 128), F32)
+    track = jax.ShapeDtypeStruct((16, WAVES, 128), F32)
     return call(
         pack_kernel,
-        (jax.ShapeDtypeStruct((4, WAVES, 128), F32), side, side, side),
-        [HBM, HBM],
-        (VMEM,) * 4,
-        [track, track, pltpu.SemaphoreType.DMA((32,))],
-        limit=WIDE,
-    )(elevation, velocity_pot)
-
-
-def surface_kernel(
-    keep_ref,
-    elevation_hbm,
-    phi_hbm,
-    coef_hbm,
-    slot_hbm,
-    rows_hbm,
-    cols_hbm,
-    above_ref,
-    below_ref,
-    west_ref,
-    east_ref,
-    eta_hbm,
-    out_hbm,
-    place_ref,
-    table_ref,
-    elevation,
-    phi,
-    coef,
-    slots,
-    far,
-    hot,
-    eta_tracks,
-    stack,
-    out,
-    sems,
-    field_sems,
-    eta_sems,
-    out_sems,
-):
-    fields = tracks(elevation_hbm, elevation) + tracks(phi_hbm, phi)
-    fields = [pltpu.make_async_copy(a, b, field_sems.at[i]) for i, (a, b) in enumerate(fields)]
-    small = [
-        (slot_hbm, slots),
-        (rows_hbm, far.at[0:1]),
-        (cols_hbm, far.at[1:2]),
-        (coef_hbm, coef),
-    ]
-    small = [pltpu.make_async_copy(a, b, sems.at[i]) for i, (a, b) in enumerate(small)]
-    for copy in small + fields:
-        copy.start()
-    for copy in small:
-        copy.wait()
-
+        (track, track, jax.ShapeDtypeStruct((40, 128), F32), rows, rows, side, side),
+        [HBM] * 6,
+        (VMEM,) * 7,
+        [
+            pltpu.VMEM((24, 128), jnp.int32),
+            pltpu.SemaphoreType.DMA((4,)),
+            pltpu.SemaphoreType.DMA((32,)),
+        ],
+        limit=PACK,
+    )(
+        elevation,
+        velocity_pot,
+        panel_slot,
+        far_rows.reshape(1, PAIRS),
+        far_cols.reshape(1, PAIRS),
+        coef,
+    )
+
+
+def order_kernel(plan_ref, hot_ref, place_ref, table_ref):
     up = iota((128, 128), 0) < iota((128, 128), 1)
     weights = jnp.concatenate([up.astype(F32), jnp.ones((128, 128), F32)], axis=1).astype(BF16)
     seen = jnp.zeros((128, 128), F32)
     for x in range(16):
-        slot = slots[x : x + 1, :]
+        slot = plan_ref[x : x + 1, :].astype(jnp.int32)
         dest, local = slot >> 11, slot & (PANELS - 1)
         hits = iota((128, 128), 0) == dest
         sums = dot(hits.astype(F32).astype(BF16), weights)
@@ -185,7 +187,7 @@
         rank = rank.astype(jnp.int32)
         row = dest * 8 + (rank & 7)
         lanes = pl.ds(x * 128, 128)
-        hot[:, lanes] = hot_block(ROWS, row)
+        hot_ref[:, lanes] = hot_block(ROWS, row)
         place_ref[0:1, lanes] = rank >> 3
         place_ref[1:2, lanes] = local >> 7
         place_ref[2:3, lanes] = local & 127
@@ -193,8 +195,8 @@
         place_ref[4:8, lanes] = jnp.zeros((4, 128), jnp.int32)
 
     turned = [
-        jnp.broadcast_to(far[k : k + 1, :].astype(F32), (128, 128)).T.astype(jnp.int32)
-        for k in range(2)
+        jnp.broadcast_to(plan_ref[k : k + 1, :], (128, 128)).T.astype(jnp.int32)
+        for k in range(16, 18)
     ]
     hits = (turned[0] >> 3) == iota((128, 128), 1)
     down = (iota((128, 128), 0) > iota((128, 128), 1)).astype(F32).astype(BF16)
@@ -207,12 +209,51 @@
             table_ref[2 * k + s : 2 * k + s + 1, :] = found.astype(jnp.int32) + base
     table_ref[6:8, :] = jnp.zeros((2, 128), jnp.int32)
 
-    for copy in fields:
-        copy.wait()
+
+def sender_order(plan):
+    return call(
+        order_kernel,
+        (
+            jax.ShapeDtypeStruct((ROWS, PANELS), BF16),
+            jax.ShapeDtypeStruct((8, PANELS), jnp.int32),
+            jax.ShapeDtypeStruct((8, 128), jnp.int32),
+        ),
+        [VMEM],
+        (VMEM,) * 3,
+        limit=8,
+    )(plan)
+
+
+def surface_kernel(
+    plan_ref,
+    elevation_ref,
+    phi_ref,
+    along_a,
+    along_b,
+    across_a,
+    across_b,
+    hot_ref,
+    place_ref,
+    table_ref,
+    eta_hbm,
+    out_hbm,
+    eta_tracks,
+    stack,
+    out,
+    eta_sems,
+    out_sems,
+):
+    row, col = lax.axis_index("along"), lax.axis_index("across")
+    first_row, last_row = row == 0, row == lax.axis_size("along") - 1
+    first_col, last_col = col == 0, col == lax.axis_size("across") - 1
     lane = iota((WAVES, 128), 1)
-    west, east = west_ref[...] * keep_ref[2], east_ref[...] * keep_ref[3]
-    above = [above_ref[k] * keep_ref[0] for k in range(4)]
-    below = below_ref[...] * keep_ref[1]
+    even_row, even_col = lax.rem(row, 2) == 0, lax.rem(col, 2) == 0
+    west = jnp.where(even_col, across_b[...], across_a[...])
+    east = jnp.where(even_col, across_a[...], across_b[...])
+    west, east = jnp.where(first_col, 0.0, west), jnp.where(last_col, 0.0, east)
+    above = [jnp.where(even_row, along_b[k], along_a[k]) for k in range(4)]
+    above = [jnp.where(first_row, 0.0, values) for values in above]
+    below = jnp.where(last_row, 0.0, jnp.where(even_row, along_a[0], along_b[0]))
 
     def views(f, x, k, ref):
         x1 = ref[x - 1] if x >= 1 else above[2 * k + 1]
@@ -232,12 +273,12 @@
     stack[0:128, pl.ds(PANELS, 128)] = jnp.zeros((128, 128), BF16)
     stores = []
     for x in range(16):
-        e, p = elevation[x], phi[x]
-        _, _, _, up, across = views(e, x, 0, elevation)
-        p1, pw, pe, phi_up, phi_across = views(p, x, 1, phi)
-        next_row = phi[x + 1] if x < 15 else below
+        e, p = elevation_ref[x], phi_ref[x]
+        _, _, _, up, across = views(e, x, 0, elevation_ref)
+        p1, pw, pe, phi_up, phi_across = views(p, x, 1, phi_ref)
+        next_row = phi_ref[x + 1] if x < 15 else below
         curvature = next_row + p1 + pe + pw - 4.0 * p
-        eta = e - 0.4 * up + 0.3 * across + coef[x : x + 1, :] * curvature
+        eta = e - 0.4 * up + 0.3 * across + plan_ref[24 + x : 25 + x, :] * curvature
         eta_tracks[x] = eta
         stores.append(pltpu.make_async_copy(eta_tracks.at[x], eta_hbm.at[:, x, :], eta_sems.at[x]))
         stores[x].start()
@@ -262,7 +303,7 @@
     for m in range(0, ROWS, 256):
         at = pl.ds(m, 256)
         owner = ((iota((256, 128), 0) + m) >> 3) == iota((256, 128), 1)
-        values = dot_nt(hot[at, :], stack[:, pl.ds(0, PANELS)])
+        values = dot_nt(hot_ref[at, :], stack[:, pl.ds(0, PANELS)])
         values += dot_nt(owner.astype(F32).astype(BF16), stack[:, pl.ds(PANELS, 128)])
         out[at, :] = values.astype(BF16)
         stores.append(pltpu.make_async_copy(out.at[at], out_hbm.at[at], out_sems.at[m // 256]))
@@ -271,44 +312,24 @@
         copy.wait()
 
 
-def surface_payload(keep, elevation, velocity_pot, coef, slots, rows, cols, halo):
-    track = pltpu.VMEM((16, WAVES, 128), F32)
+def surface_payload(plan, fields, halo, hot, place, table):
     return call(
         surface_kernel,
         (
             jax.ShapeDtypeStruct((WAVES, 16, 128), F32),
             jax.ShapeDtypeStruct((ROWS, 256), BF16),
-            jax.ShapeDtypeStruct((8, PANELS), jnp.int32),
-            jax.ShapeDtypeStruct((8, 128), jnp.int32),
         ),
-        [SMEM] + [HBM] * 6 + [VMEM] * 4,
-        (HBM, HBM, VMEM, VMEM),
+        [VMEM] * 10,
+        (HBM, HBM),
         [
-            track,
-            track,
-            pltpu.VMEM((16, 128), F32),
-            pltpu.VMEM((16, 128), jnp.int32),
-            pltpu.VMEM((2, 128), jnp.int32),
-            pltpu.VMEM((ROWS, PANELS), BF16),
-            track,
+            pltpu.VMEM((16, WAVES, 128), F32),
             pltpu.VMEM((256, PANELS + 128), BF16),
             pltpu.VMEM((ROWS, 256), BF16),
-            pltpu.SemaphoreType.DMA((4,)),
-            pltpu.SemaphoreType.DMA((32,)),
             pltpu.SemaphoreType.DMA((16,)),
             pltpu.SemaphoreType.DMA((4,)),
         ],
-        limit=WIDE,
-    )(
-        keep,
-        elevation,
-        velocity_pot,
-        coef,
-        slots,
-        rows.reshape(1, PAIRS),
-        cols.reshape(1, PAIRS),
-        *halo,
-    )
+        limit=12,
+    )(plan, *fields, *halo, hot, place, table)
 
 
 def cluster_kernel(arrived_ref, clustered_ref, info_ref, hot, right):
@@ -400,8 +421,8 @@
             pltpu.SemaphoreType.DMA((4,)),
         ],
         input_output_aliases={3: 0},
-        compiler_params=pltpu.CompilerParams(vmem_limit_bytes=WIDE * 2**20),
-        cost_estimate=pl.CostEstimate(flops=0, bytes_accessed=0, transcendentals=0),
+        compiler_params=pltpu.CompilerParams(vmem_limit_bytes=TIGHT * 2**20),
+        cost_estimate=pl.CostEstimate(flops=0, bytes_accessed=32 * 2**20, transcendentals=0),
     )(table, clustered, far_v, big)
 
 
@@ -463,50 +484,63 @@
                 pltpu.SemaphoreType.DMA((2,)),
             ],
         ),
-        compiler_params=pltpu.CompilerParams(vmem_limit_bytes=WIDE * 2**20),
-        cost_estimate=pl.CostEstimate(flops=0, bytes_accessed=12 * 2**20, transcendentals=0),
+        compiler_params=pltpu.CompilerParams(vmem_limit_bytes=TIGHT * 2**20),
+        cost_estimate=pl.CostEstimate(flops=0, bytes_accessed=512 * 2**20, transcendentals=0),
     )(relative, before, own, after, info, place, near_blocks)
 
 
 def total_kernel(
-    big_hbm, near_ref, hot_hbm, info_ref, out_hbm, big, hot, acc, masked, grid, out, sems, hot_sems, out_sems
+    big_hbm,
+    near_ref,
+    hot_hbm,
+    info_ref,
+    out_hbm,
+    coeffs,
+    basis,
+    hot,
+    acc,
+    masked,
+    grid,
+    out,
+    sems,
+    out_sems,
 ):
-    pieces = [
-        pltpu.make_async_copy(big_hbm.at[pl.ds(m * 16, 16)], big.at[pl.ds(m * 16, 16)], sems.at[m])
-        for m in range(8)
-    ]
-    for piece in pieces:
-        piece.start()
-    hot_copy = pltpu.make_async_copy(hot_hbm, hot, hot_sems.at[0])
-    hot_copy.start()
+    copies = [pltpu.make_async_copy(big_hbm.at[:, 64:80, :], coeffs, sems.at[4])]
+    for n in range(4):
+        part = big_hbm.at[:, pl.ds(16 * n, 16), :]
+        copies.append(pltpu.make_async_copy(part, basis.at[n], sems.at[n]))
+    copies.append(pltpu.make_async_copy(hot_hbm, hot, sems.at[5]))
+    for copy in copies:
+        copy.start()
     spread = ((iota((128, 256), 0) >> 3) == (iota((128, 256), 1) >> 4)) & (
         (iota((128, 256), 0) & 7) == 0
     )
     spread = spread.astype(F32).astype(BF16)
+    identity = (iota((128, 128), 0) == iota((128, 128), 1)).astype(F32).astype(BF16)
+    copies[0].wait()
     for m in range(8):
-        pieces[m].wait()
         src = pl.ds(m * 16, 16)
-        slot = m % 2
+        at = pl.ds(m * 256, 256)
         rows = dot(info_ref[:, pl.ds(m * 128, 128)].astype(BF16), spread)
-        bases = []
         for part in range(2):
-            mine = big[src, 64:80, pl.ds(part * 128, 128)].reshape(256, 128)
-            turned = mine.astype(F32).T.astype(BF16)
+            mine = coeffs[src, :, pl.ds(part * 128, 128)].reshape(256, 128)
+            turned = dot_nt(identity, mine).astype(BF16)
             for s in range(2):
-                at = pl.ds((2 * part + s) * 256, 256)
                 for cluster in range(8):
                     hit = (rows[2 + s : 3 + s] == float(cluster)).astype(F32).astype(BF16)
-                    masked[slot, pl.ds(cluster * 64, 64), at] = turned[s * 64 : s * 64 + 64] * hit
-                bases.append(big[src, pl.ds(s * RANK + part * 16, 16), :].reshape(256, CL))
-        product = dot(masked[slot], jnp.concatenate(bases, axis=0))
-        if m == 0:
+                    values = turned[s * 64 : s * 64 + 64] * hit
+                    masked[2 * s + part, pl.ds(cluster * 64, 64), at] = values
+    for n in range(4):
+        copies[1 + n].wait()
+        product = dot(masked[n], basis[n].reshape(2048, CL))
+        if n == 0:
             acc[...] = product
         else:
             acc[...] += product
     for cluster in range(8):
         total = near_ref[cluster] + acc[pl.ds(cluster * 64, 64), :]
         grid[pl.ds((cluster >> 2) * 64, 64), pl.ds((cluster & 3) * 256, 256)] = total.astype(BF16)
-    hot_copy.wait()
+    copies[5].wait()
     stores = []
     for m in range(0, ROWS, 256):
         at = pl.ds(m, 256)
@@ -529,17 +563,17 @@
         [HBM, VMEM, HBM, VMEM],
         HBM,
         [
-            pltpu.VMEM((OWNERS, 80, CL), BF16),
+            pltpu.VMEM((OWNERS, 16, CL), BF16),
+            pltpu.VMEM((4, OWNERS, 16, CL), BF16),
             pltpu.VMEM((1024, PANELS), BF16),
             pltpu.VMEM((512, CL), F32),
-            pltpu.VMEM((2, 512, 1024), BF16),
+            pltpu.VMEM((4, 512, 2048), BF16),
             pltpu.VMEM((128, 1024), BF16),
             pltpu.VMEM((ROWS, 128), BF16),
-            pltpu.SemaphoreType.DMA((8,)),
-            pltpu.SemaphoreType.DMA((1,)),
+            pltpu.SemaphoreType.DMA((6,)),
             pltpu.SemaphoreType.DMA((4,)),
         ],
-        limit=WIDE,
+        limit=TIGHT,
     )(big, near, hot, info)
 
 
@@ -572,6 +606,12 @@
 def ring(axis, step):
     size = lax.axis_size(axis)
     return [(i, (i + step) % size) for i in range(size)]
+
+
+def swap(axis, first):
+    size = lax.axis_size(axis)
+    pairs = [(i, (i + 1) % size) for i in range(first, size, 2)]
+    return pairs + [(j, i) for i, j in pairs]
 
 
 def body(
@@ -588,26 +628,16 @@
 ):
     per_owner, clusters = 8, 1024
     me = lax.axis_index(BOTH)
-    row, col = lax.axis_index("along"), lax.axis_index("across")
-    keep = jnp.stack(
-        [row > 0, row < lax.axis_size("along") - 1, col > 0, col < lax.axis_size("across") - 1]
-    ).astype(F32)
-
-    down, up, right, left = pack_edges(elevation, velocity_pot)
-    above = lax.ppermute(down, "along", ring("along", 1))
-    below = lax.ppermute(up, "along", ring("along", -1))
-    west = lax.ppermute(right, "across", ring("across", 1))
-    east = lax.ppermute(left, "across", ring("across", -1))
-    eta, payload, place, table = surface_payload(
-        keep,
-        elevation,
-        velocity_pot,
-        surface_coef,
-        panel_slot,
-        far_rows,
-        far_cols,
-        (above, below, west, east),
+    *fields, plan, along_a, along_b, across_a, across_b = pack_edges(
+        elevation, velocity_pot, panel_slot, far_rows, far_cols, surface_coef
     )
+    along_a = lax.ppermute(along_a, "along", swap("along", 0))
+    along_b = lax.ppermute(along_b, "along", swap("along", 1))
+    across_a = lax.ppermute(across_a, "across", swap("across", 0))
+    across_b = lax.ppermute(across_b, "across", swap("across", 1))
+    hot, place, table = sender_order(plan)
+    halo = (along_a, along_b, across_a, across_b)
+    eta, payload = surface_payload(plan, fields, halo, hot, place, table)
     table = table.reshape(8 * 128)
     arrived = exchange(payload.reshape(OWNERS, 8, 256)).reshape(ROWS, 256)
     big = far_bucket(table, far_u)

time: 161 us -> 154 us (0.957)
  Pallas kernels: 52 us -> 45.6 us
    pallas_call x1, Pallas kernels: 9.78 us -> 4.84 us  [surface_payload(): call(surface_kernel, (jax.ShapeDtypeStruct((WAVES, 16, 128), F32), jax.Sh...]
    pallas_call x1 -> x2, Pallas kernels: 2.8 us -> 4.7 us  [the longest x1 2.87 us: pack_edges(): call(pack_kernel, (track, track, jax.ShapeDtypeStruct((40, 128), F32), ro...]
    pallas_call x1, Pallas kernels: 10.2 us -> 8.43 us  [total_home(): call(total_kernel, jax.ShapeDtypeStruct((ROWS, 128), BF16), [HBM, VMEM, H...]
    all_to_all x2, waiting for transfers between devices: 59.4 us -> 61 us  [exchange(): return lax.all_to_all(x, BOTH, split_axis=0, concat_axis=0, tiled=True)]
  transfers between devices with their start and end apart: 8 -> 8, of which waited for: 5 -> 3; matrix products, arithmetic and copies ran while one was open for 1% -> 0% of each run, Pallas kernels for 16% -> 17%
where the time goes in v2:
time: 154 us
  waiting for transfers between devices  64.5 us (42%)
  Pallas kernels  45.6 us (30%)
  starting transfers between devices  24.6 us (16%)
  blocking collectives  15.1 us (10%)
  local copies, waits for them, and re-layouts  2.89 us (2%)
    all_to_all x2, waiting for transfers between devices, exchange(): return lax.all_to_all(x, BOTH, split_axis=0, concat_axis=0, tiled=True)  61 us
    all_to_all x2, starting transfers between devices, exchange(): return lax.all_to_all(x, BOTH, split_axis=0, concat_axis=0, tiled=True)  17.2 us
    all_to_all x1, blocking collectives, exchange(): return lax.all_to_all(x, BOTH, split_axis=0, concat_axis=0, tiled=True)  15.1 us
    pallas_call x1, Pallas kernels, near_product(): pl.pallas_call(near_kernel, out_shape=(jax.ShapeDtypeStruct((8, WAVES, CL...  12.6 us
    pallas_call x1, Pallas kernels, total_home(): call(total_kernel, jax.ShapeDtypeStruct((ROWS, 128), BF16), [HBM, VMEM, H...  8.43 us
    pallas_call x1, Pallas kernels, add_coeff(): pl.pallas_call(coeff_kernel, out_shape=jax.ShapeDtypeStruct((OWNERS, 80,...  6.39 us
    pallas_call x1, Pallas kernels, far_bucket(): call(bucket_kernel, jax.ShapeDtypeStruct((OWNERS, 80, CL), BF16), [SMEM,...  5.1 us
    pallas_call x1, Pallas kernels, surface_payload(): call(surface_kernel, (jax.ShapeDtypeStruct((WAVES, 16, 128), F32), jax.Sh...  4.84 us
  transfers between devices with their start and end apart: 8, of which 3 were waited for; matrix products, arithmetic and copies ran while one was open for 0% of the time, Pallas kernels for 17%

profile of v2, /device:TPU:1, one launch (start us, length us, event | category | flops | bytes accessed | tf_op | source)
XLA Modules:
  0.0 153.5 jit_solution(11234773013693919028)
XLA Ops:
  0.6 2.9 %shard_map.113 = (f32[16,64,128]{2,1,0:T(8,128)}, f32[16,64,128]{2,1,0:T(8,128)}, f32[40,128]{1,0:T(8,128)}, f32[4,64,128]{2,1,0:T(8,128)}, f32[4,64,128]{2,1,0:...) custom-call(f32[64,16,128]{2,1,0:T(8,128)} %elevation_hbm.1, f32[64,16,128]{2,1,0:T(8,128)} %phi_hbm.1, ...), custom_call_target="tpu_custom_call" | custom-call | tf_op jit(solution)/shard_map/pallas_call | solution.py:155
  3.5 1.5 collective-permute-start
  5.0 1.4 collective-permute-start.1
  6.4 1.2 collective-permute-start.2
  7.6 1.8 %collective-permute-start.3 = (f32[64,128]{1,0:T(8,128)}, f32[64,128]{1,0:T(8,128)S(1)}, u32[]{:S(2)}, u32[]{:S(2)}) collective-permute-start(f32[64,128]{1,0:T(8,128)} %get-tuple-element.30), channel_id=1, source_target_pairs={{1,2},{3,0},{2,1},{0,3},{5,6},{7,4},{6,5},{4,7},{9,10},{11,8},{10,... | collective-permute-start | bytes 98312 | tf_op jit(solution)/shard_map/ppermute | solution.py:637
  9.4 0.0 copy-start.3
  9.4 0.7 copy-done.3
  10.1 1.8 %shard_map.114 = (bf16[1024,2048]{1,0:T(8,128)(2,1)S(1)}, s32[8,2048]{1,0:T(8,128)S(1)}, s32[8,128]{1,0:T(8,128)S(1)}) custom-call(f32[40,128]{1,0:T(8,128)S(1)} %copy-done.3), custom_call_target="tpu_custom_call" | custom-call | tf_op jit(solution)/shard_map/pallas_call | solution.py:214
  12.0 0.0 collective-permute-done.2.across_a
  12.0 0.0 collective-permute-done.3.across_b
  12.0 0.0 collective-permute-done.along_a
  12.0 0.0 collective-permute-done.1.along_b
  12.0 0.0 copy-start.1
  12.0 1.0 copy-done.1
  13.0 0.0 copy-start.2
  13.0 1.0 copy-done.2
  14.1 4.8 %shard_map.115 = (f32[64,16,128]{2,1,0:T(8,128)}, bf16[1024,256]{1,0:T(8,128)(2,1)}) custom-call(f32[40,128]{1,0:T(8,128)S(1)} %copy-done.3, f32[16,64,128]{2,1,0:T(8,128)S(1)} %copy-done.1, f32[16,64,128]{2,1,0:T(8,128)S(1)} %copy-done.2, f32[4,64,128]{2,1,0:T(8,128)S(1)} %collective-permute-done.along_a, f32[4,64,128]{2,1,0:T(8,128)S(1)} %collective-permute-done.1.along_b, ...), custom_call_target="tpu_custom_call" | custom-call | tf_op jit(solution)/shard_map/pallas_call | solution.py:316
  18.9 11.0 %all-to-all-start = ((bf16[128,8,256]{2,1,0:T(8,128)(2,1)}), bf16[128,8,256]{2,1,0:T(8,128)(2,1)S(1)}, u32[]{:S(2)}, u32[]{:S(2)}) async-start(bf16[128,8,256]{2,1,0:T(8,128)(2,1)} %bitcast.2), calls=%async_computation | async-start | bytes 1048576 | tf_op jit(solution)/shard_map/all_to_all | solution.py:603
  29.9 5.1 %shard_map.116.big_hbm = bf16[128,80,256]{2,1,0:T(8,128)(2,1)} custom-call(s32[1024]{0:T(1024)S(1)} %bitcast.10, bf16[128,32,256]{2,1,0:T(8,128)(2,1)} %u_hbm.1), custom_call_target="tpu_custom_call" | custom-call | bytes 9437184 | tf_op jit(solution)/shard_map/pallas_call | solution.py:71
  35.0 8.9 %all-to-all-done = bf16[128,8,256]{2,1,0:T(8,128)(2,1)S(1)} async-done(((bf16[128,8,256]{2,1,0:T(8,128)(2,1)}), bf16[128,8,256]{2,1,0:T(8,128)(2,1)S(1)}, u32[]{:S(2)}, u32[]{:S(2)}) %all-to-all-start) | async-done | bytes 524320 | tf_op jit(solution)/shard_map/all_to_all | solution.py:603
  43.9 1.7 %shard_map.117 = (bf16[1024,128]{1,0:T(8,128)(2,1)S(1)}, f32[8,1024]{1,0:T(8,128)S(1)}) custom-call(bf16[1024,256]{1,0:T(8,128)(2,1)S(1)} %bitcast.7), custom_call_target="tpu_custom_call" | custom-call | tf_op jit(solution)/shard_map/pallas_call | solution.py:359
  45.6 1.5 collective-permute-start.5
  47.1 0.1 collective-permute-start.4
  47.2 6.4 %shard_map.118 = bf16[128,80,256]{2,1,0:T(8,128)(2,1)} custom-call(s32[1024]{0:T(1024)S(1)} %bitcast.11, bf16[1024,128]{1,0:T(8,128)(2,1)S(1)} %get-tuple-element.37.clustered_ref.own_ref, bf16[128,32,256]{2,1,0:T(8,128)(2,1)} %v_hbm.1, bf16[128,80,256]{2,1,0:T(8,128)(2,1)} %shard_map.116.big_hbm), custom_call_target="tpu_custom_call", output_to_operand_aliasing={{}: (3, {})} | custom-call | bytes 33554432 | tf_op jit(solution)/shard_map/pallas_call | solution.py:412
  53.6 0.0 copy-start.4
  53.6 0.0 collective-permute-done.5.after_ref
  53.6 3.5 %collective-permute-done.4.before_ref = bf16[1024,128]{1,0:T(8,128)(2,1)S(1)} collective-permute-done((bf16[1024,128]{1,0:T(8,128)(2,1)S(1)}, bf16[1024,128]{1,0:T(8,128)(2,1)S(1)}, u32[]{:S(2)}, u32[]{:S(2)}) %collective-permute-start.4) | collective-permute-done | bytes 262176 | tf_op jit(solution)/shard_map/ppermute | solution.py:647
  57.1 6.2 %all-to-all-start.1 = ((bf16[128,80,256]{2,1,0:T(8,128)(2,1)}), bf16[128,80,256]{2,1,0:T(8,128)(2,1)}, u32[]{:S(2)}, u32[]{:S(2)}) async-start(bf16[128,80,256]{2,1,0:T(8,128)(2,1)} %shard_map.118), calls=%async_computation.1 | async-start | bytes 10485760 | tf_op jit(solution)/shard_map/all_to_all | solution.py:603
  63.3 0.0 copy-done.4
  63.4 0.1 reshape.33.rel_ref
  63.4 12.6 %shard_map.119 = (f32[8,64,256]{2,1,0:T(8,128)S(1)}, bf16[1024,2048]{1,0:T(8,128)(2,1)}, bf16[1024,2048]{1,0:T(8,128)(2,1)}) custom-call(s32[72]{0:T(128)S(1)} %reshape.33.rel_ref, bf16[1024,128]{1,0:T(8,128)(2,1)S(1)} %collective-permute-done.4.before_ref, bf16[1024,128]{1,0:T(8,128)(2,1)S(1)} %get-tuple-element.37.clustered_ref.own_ref, ...), custom_call_target="tpu_custom_call" | custom-call | bytes 536870912 | tf_op jit(solution)/shard_map/pallas_call | solution.py:472
  76.1 52.2 %all-to-all-done.1.big_hbm = bf16[128,80,256]{2,1,0:T(8,128)(2,1)} async-done(((bf16[128,80,256]{2,1,0:T(8,128)(2,1)}), bf16[128,80,256]{2,1,0:T(8,128)(2,1)}, u32[]{:S(2)}, u32[]{:S(2)}) %all-to-all-start.1) | async-done | bytes 5242912 | tf_op jit(solution)/shard_map/all_to_all | solution.py:603
  128.2 0.0 copy-start
  128.2 8.4 %shard_map.120 = bf16[1024,128]{1,0:T(8,128)(2,1)S(1)} custom-call(bf16[128,80,256]{2,1,0:T(8,128)(2,1)} %all-to-all-done.1.big_hbm, f32[8,64,256]{2,1,0:T(8,128)S(1)} %get-tuple-element.43.near_ref, bf16[1024,2048]{1,0:T(8,128)(2,1)} %get-tuple-element.44.hot_hbm, f32[8,1024]{1,0:T(8,128)S(1)} %get-tuple-element.42.info_ref), custom_call_target="tpu_custom_call" | custom-call | tf_op jit(solution)/shard_map/pallas_call | solution.py:560
  136.7 15.1 %all_to_all.15 = bf16[128,8,128]{2,1,0:T(8,128)(2,1)S(1)} all-to-all(bf16[128,8,128]{2,1,0:T(8,128)(2,1)S(1)} %bitcast.8), channel_id=1, replica_groups=mesh['along'=32,'across'=4] {'along','across'}, dimensions={0} | all-to-all | bytes 524288 | tf_op jit(solution)/shard_map/all_to_all | solution.py:603
  151.7 0.0 copy-done
  151.7 1.8 %shard_map.121 = bf16[64,16,128]{2,1,0:T(8,128)(2,1)} custom-call(bf16[1024,128]{1,0:T(8,128)(2,1)S(1)} %bitcast.9, bf16[1024,2048]{1,0:T(8,128)(2,1)S(1)} %copy-done, s32[8,2048]{1,0:T(8,128)S(1)} %get-tuple-element.32.place_ref), custom_call_target="tpu_custom_call" | custom-call | tf_op jit(solution)/shard_map/pallas_call | solution.py:593
  (1 shorter events, 0.0 us)
Async XLA Ops:
  3.5 8.5 %collective-permute-start = (f32[4,64,128]{2,1,0:T(8,128)}, f32[4,64,128]{2,1,0:T(8,128)S(1)}, u32[]{:S(2)}, u32[]{:S(2)}) collective-permute-start(f32[4,64,128]{2,1,0:T(8,128)} %get-tuple-element.27), channel_id=1, source_target_pairs={{0,4},{8,12},{16,20},{24,28},{32,36},{40,44},{48,52},{56,60},{64,6... | collective-permute-start | bytes 393224 | tf_op jit(solution)/shard_map/ppermute | solution.py:634
  5.0 7.0 %collective-permute-start.1 = (f32[4,64,128]{2,1,0:T(8,128)}, f32[4,64,128]{2,1,0:T(8,128)S(1)}, u32[]{:S(2)}, u32[]{:S(2)}) collective-permute-start(f32[4,64,128]{2,1,0:T(8,128)} %get-tuple-element.28), channel_id=1, source_target_pairs={{4,8},{12,16},{20,24},{28,32},{36,40},{44,48},{52,56},{60,64},{68,... | collective-permute-start | bytes 393224 | tf_op jit(solution)/shard_map/ppermute | solution.py:635
  6.4 5.6 %collective-permute-start.2 = (f32[64,128]{1,0:T(8,128)}, f32[64,128]{1,0:T(8,128)S(1)}, u32[]{:S(2)}, u32[]{:S(2)}) collective-permute-start(f32[64,128]{1,0:T(8,128)} %get-tuple-element.29), channel_id=1, source_target_pairs={{0,1},{2,3},{1,0},{3,2},{4,5},{6,7},{5,4},{7,6},{8,9},{10,11},{9,8... | collective-permute-start | bytes 98312 | tf_op jit(solution)/shard_map/ppermute | solution.py:636
  7.6 4.4 %collective-permute-start.3 = (f32[64,128]{1,0:T(8,128)}, f32[64,128]{1,0:T(8,128)S(1)}, u32[]{:S(2)}, u32[]{:S(2)}) collective-permute-start(f32[64,128]{1,0:T(8,128)} %get-tuple-element.30), channel_id=1, source_target_pairs={{1,2},{3,0},{2,1},{0,3},{5,6},{7,4},{6,5},{4,7},{9,10},{11,8},{10,... | collective-permute-start | bytes 98312 | tf_op jit(solution)/shard_map/ppermute | solution.py:637
  9.4 0.7 copy-start.3
  12.0 1.0 copy-start.1
  13.0 1.0 copy-start.2
  18.9 24.9 %all-to-all-start = ((bf16[128,8,256]{2,1,0:T(8,128)(2,1)}), bf16[128,8,256]{2,1,0:T(8,128)(2,1)S(1)}, u32[]{:S(2)}, u32[]{:S(2)}) async-start(bf16[128,8,256]{2,1,0:T(8,128)(2,1)} %bitcast.2), calls=%async_computation | async-start | bytes 1048576 | tf_op jit(solution)/shard_map/all_to_all | solution.py:603
  45.6 8.0 %collective-permute-start.5 = (bf16[1024,128]{1,0:T(8,128)(2,1)S(1)}, bf16[1024,128]{1,0:T(8,128)(2,1)S(1)}, u32[]{:S(2)}, u32[]{:S(2)}) collective-permute-start(bf16[1024,128]{1,0:T(8,128)(2,1)S(1)} %get-tuple-element.37.clustered_ref.own_ref), channel_id=1, source_target_pairs={{0,127},{1,0},{2,1},{3,2},{4,3},{5,4},{6,5},{7,6},{8,7},{9,8},{10,... | collective-permute-start | bytes 786440 | tf_op jit(solution)/shard_map/ppermute | solution.py:648
  47.1 10.0 %collective-permute-start.4 = (bf16[1024,128]{1,0:T(8,128)(2,1)S(1)}, bf16[1024,128]{1,0:T(8,128)(2,1)S(1)}, u32[]{:S(2)}, u32[]{:S(2)}) collective-permute-start(bf16[1024,128]{1,0:T(8,128)(2,1)S(1)} %get-tuple-element.37.clustered_ref.own_ref), channel_id=1, source_target_pairs={{0,1},{1,2},{2,3},{3,4},{4,5},{5,6},{6,7},{7,8},{8,9},{9,10},{10,1... | collective-permute-start | bytes 786440 | tf_op jit(solution)/shard_map/ppermute | solution.py:647
  53.6 9.8 %copy-start.4 = (s32[8,9]{1,0:T(8,128)S(1)}, s32[8,9]{1,0:T(8,128)}, u32[]{:S(2)}) copy-start(s32[8,9]{1,0:T(8,128)} %param.15) | copy-start | bytes 868
  57.1 71.2 %all-to-all-start.1 = ((bf16[128,80,256]{2,1,0:T(8,128)(2,1)}), bf16[128,80,256]{2,1,0:T(8,128)(2,1)}, u32[]{:S(2)}, u32[]{:S(2)}) async-start(bf16[128,80,256]{2,1,0:T(8,128)(2,1)} %shard_map.118), calls=%async_computation.1 | async-start | bytes 10485760 | tf_op jit(solution)/shard_map/all_to_all | solution.py:603
  128.2 23.5 %copy-start = (bf16[1024,2048]{1,0:T(8,128)(2,1)S(1)}, bf16[1024,2048]{1,0:T(8,128)(2,1)}, u32[]{:S(2)}) copy-start(bf16[1024,2048]{1,0:T(8,128)(2,1)} %get-tuple-element.45.hot_ref) | copy-start | bytes 12582916

commit v3 on v2

--- a/solution.py
+++ b/solution.py
@@ -98,8 +98,7 @@
     rows_hbm,
     cols_hbm,
     coef_hbm,
-    elevation_ref,
-    phi_ref,
+    fields_ref,
     plan_ref,
     along_a,
     along_b,
@@ -118,8 +117,8 @@
     small = [pltpu.make_async_copy(a, b, sems.at[i]) for i, (a, b) in enumerate(small)]
     fields = []
     for x in range(16):
-        fields.append((elevation_hbm.at[:, x, :], elevation_ref.at[x]))
-        fields.append((phi_hbm.at[:, x, :], phi_ref.at[x]))
+        fields.append((elevation_hbm.at[:, x, :], fields_ref.at[x]))
+        fields.append((phi_hbm.at[:, x, :], fields_ref.at[16 + x]))
     fields = [pltpu.make_async_copy(a, b, field_sems.at[i]) for i, (a, b) in enumerate(fields)]
     for copy in fields + small:
         copy.start()
@@ -133,17 +132,17 @@
     lane = iota((WAVES, 128), 1)
     right = jnp.zeros((WAVES, 128), F32)
     left = jnp.zeros((WAVES, 128), F32)
-    for k, ref in enumerate((elevation_ref, phi_ref)):
+    for k in range(2):
         for x in range(16):
-            values = ref[x]
+            values = fields_ref[16 * k + x]
             at = 64 * k + 2 * x
             here = (lane >> 1) == at // 2
             right = jnp.where(here, pltpu.roll(values, (at + 2) % 128, 1), right)
             left = jnp.where(here, pltpu.roll(values, at, 1) if at else values, left)
     across_a[...] = jnp.where(even_col, right, left)
     across_b[...] = jnp.where(even_col, left, right)
-    upward = phi_ref[0]
-    for k, downward in enumerate((elevation_ref[14], elevation_ref[15], phi_ref[14], phi_ref[15])):
+    upward = fields_ref[16]
+    for k, downward in enumerate([fields_ref[n] for n in (14, 15, 30, 31)]):
         along_a[k] = jnp.where(even_row, downward, upward)
         along_b[k] = jnp.where(even_row, upward, downward)
 
@@ -151,12 +150,12 @@
 def pack_edges(elevation, velocity_pot, panel_slot, far_rows, far_cols, coef):
     side = jax.ShapeDtypeStruct((WAVES, 128), F32)
     rows = jax.ShapeDtypeStruct((4, WAVES, 128), F32)
-    track = jax.ShapeDtypeStruct((16, WAVES, 128), F32)
+    tracks = jax.ShapeDtypeStruct((32, WAVES, 128), F32)
     return call(
         pack_kernel,
-        (track, track, jax.ShapeDtypeStruct((40, 128), F32), rows, rows, side, side),
+        (tracks, jax.ShapeDtypeStruct((40, 128), F32), rows, rows, side, side),
         [HBM] * 6,
-        (VMEM,) * 7,
+        (VMEM,) * 6,
         [
             pltpu.VMEM((24, 128), jnp.int32),
             pltpu.SemaphoreType.DMA((4,)),
@@ -226,8 +225,7 @@
 
 def surface_kernel(
     plan_ref,
-    elevation_ref,
-    phi_ref,
+    fields,
     along_a,
     along_b,
     across_a,
@@ -255,9 +253,9 @@
     above = [jnp.where(first_row, 0.0, values) for values in above]
     below = jnp.where(last_row, 0.0, jnp.where(even_row, along_a[0], along_b[0]))
 
-    def views(f, x, k, ref):
-        x1 = ref[x - 1] if x >= 1 else above[2 * k + 1]
-        x2 = ref[x - 2] if x >= 2 else above[2 * k + x]
+    def views(f, x, k):
+        x1 = fields[16 * k + x - 1] if x >= 1 else above[2 * k + 1]
+        x2 = fields[16 * k + x - 2] if x >= 2 else above[2 * k + x]
         at = 64 * k + 2 * x
         left = pltpu.roll(west, 128 - at, 1) if at else west
         right = pltpu.roll(east, 126 - at, 1)
@@ -273,10 +271,10 @@
     stack[0:128, pl.ds(PANELS, 128)] = jnp.zeros((128, 128), BF16)
     stores = []
     for x in range(16):
-        e, p = elevation_ref[x], phi_ref[x]
-        _, _, _, up, across = views(e, x, 0, elevation_ref)
-        p1, pw, pe, phi_up, phi_across = views(p, x, 1, phi_ref)
-        next_row = phi_ref[x + 1] if x < 15 else below
+        e, p = fields[x], fields[16 + x]
+        _, _, _, up, across = views(e, x, 0)
+        p1, pw, pe, phi_up, phi_across = views(p, x, 1)
+        next_row = fields[17 + x] if x < 15 else below
         curvature = next_row + p1 + pe + pw - 4.0 * p
         eta = e - 0.4 * up + 0.3 * across + plan_ref[24 + x : 25 + x, :] * curvature
         eta_tracks[x] = eta
@@ -319,7 +317,7 @@
             jax.ShapeDtypeStruct((WAVES, 16, 128), F32),
             jax.ShapeDtypeStruct((ROWS, 256), BF16),
         ),
-        [VMEM] * 10,
+        [VMEM] * 9,
         (HBM, HBM),
         [
             pltpu.VMEM((16, WAVES, 128), F32),
@@ -329,7 +327,7 @@
             pltpu.SemaphoreType.DMA((4,)),
         ],
         limit=12,
-    )(plan, *fields, *halo, hot, place, table)
+    )(plan, fields, *halo, hot, place, table)
 
 
 def cluster_kernel(arrived_ref, clustered_ref, info_ref, hot, right):
@@ -516,7 +514,6 @@
         (iota((128, 256), 0) & 7) == 0
     )
     spread = spread.astype(F32).astype(BF16)
-    identity = (iota((128, 128), 0) == iota((128, 128), 1)).astype(F32).astype(BF16)
     copies[0].wait()
     for m in range(8):
         src = pl.ds(m * 16, 16)
@@ -524,23 +521,23 @@
         rows = dot(info_ref[:, pl.ds(m * 128, 128)].astype(BF16), spread)
         for part in range(2):
             mine = coeffs[src, :, pl.ds(part * 128, 128)].reshape(256, 128)
-            turned = dot_nt(identity, mine).astype(BF16)
+            turned = mine.astype(F32).T.astype(BF16)
             for s in range(2):
                 for cluster in range(8):
                     hit = (rows[2 + s : 3 + s] == float(cluster)).astype(F32).astype(BF16)
                     values = turned[s * 64 : s * 64 + 64] * hit
                     masked[2 * s + part, pl.ds(cluster * 64, 64), at] = values
-    for n in range(4):
-        copies[1 + n].wait()
-        product = dot(masked[n], basis[n].reshape(2048, CL))
-        if n == 0:
-            acc[...] = product
-        else:
-            acc[...] += product
+    for copy in copies[1:]:
+        copy.wait()
+    for r in range(0, 512, 128):
+        at = pl.ds(r, 128)
+        product = dot(masked[0, at, :], basis[0].reshape(2048, CL))
+        for n in range(1, 4):
+            product += dot(masked[n, at, :], basis[n].reshape(2048, CL))
+        acc[at, :] = product
     for cluster in range(8):
         total = near_ref[cluster] + acc[pl.ds(cluster * 64, 64), :]
         grid[pl.ds((cluster >> 2) * 64, 64), pl.ds((cluster & 3) * 256, 256)] = total.astype(BF16)
-    copies[5].wait()
     stores = []
     for m in range(0, ROWS, 256):
         at = pl.ds(m, 256)
@@ -628,7 +625,7 @@
 ):
     per_owner, clusters = 8, 1024
     me = lax.axis_index(BOTH)
-    *fields, plan, along_a, along_b, across_a, across_b = pack_edges(
+    fields, plan, along_a, along_b, across_a, across_b = pack_edges(
         elevation, velocity_pot, panel_slot, far_rows, far_cols, surface_coef
     )
     along_a = lax.ppermute(along_a, "along", swap("along", 0))

time: 154 us -> 153 us (level)
  no operation moved by 1% of the time
where the time goes in v3:
time: 153 us
  waiting for transfers between devices  64.5 us (42%)
  Pallas kernels  45.5 us (30%)
  starting transfers between devices  24.6 us (16%)
  blocking collectives  15.1 us (10%)
  local copies, waits for them, and re-layouts  2.03 us (1%)
    all_to_all x2, waiting for transfers between devices, exchange(): return lax.all_to_all(x, BOTH, split_axis=0, concat_axis=0, tiled=True)  61.1 us
    all_to_all x2, starting transfers between devices, exchange(): return lax.all_to_all(x, BOTH, split_axis=0, concat_axis=0, tiled=True)  17.2 us
    all_to_all x1, blocking collectives, exchange(): return lax.all_to_all(x, BOTH, split_axis=0, concat_axis=0, tiled=True)  15.1 us
    pallas_call x1, Pallas kernels, near_product(): pl.pallas_call(near_kernel, out_shape=(jax.ShapeDtypeStruct((8, WAVES, CL...  12.6 us
    pallas_call x1, Pallas kernels, total_home(): call(total_kernel, jax.ShapeDtypeStruct((ROWS, 128), BF16), [HBM, VMEM, H...  8.21 us
    pallas_call x1, Pallas kernels, add_coeff(): pl.pallas_call(coeff_kernel, out_shape=jax.ShapeDtypeStruct((OWNERS, 80,...  6.44 us
    pallas_call x1, Pallas kernels, far_bucket(): call(bucket_kernel, jax.ShapeDtypeStruct((OWNERS, 80, CL), BF16), [SMEM,...  5.06 us
    pallas_call x1, Pallas kernels, surface_payload(): call(surface_kernel, (jax.ShapeDtypeStruct((WAVES, 16, 128), F32), jax.Sh...  4.84 us
  transfers between devices with their start and end apart: 8, of which 3 were waited for; matrix products, arithmetic and copies ran while one was open for 0% of the time, Pallas kernels for 17%

profile of v3, /device:TPU:1, one launch (start us, length us, event | category | flops | bytes accessed | tf_op | source)
XLA Modules:
  0.0 152.5 jit_solution(3413511166704848526)
XLA Ops:
  0.6 2.9 %shard_map.113 = (f32[32,64,128]{2,1,0:T(8,128)}, f32[40,128]{1,0:T(8,128)}, f32[4,64,128]{2,1,0:T(8,128)}, f32[4,64,128]{2,1,0:T(8,128)}, f32[64,128]{1,0:T(8,128)}, /*index=5*/f32[64,128]{1,0:T(8,128)}) custom-call(f32[64,16,128]{2,1,0:T(8,128)} %elevation_hbm.1, f32[64,16,128]{2,1,0:T(8,128)} %phi_hbm.1, s32[16,128]{1,0:T(8,128)} %slot_hbm.1, ...), custom_call_target="tpu_custom_call" | custom-call | tf_op jit(solution)/shard_map/pallas_call | solution.py:154
  3.6 1.5 collective-permute-start
  5.1 1.4 collective-permute-start.1
  6.4 1.2 collective-permute-start.2
  7.7 1.8 %collective-permute-start.3 = (f32[64,128]{1,0:T(8,128)}, f32[64,128]{1,0:T(8,128)S(1)}, u32[]{:S(2)}, u32[]{:S(2)}) collective-permute-start(f32[64,128]{1,0:T(8,128)} %get-tuple-element.28), channel_id=1, source_target_pairs={{1,2},{3,0},{2,1},{0,3},{5,6},{7,4},{6,5},{4,7},{9,10},{11,8},{10,... | collective-permute-start | bytes 98312 | tf_op jit(solution)/shard_map/ppermute | solution.py:634
  9.5 0.0 copy-start.2
  9.5 0.7 copy-done.2
  10.2 1.8 %shard_map.114 = (bf16[1024,2048]{1,0:T(8,128)(2,1)S(1)}, s32[8,2048]{1,0:T(8,128)S(1)}, s32[8,128]{1,0:T(8,128)S(1)}) custom-call(f32[40,128]{1,0:T(8,128)S(1)} %copy-done.2), custom_call_target="tpu_custom_call" | custom-call | tf_op jit(solution)/shard_map/pallas_call | solution.py:213
  12.0 0.0 collective-permute-done.2.across_a
  12.0 0.0 collective-permute-done.3.across_b
  12.0 0.0 collective-permute-done.along_a
  12.1 0.0 collective-permute-done.1.along_b
  12.1 0.0 copy-start.1
  12.1 1.2 copy-done.1
  13.3 4.8 %shard_map.115 = (f32[64,16,128]{2,1,0:T(8,128)}, bf16[1024,256]{1,0:T(8,128)(2,1)}) custom-call(f32[40,128]{1,0:T(8,128)S(1)} %copy-done.2, f32[32,64,128]{2,1,0:T(8,128)S(1)} %copy-done.1, f32[4,64,128]{2,1,0:T(8,128)S(1)} %collective-permute-done.along_a, f32[4,64,128]{2,1,0:T(8,128)S(1)} %collective-permute-done.1.along_b, ...), custom_call_target="tpu_custom_call" | custom-call | tf_op jit(solution)/shard_map/pallas_call | solution.py:314
  18.1 11.0 %all-to-all-start = ((bf16[128,8,256]{2,1,0:T(8,128)(2,1)}), bf16[128,8,256]{2,1,0:T(8,128)(2,1)S(1)}, u32[]{:S(2)}, u32[]{:S(2)}) async-start(bf16[128,8,256]{2,1,0:T(8,128)(2,1)} %bitcast.2), calls=%async_computation | async-start | bytes 1048576 | tf_op jit(solution)/shard_map/all_to_all | solution.py:600
  29.1 5.1 %shard_map.116.big_hbm = bf16[128,80,256]{2,1,0:T(8,128)(2,1)} custom-call(s32[1024]{0:T(1024)S(1)} %bitcast.10, bf16[128,32,256]{2,1,0:T(8,128)(2,1)} %u_hbm.1), custom_call_target="tpu_custom_call" | custom-call | bytes 9437184 | tf_op jit(solution)/shard_map/pallas_call | solution.py:71
  34.2 8.9 %all-to-all-done = bf16[128,8,256]{2,1,0:T(8,128)(2,1)S(1)} async-done(((bf16[128,8,256]{2,1,0:T(8,128)(2,1)}), bf16[128,8,256]{2,1,0:T(8,128)(2,1)S(1)}, u32[]{:S(2)}, u32[]{:S(2)}) %all-to-all-start) | async-done | bytes 524320 | tf_op jit(solution)/shard_map/all_to_all | solution.py:600
  43.1 1.7 %shard_map.117 = (bf16[1024,128]{1,0:T(8,128)(2,1)S(1)}, f32[8,1024]{1,0:T(8,128)S(1)}) custom-call(bf16[1024,256]{1,0:T(8,128)(2,1)S(1)} %bitcast.7), custom_call_target="tpu_custom_call" | custom-call | tf_op jit(solution)/shard_map/pallas_call | solution.py:357
  44.8 1.5 collective-permute-start.5
  46.3 0.1 collective-permute-start.4
  46.4 6.4 %shard_map.118 = bf16[128,80,256]{2,1,0:T(8,128)(2,1)} custom-call(s32[1024]{0:T(1024)S(1)} %bitcast.11, bf16[1024,128]{1,0:T(8,128)(2,1)S(1)} %get-tuple-element.35.clustered_ref.own_ref, bf16[128,32,256]{2,1,0:T(8,128)(2,1)} %v_hbm.1, bf16[128,80,256]{2,1,0:T(8,128)(2,1)} %shard_map.116.big_hbm), custom_call_target="tpu_custom_call", output_to_operand_aliasing={{}: (3, {})} | custom-call | bytes 33554432 | tf_op jit(solution)/shard_map/pallas_call | solution.py:410
  52.8 0.0 copy-start.3
  52.8 0.0 collective-permute-done.5.after_ref
  52.8 3.4 %collective-permute-done.4.before_ref = bf16[1024,128]{1,0:T(8,128)(2,1)S(1)} collective-permute-done((bf16[1024,128]{1,0:T(8,128)(2,1)S(1)}, bf16[1024,128]{1,0:T(8,128)(2,1)S(1)}, u32[]{:S(2)}, u32[]{:S(2)}) %collective-permute-start.4) | collective-permute-done | bytes 262176 | tf_op jit(solution)/shard_map/ppermute | solution.py:644
  56.3 6.2 %all-to-all-start.1 = ((bf16[128,80,256]{2,1,0:T(8,128)(2,1)}), bf16[128,80,256]{2,1,0:T(8,128)(2,1)}, u32[]{:S(2)}, u32[]{:S(2)}) async-start(bf16[128,80,256]{2,1,0:T(8,128)(2,1)} %shard_map.118), calls=%async_computation.1 | async-start | bytes 10485760 | tf_op jit(solution)/shard_map/all_to_all | solution.py:600
  62.5 0.0 copy-done.3
  62.6 0.1 reshape.33.rel_ref
  62.7 12.6 %shard_map.119 = (f32[8,64,256]{2,1,0:T(8,128)S(1)}, bf16[1024,2048]{1,0:T(8,128)(2,1)}, bf16[1024,2048]{1,0:T(8,128)(2,1)}) custom-call(s32[72]{0:T(128)S(1)} %reshape.33.rel_ref, bf16[1024,128]{1,0:T(8,128)(2,1)S(1)} %collective-permute-done.4.before_ref, bf16[1024,128]{1,0:T(8,128)(2,1)S(1)} %get-tuple-element.35.clustered_ref.own_ref, ...), custom_call_target="tpu_custom_call" | custom-call | bytes 536870912 | tf_op jit(solution)/shard_map/pallas_call | solution.py:470
  75.3 52.2 %all-to-all-done.1.big_hbm = bf16[128,80,256]{2,1,0:T(8,128)(2,1)} async-done(((bf16[128,80,256]{2,1,0:T(8,128)(2,1)}), bf16[128,80,256]{2,1,0:T(8,128)(2,1)}, u32[]{:S(2)}, u32[]{:S(2)}) %all-to-all-start.1) | async-done | bytes 5242912 | tf_op jit(solution)/shard_map/all_to_all | solution.py:600
  127.5 0.0 copy-start
  127.5 8.2 %shard_map.120 = bf16[1024,128]{1,0:T(8,128)(2,1)S(1)} custom-call(bf16[128,80,256]{2,1,0:T(8,128)(2,1)} %all-to-all-done.1.big_hbm, f32[8,64,256]{2,1,0:T(8,128)S(1)} %get-tuple-element.41.near_ref, bf16[1024,2048]{1,0:T(8,128)(2,1)} %get-tuple-element.42.hot_hbm, f32[8,1024]{1,0:T(8,128)S(1)} %get-tuple-element.40.info_ref), custom_call_target="tpu_custom_call" | custom-call | tf_op jit(solution)/shard_map/pallas_call | solution.py:557
  135.7 15.1 %all_to_all.15 = bf16[128,8,128]{2,1,0:T(8,128)(2,1)S(1)} all-to-all(bf16[128,8,128]{2,1,0:T(8,128)(2,1)S(1)} %bitcast.8), channel_id=1, replica_groups=mesh['along'=32,'across'=4] {'along','across'}, dimensions={0} | all-to-all | bytes 524288 | tf_op jit(solution)/shard_map/all_to_all | solution.py:600
  150.8 0.0 copy-done
  150.8 1.8 %shard_map.121 = bf16[64,16,128]{2,1,0:T(8,128)(2,1)} custom-call(bf16[1024,128]{1,0:T(8,128)(2,1)S(1)} %bitcast.9, bf16[1024,2048]{1,0:T(8,128)(2,1)S(1)} %copy-done, s32[8,2048]{1,0:T(8,128)S(1)} %get-tuple-element.30.place_ref), custom_call_target="tpu_custom_call" | custom-call | tf_op jit(solution)/shard_map/pallas_call | solution.py:590
  (1 shorter events, 0.0 us)
Async XLA Ops:
  3.6 8.5 %collective-permute-start = (f32[4,64,128]{2,1,0:T(8,128)}, f32[4,64,128]{2,1,0:T(8,128)S(1)}, u32[]{:S(2)}, u32[]{:S(2)}) collective-permute-start(f32[4,64,128]{2,1,0:T(8,128)} %get-tuple-element.25), channel_id=1, source_target_pairs={{0,4},{8,12},{16,20},{24,28},{32,36},{40,44},{48,52},{56,60},{64,6... | collective-permute-start | bytes 393224 | tf_op jit(solution)/shard_map/ppermute | solution.py:631
  5.1 7.0 %collective-permute-start.1 = (f32[4,64,128]{2,1,0:T(8,128)}, f32[4,64,128]{2,1,0:T(8,128)S(1)}, u32[]{:S(2)}, u32[]{:S(2)}) collective-permute-start(f32[4,64,128]{2,1,0:T(8,128)} %get-tuple-element.26), channel_id=1, source_target_pairs={{4,8},{12,16},{20,24},{28,32},{36,40},{44,48},{52,56},{60,64},{68,... | collective-permute-start | bytes 393224 | tf_op jit(solution)/shard_map/ppermute | solution.py:632
  6.4 5.6 %collective-permute-start.2 = (f32[64,128]{1,0:T(8,128)}, f32[64,128]{1,0:T(8,128)S(1)}, u32[]{:S(2)}, u32[]{:S(2)}) collective-permute-start(f32[64,128]{1,0:T(8,128)} %get-tuple-element.27), channel_id=1, source_target_pairs={{0,1},{2,3},{1,0},{3,2},{4,5},{6,7},{5,4},{7,6},{8,9},{10,11},{9,8... | collective-permute-start | bytes 98312 | tf_op jit(solution)/shard_map/ppermute | solution.py:633
  7.7 4.4 %collective-permute-start.3 = (f32[64,128]{1,0:T(8,128)}, f32[64,128]{1,0:T(8,128)S(1)}, u32[]{:S(2)}, u32[]{:S(2)}) collective-permute-start(f32[64,128]{1,0:T(8,128)} %get-tuple-element.28), channel_id=1, source_target_pairs={{1,2},{3,0},{2,1},{0,3},{5,6},{7,4},{6,5},{4,7},{9,10},{11,8},{10,... | collective-permute-start | bytes 98312 | tf_op jit(solution)/shard_map/ppermute | solution.py:634
  9.5 0.7 copy-start.2
  12.1 1.2 copy-start.1
  18.1 24.9 %all-to-all-start = ((bf16[128,8,256]{2,1,0:T(8,128)(2,1)}), bf16[128,8,256]{2,1,0:T(8,128)(2,1)S(1)}, u32[]{:S(2)}, u32[]{:S(2)}) async-start(bf16[128,8,256]{2,1,0:T(8,128)(2,1)} %bitcast.2), calls=%async_computation | async-start | bytes 1048576 | tf_op jit(solution)/shard_map/all_to_all | solution.py:600
  44.8 8.0 %collective-permute-start.5 = (bf16[1024,128]{1,0:T(8,128)(2,1)S(1)}, bf16[1024,128]{1,0:T(8,128)(2,1)S(1)}, u32[]{:S(2)}, u32[]{:S(2)}) collective-permute-start(bf16[1024,128]{1,0:T(8,128)(2,1)S(1)} %get-tuple-element.35.clustered_ref.own_ref), channel_id=1, source_target_pairs={{0,127},{1,0},{2,1},{3,2},{4,3},{5,4},{6,5},{7,6},{8,7},{9,8},{10,... | collective-permute-start | bytes 786440 | tf_op jit(solution)/shard_map/ppermute | solution.py:645
  46.3 10.0 %collective-permute-start.4 = (bf16[1024,128]{1,0:T(8,128)(2,1)S(1)}, bf16[1024,128]{1,0:T(8,128)(2,1)S(1)}, u32[]{:S(2)}, u32[]{:S(2)}) collective-permute-start(bf16[1024,128]{1,0:T(8,128)(2,1)S(1)} %get-tuple-element.35.clustered_ref.own_ref), channel_id=1, source_target_pairs={{0,1},{1,2},{2,3},{3,4},{4,5},{5,6},{6,7},{7,8},{8,9},{9,10},{10,1... | collective-permute-start | bytes 786440 | tf_op jit(solution)/shard_map/ppermute | solution.py:644
  52.8 9.7 %copy-start.3 = (s32[8,9]{1,0:T(8,128)S(1)}, s32[8,9]{1,0:T(8,128)}, u32[]{:S(2)}) copy-start(s32[8,9]{1,0:T(8,128)} %param.15) | copy-start | bytes 868
  56.3 71.2 %all-to-all-start.1 = ((bf16[128,80,256]{2,1,0:T(8,128)(2,1)}), bf16[128,80,256]{2,1,0:T(8,128)(2,1)}, u32[]{:S(2)}, u32[]{:S(2)}) async-start(bf16[128,80,256]{2,1,0:T(8,128)(2,1)} %shard_map.118), calls=%async_computation.1 | async-start | bytes 10485760 | tf_op jit(solution)/shard_map/all_to_all | solution.py:600
  127.5 23.3 %copy-start = (bf16[1024,2048]{1,0:T(8,128)(2,1)S(1)}, bf16[1024,2048]{1,0:T(8,128)(2,1)}, u32[]{:S(2)}) copy-start(bf16[1024,2048]{1,0:T(8,128)(2,1)} %get-tuple-element.43.hot_ref) | copy-start | bytes 12582916

commit v4 on v3

--- a/solution.py
+++ b/solution.py
@@ -429,14 +429,11 @@
     before_ref,
     own_ref,
     after_ref,
-    info_ref,
     place_ref,
     blocks_ref,
     out_ref,
-    unhot_hbm,
     hot_hbm,
     wide,
-    unhot,
     hot,
     sems,
 ):
@@ -451,9 +448,6 @@
                 wide[8 * k + 4 + q] = turned[64:128]
 
     lanes = pl.ds(pl.multiple_of(c * 256, 256), 256)
-    info = info_ref[:, pl.ds(pl.multiple_of(lax.rem(c, 4) * 256, 256), 256)]
-    slot = jnp.where(c < 4, info[0:1], info[1:2]).astype(jnp.int32)
-    unhot[:, lanes] = hot_block(1024, slot & 1023)
     hot[:, lanes] = hot_block(ROWS, place_ref[3:4, lanes])
     total = jnp.zeros((WAVES, CL), F32)
     for k in range(9):
@@ -462,79 +456,58 @@
 
     @pl.when(c == 7)
     def _():
-        load([(unhot, unhot_hbm), (hot, hot_hbm)], sems)
-
-
-def near_product(relative, before, own, after, info, place, near_blocks):
+        load([(hot, hot_hbm)], sems)
+
+
+def near_product(relative, before, own, after, place, near_blocks):
     matrix = jax.ShapeDtypeStruct((1024, PANELS), BF16)
     return pl.pallas_call(
         near_kernel,
-        out_shape=(jax.ShapeDtypeStruct((8, WAVES, CL), F32), matrix, matrix),
+        out_shape=(jax.ShapeDtypeStruct((8, WAVES, CL), F32), matrix),
         grid_spec=pltpu.PrefetchScalarGridSpec(
             num_scalar_prefetch=1,
             grid=(8,),
-            in_specs=[VMEM] * 5 + [pl.BlockSpec((1, 9, CL, CL), lambda c, r: (c, 0, 0, 0))],
-            out_specs=(pl.BlockSpec((1, WAVES, CL), lambda c, r: (c, 0, 0)), HBM, HBM),
+            in_specs=[VMEM] * 4 + [pl.BlockSpec((1, 9, CL, CL), lambda c, r: (c, 0, 0, 0))],
+            out_specs=(pl.BlockSpec((1, WAVES, CL), lambda c, r: (c, 0, 0)), HBM),
             scratch_shapes=[
                 pltpu.VMEM((24, WAVES, CL), BF16),
                 pltpu.VMEM((1024, PANELS), BF16),
-                pltpu.VMEM((1024, PANELS), BF16),
-                pltpu.SemaphoreType.DMA((2,)),
+                pltpu.SemaphoreType.DMA((1,)),
             ],
         ),
         compiler_params=pltpu.CompilerParams(vmem_limit_bytes=TIGHT * 2**20),
         cost_estimate=pl.CostEstimate(flops=0, bytes_accessed=512 * 2**20, transcendentals=0),
-    )(relative, before, own, after, info, place, near_blocks)
-
-
-def total_kernel(
-    big_hbm,
-    near_ref,
-    hot_hbm,
-    info_ref,
-    out_hbm,
-    coeffs,
-    basis,
-    hot,
-    acc,
-    masked,
-    grid,
-    out,
-    sems,
-    out_sems,
-):
-    copies = [pltpu.make_async_copy(big_hbm.at[:, 64:80, :], coeffs, sems.at[4])]
-    for n in range(4):
-        part = big_hbm.at[:, pl.ds(16 * n, 16), :]
-        copies.append(pltpu.make_async_copy(part, basis.at[n], sems.at[n]))
-    copies.append(pltpu.make_async_copy(hot_hbm, hot, sems.at[5]))
-    for copy in copies:
-        copy.start()
+    )(relative, before, own, after, place, near_blocks)
+
+
+def total_kernel(big_ref, near_ref, info_ref, out_hbm, hot, acc, masked, grid, out, out_sems):
     spread = ((iota((128, 256), 0) >> 3) == (iota((128, 256), 1) >> 4)) & (
         (iota((128, 256), 0) & 7) == 0
     )
     spread = spread.astype(F32).astype(BF16)
-    copies[0].wait()
     for m in range(8):
         src = pl.ds(m * 16, 16)
         at = pl.ds(m * 256, 256)
         rows = dot(info_ref[:, pl.ds(m * 128, 128)].astype(BF16), spread)
         for part in range(2):
-            mine = coeffs[src, :, pl.ds(part * 128, 128)].reshape(256, 128)
+            mine = big_ref[src, 64:80, pl.ds(part * 128, 128)].reshape(256, 128)
             turned = mine.astype(F32).T.astype(BF16)
             for s in range(2):
                 for cluster in range(8):
                     hit = (rows[2 + s : 3 + s] == float(cluster)).astype(F32).astype(BF16)
                     values = turned[s * 64 : s * 64 + 64] * hit
                     masked[2 * s + part, pl.ds(cluster * 64, 64), at] = values
-    for copy in copies[1:]:
-        copy.wait()
+    basis = [big_ref[:, pl.ds(16 * n, 16), :].reshape(2048, CL) for n in range(4)]
     for r in range(0, 512, 128):
         at = pl.ds(r, 128)
-        product = dot(masked[0, at, :], basis[0].reshape(2048, CL))
+        product = dot(masked[0, at, :], basis[0])
         for n in range(1, 4):
-            product += dot(masked[n, at, :], basis[n].reshape(2048, CL))
+            product += dot(masked[n, at, :], basis[n])
         acc[at, :] = product
+    for half in range(2):
+        for m in range(0, ROWS, 128):
+            slot = info_ref[half : half + 1, pl.ds(m, 128)].astype(jnp.int32)
+            hot[:, pl.ds(half * ROWS + m, 128)] = hot_block(1024, slot & 1023)
     for cluster in range(8):
         total = near_ref[cluster] + acc[pl.ds(cluster * 64, 64), :]
         grid[pl.ds((cluster >> 2) * 64, 64), pl.ds((cluster & 3) * 256, 256)] = total.astype(BF16)
@@ -553,25 +526,22 @@
         copy.wait()
 
 
-def total_home(big, near, hot, info):
+def total_home(big, near, info):
     return call(
         total_kernel,
         jax.ShapeDtypeStruct((ROWS, 128), BF16),
-        [HBM, VMEM, HBM, VMEM],
+        [VMEM, VMEM, VMEM],
         HBM,
         [
-            pltpu.VMEM((OWNERS, 16, CL), BF16),
-            pltpu.VMEM((4, OWNERS, 16, CL), BF16),
             pltpu.VMEM((1024, PANELS), BF16),
             pltpu.VMEM((512, CL), F32),
             pltpu.VMEM((4, 512, 2048), BF16),
             pltpu.VMEM((128, 1024), BF16),
             pltpu.VMEM((ROWS, 128), BF16),
-            pltpu.SemaphoreType.DMA((6,)),
             pltpu.SemaphoreType.DMA((4,)),
         ],
-        limit=TIGHT,
-    )(big, near, hot, info)
+        limit=24,
+    )(big, near, info)
 
 
 def potential_kernel(returned_ref, hot_ref, place_ref, out_ref, turned, wide):
@@ -644,15 +614,15 @@
     before = lax.ppermute(clustered, BOTH, ring(BOTH, 1))
     after = lax.ppermute(clustered, BOTH, ring(BOTH, -1))
     big = add_coeff(table, clustered, far_v, big)
-    before, after, big = lax.optimization_barrier((before, after, big))
+    after, before, big = lax.optimization_barrier((after, before, big))
     big = exchange(big)
 
     relative = (near_cols - (me * per_owner - per_owner)) % clusters
-    near, unhot, hot = near_product(
-        relative.reshape(72), before, clustered, after, info, place, near_blocks
+    near, hot = near_product(
+        relative.reshape(72), before, clustered, after, place, near_blocks
     )
 
-    home = total_home(big, near, unhot, info).reshape(OWNERS, 8, 128)
+    home = total_home(big, near, info).reshape(OWNERS, 8, 128)
     returned = exchange(home).reshape(ROWS, 128)
     potential = panel_potential(returned, hot, place)
     return (eta, potential)

time: 153 us -> 153 us (level)
  Pallas kernels: 45.5 us -> 43.2 us
  waiting for transfers between devices: 64.5 us -> 66.1 us
    pallas_call x1, Pallas kernels: 12.6 us -> 11 us  [near_product(): pl.pallas_call(near_kernel, out_shape=(jax.ShapeDtypeStruct((8, WAVES, CL...]
    all_to_all x2, waiting for transfers between devices: 61.1 us -> 62.7 us  [exchange(): return lax.all_to_all(x, BOTH, split_axis=0, concat_axis=0, tiled=True)]
  transfers between devices with their start and end apart: 8 -> 8, of which waited for: 3 -> 3; matrix products, arithmetic and copies ran while one was open for 0% -> 0% of each run, Pallas kernels for 17% -> 16%
where the time goes in v4:
time: 153 us; the launch traced here: 152 us
  waiting for transfers between devices  66.1 us (43%)
  Pallas kernels  43.2 us (28%)
  starting transfers between devices  24.6 us (16%)
  blocking collectives  15.1 us (10%)
  local copies, waits for them, and re-layouts  2.03 us (1%)
    all_to_all x2, waiting for transfers between devices, exchange(): return lax.all_to_all(x, BOTH, split_axis=0, concat_axis=0, tiled=True)  62.7 us
    all_to_all x2, starting transfers between devices, exchange(): return lax.all_to_all(x, BOTH, split_axis=0, concat_axis=0, tiled=True)  17.2 us
    all_to_all x1, blocking collectives, exchange(): return lax.all_to_all(x, BOTH, split_axis=0, concat_axis=0, tiled=True)  15.1 us
    pallas_call x1, Pallas kernels, near_product(): pl.pallas_call(near_kernel, out_shape=(jax.ShapeDtypeStruct((8, WAVES, CL...  11 us
    pallas_call x1, Pallas kernels, total_home(): call(total_kernel, jax.ShapeDtypeStruct((ROWS, 128), BF16), [VMEM, VMEM,...  7.6 us
    pallas_call x1, Pallas kernels, add_coeff(): pl.pallas_call(coeff_kernel, out_shape=jax.ShapeDtypeStruct((OWNERS, 80,...  6.44 us
    pallas_call x1, Pallas kernels, far_bucket(): call(bucket_kernel, jax.ShapeDtypeStruct((OWNERS, 80, CL), BF16), [SMEM,...  5.06 us
    pallas_call x1, Pallas kernels, surface_payload(): call(surface_kernel, (jax.ShapeDtypeStruct((WAVES, 16, 128), F32), jax.Sh...  4.84 us
  transfers between devices with their start and end apart: 8, of which 3 were waited for; matrix products, arithmetic and copies ran while one was open for 0% of the time, Pallas kernels for 16%

profile of v4, /device:TPU:1, one launch (start us, length us, event | category | flops | bytes accessed | tf_op | source)
XLA Modules:
  0.0 151.9 jit_solution(16494368686817812359)
XLA Ops:
  0.6 2.9 %shard_map.113 = (f32[32,64,128]{2,1,0:T(8,128)}, f32[40,128]{1,0:T(8,128)}, f32[4,64,128]{2,1,0:T(8,128)}, f32[4,64,128]{2,1,0:T(8,128)}, f32[64,128]{1,0:T(8,128)}, /*index=5*/f32[64,128]{1,0:T(8,128)}) custom-call(f32[64,16,128]{2,1,0:T(8,128)} %elevation_hbm.1, f32[64,16,128]{2,1,0:T(8,128)} %phi_hbm.1, s32[16,128]{1,0:T(8,128)} %slot_hbm.1, ...), custom_call_target="tpu_custom_call" | custom-call | tf_op jit(solution)/shard_map/pallas_call | solution.py:154
  3.6 1.5 collective-permute-start
  5.1 1.4 collective-permute-start.1
  6.4 1.2 collective-permute-start.2
  7.7 1.8 %collective-permute-start.3 = (f32[64,128]{1,0:T(8,128)}, f32[64,128]{1,0:T(8,128)S(1)}, u32[]{:S(2)}, u32[]{:S(2)}) collective-permute-start(f32[64,128]{1,0:T(8,128)} %get-tuple-element.27), channel_id=1, source_target_pairs={{1,2},{3,0},{2,1},{0,3},{5,6},{7,4},{6,5},{4,7},{9,10},{11,8},{10,... | collective-permute-start | bytes 98312 | tf_op jit(solution)/shard_map/ppermute | solution.py:604
  9.5 0.0 copy-start.2
  9.5 0.7 copy-done.2
  10.2 1.8 %shard_map.114 = (bf16[1024,2048]{1,0:T(8,128)(2,1)S(1)}, s32[8,2048]{1,0:T(8,128)S(1)}, s32[8,128]{1,0:T(8,128)S(1)}) custom-call(f32[40,128]{1,0:T(8,128)S(1)} %copy-done.2), custom_call_target="tpu_custom_call" | custom-call | tf_op jit(solution)/shard_map/pallas_call | solution.py:213
  12.0 0.0 collective-permute-done.2.across_a
  12.0 0.0 collective-permute-done.3.across_b
  12.0 0.0 collective-permute-done.along_a
  12.1 0.0 collective-permute-done.1.along_b
  12.1 0.0 copy-start.1
  12.1 1.2 copy-done.1
  13.3 4.8 %shard_map.115 = (f32[64,16,128]{2,1,0:T(8,128)}, bf16[1024,256]{1,0:T(8,128)(2,1)}) custom-call(f32[40,128]{1,0:T(8,128)S(1)} %copy-done.2, f32[32,64,128]{2,1,0:T(8,128)S(1)} %copy-done.1, f32[4,64,128]{2,1,0:T(8,128)S(1)} %collective-permute-done.along_a, f32[4,64,128]{2,1,0:T(8,128)S(1)} %collective-permute-done.1.along_b, ...), custom_call_target="tpu_custom_call" | custom-call | tf_op jit(solution)/shard_map/pallas_call | solution.py:314
  18.1 11.0 %all-to-all-start = ((bf16[128,8,256]{2,1,0:T(8,128)(2,1)}), bf16[128,8,256]{2,1,0:T(8,128)(2,1)S(1)}, u32[]{:S(2)}, u32[]{:S(2)}) async-start(bf16[128,8,256]{2,1,0:T(8,128)(2,1)} %bitcast.2), calls=%async_computation | async-start | bytes 1048576 | tf_op jit(solution)/shard_map/all_to_all | solution.py:570
  29.1 5.1 %shard_map.116.big_hbm = bf16[128,80,256]{2,1,0:T(8,128)(2,1)} custom-call(s32[1024]{0:T(1024)S(1)} %bitcast.10, bf16[128,32,256]{2,1,0:T(8,128)(2,1)} %u_hbm.1), custom_call_target="tpu_custom_call" | custom-call | bytes 9437184 | tf_op jit(solution)/shard_map/pallas_call | solution.py:71
  34.2 8.9 %all-to-all-done = bf16[128,8,256]{2,1,0:T(8,128)(2,1)S(1)} async-done(((bf16[128,8,256]{2,1,0:T(8,128)(2,1)}), bf16[128,8,256]{2,1,0:T(8,128)(2,1)S(1)}, u32[]{:S(2)}, u32[]{:S(2)}) %all-to-all-start) | async-done | bytes 524320 | tf_op jit(solution)/shard_map/all_to_all | solution.py:570
  43.1 1.7 %shard_map.117 = (bf16[1024,128]{1,0:T(8,128)(2,1)S(1)}, f32[8,1024]{1,0:T(8,128)S(1)}) custom-call(bf16[1024,256]{1,0:T(8,128)(2,1)S(1)} %bitcast.7), custom_call_target="tpu_custom_call" | custom-call | tf_op jit(solution)/shard_map/pallas_call | solution.py:357
  44.8 1.5 collective-permute-start.4
  46.3 0.1 collective-permute-start.5
  46.4 6.4 %shard_map.118 = bf16[128,80,256]{2,1,0:T(8,128)(2,1)} custom-call(s32[1024]{0:T(1024)S(1)} %bitcast.11, bf16[1024,128]{1,0:T(8,128)(2,1)S(1)} %get-tuple-element.34.clustered_ref.own_ref, bf16[128,32,256]{2,1,0:T(8,128)(2,1)} %v_hbm.1, bf16[128,80,256]{2,1,0:T(8,128)(2,1)} %shard_map.116.big_hbm), custom_call_target="tpu_custom_call", output_to_operand_aliasing={{}: (3, {})} | custom-call | bytes 33554432 | tf_op jit(solution)/shard_map/pallas_call | solution.py:410
  52.8 0.0 copy-start.3
  52.8 0.0 collective-permute-done.4.after_ref
  52.8 3.4 %collective-permute-done.5.before_ref = bf16[1024,128]{1,0:T(8,128)(2,1)S(1)} collective-permute-done((bf16[1024,128]{1,0:T(8,128)(2,1)S(1)}, bf16[1024,128]{1,0:T(8,128)(2,1)S(1)}, u32[]{:S(2)}, u32[]{:S(2)}) %collective-permute-start.5) | collective-permute-done | bytes 262176 | tf_op jit(solution)/shard_map/ppermute | solution.py:614
  56.3 6.2 %all-to-all-start.1 = ((bf16[128,80,256]{2,1,0:T(8,128)(2,1)}), bf16[128,80,256]{2,1,0:T(8,128)(2,1)}, u32[]{:S(2)}, u32[]{:S(2)}) async-start(bf16[128,80,256]{2,1,0:T(8,128)(2,1)} %shard_map.118), calls=%async_computation.1 | async-start | bytes 10485760 | tf_op jit(solution)/shard_map/all_to_all | solution.py:570
  62.5 0.0 copy-done.3
  62.6 0.1 reshape.33.rel_ref
  62.7 11.0 %shard_map.119 = (f32[8,64,256]{2,1,0:T(8,128)S(1)}, bf16[1024,2048]{1,0:T(8,128)(2,1)}) custom-call(s32[72]{0:T(128)S(1)} %reshape.33.rel_ref, bf16[1024,128]{1,0:T(8,128)(2,1)S(1)} %collective-permute-done.5.before_ref, bf16[1024,128]{1,0:T(8,128)(2,1)S(1)} %get-tuple-element.34.clustered_ref.own_ref, ...), custom_call_target="tpu_custom_call" | custom-call | bytes 536870912 | tf_op jit(solution)/shard_map/pallas_call | solution.py:464
  73.7 53.8 %all-to-all-done.1.big_ref = bf16[128,80,256]{2,1,0:T(8,128)(2,1)} async-done(((bf16[128,80,256]{2,1,0:T(8,128)(2,1)}), bf16[128,80,256]{2,1,0:T(8,128)(2,1)}, u32[]{:S(2)}, u32[]{:S(2)}) %all-to-all-start.1) | async-done | bytes 5242912 | tf_op jit(solution)/shard_map/all_to_all | solution.py:570
  127.5 0.0 copy-start
  127.5 7.6 %shard_map.120 = bf16[1024,128]{1,0:T(8,128)(2,1)S(1)} custom-call(bf16[128,80,256]{2,1,0:T(8,128)(2,1)} %all-to-all-done.1.big_ref, f32[8,64,256]{2,1,0:T(8,128)S(1)} %get-tuple-element.39.near_ref, f32[8,1024]{1,0:T(8,128)S(1)} %get-tuple-element.40.info_ref), custom_call_target="tpu_custom_call" | custom-call | tf_op jit(solution)/shard_map/pallas_call | solution.py:530
  135.1 15.1 %all_to_all.15 = bf16[128,8,128]{2,1,0:T(8,128)(2,1)S(1)} all-to-all(bf16[128,8,128]{2,1,0:T(8,128)(2,1)S(1)} %bitcast.9), channel_id=1, replica_groups=mesh['along'=32,'across'=4] {'along','across'}, dimensions={0} | all-to-all | bytes 524288 | tf_op jit(solution)/shard_map/all_to_all | solution.py:570
  150.1 0.0 copy-done
  150.1 1.8 %shard_map.121 = bf16[64,16,128]{2,1,0:T(8,128)(2,1)} custom-call(bf16[1024,128]{1,0:T(8,128)(2,1)S(1)} %bitcast.8, bf16[1024,2048]{1,0:T(8,128)(2,1)S(1)} %copy-done, s32[8,2048]{1,0:T(8,128)S(1)} %get-tuple-element.29.place_ref), custom_call_target="tpu_custom_call" | custom-call | tf_op jit(solution)/shard_map/pallas_call | solution.py:560
  (1 shorter events, 0.0 us)
Async XLA Ops:
  3.6 8.5 %collective-permute-start = (f32[4,64,128]{2,1,0:T(8,128)}, f32[4,64,128]{2,1,0:T(8,128)S(1)}, u32[]{:S(2)}, u32[]{:S(2)}) collective-permute-start(f32[4,64,128]{2,1,0:T(8,128)} %get-tuple-element.24), channel_id=1, source_target_pairs={{0,4},{8,12},{16,20},{24,28},{32,36},{40,44},{48,52},{56,60},{64,6... | collective-permute-start | bytes 393224 | tf_op jit(solution)/shard_map/ppermute | solution.py:601
  5.1 7.0 %collective-permute-start.1 = (f32[4,64,128]{2,1,0:T(8,128)}, f32[4,64,128]{2,1,0:T(8,128)S(1)}, u32[]{:S(2)}, u32[]{:S(2)}) collective-permute-start(f32[4,64,128]{2,1,0:T(8,128)} %get-tuple-element.25), channel_id=1, source_target_pairs={{4,8},{12,16},{20,24},{28,32},{36,40},{44,48},{52,56},{60,64},{68,... | collective-permute-start | bytes 393224 | tf_op jit(solution)/shard_map/ppermute | solution.py:602
  6.4 5.6 %collective-permute-start.2 = (f32[64,128]{1,0:T(8,128)}, f32[64,128]{1,0:T(8,128)S(1)}, u32[]{:S(2)}, u32[]{:S(2)}) collective-permute-start(f32[64,128]{1,0:T(8,128)} %get-tuple-element.26), channel_id=1, source_target_pairs={{0,1},{2,3},{1,0},{3,2},{4,5},{6,7},{5,4},{7,6},{8,9},{10,11},{9,8... | collective-permute-start | bytes 98312 | tf_op jit(solution)/shard_map/ppermute | solution.py:603
  7.7 4.4 %collective-permute-start.3 = (f32[64,128]{1,0:T(8,128)}, f32[64,128]{1,0:T(8,128)S(1)}, u32[]{:S(2)}, u32[]{:S(2)}) collective-permute-start(f32[64,128]{1,0:T(8,128)} %get-tuple-element.27), channel_id=1, source_target_pairs={{1,2},{3,0},{2,1},{0,3},{5,6},{7,4},{6,5},{4,7},{9,10},{11,8},{10,... | collective-permute-start | bytes 98312 | tf_op jit(solution)/shard_map/ppermute | solution.py:604
  9.5 0.7 copy-start.2
  12.1 1.2 copy-start.1
  18.1 24.9 %all-to-all-start = ((bf16[128,8,256]{2,1,0:T(8,128)(2,1)}), bf16[128,8,256]{2,1,0:T(8,128)(2,1)S(1)}, u32[]{:S(2)}, u32[]{:S(2)}) async-start(bf16[128,8,256]{2,1,0:T(8,128)(2,1)} %bitcast.2), calls=%async_computation | async-start | bytes 1048576 | tf_op jit(solution)/shard_map/all_to_all | solution.py:570
  44.8 8.0 %collective-permute-start.4 = (bf16[1024,128]{1,0:T(8,128)(2,1)S(1)}, bf16[1024,128]{1,0:T(8,128)(2,1)S(1)}, u32[]{:S(2)}, u32[]{:S(2)}) collective-permute-start(bf16[1024,128]{1,0:T(8,128)(2,1)S(1)} %get-tuple-element.34.clustered_ref.own_ref), channel_id=1, source_target_pairs={{0,127},{1,0},{2,1},{3,2},{4,3},{5,4},{6,5},{7,6},{8,7},{9,8},{10,... | collective-permute-start | bytes 786440 | tf_op jit(solution)/shard_map/ppermute | solution.py:615
  46.3 10.0 %collective-permute-start.5 = (bf16[1024,128]{1,0:T(8,128)(2,1)S(1)}, bf16[1024,128]{1,0:T(8,128)(2,1)S(1)}, u32[]{:S(2)}, u32[]{:S(2)}) collective-permute-start(bf16[1024,128]{1,0:T(8,128)(2,1)S(1)} %get-tuple-element.34.clustered_ref.own_ref), channel_id=1, source_target_pairs={{0,1},{1,2},{2,3},{3,4},{4,5},{5,6},{6,7},{7,8},{8,9},{9,10},{10,1... | collective-permute-start | bytes 786440 | tf_op jit(solution)/shard_map/ppermute | solution.py:614
  52.8 9.7 %copy-start.3 = (s32[8,9]{1,0:T(8,128)S(1)}, s32[8,9]{1,0:T(8,128)}, u32[]{:S(2)}) copy-start(s32[8,9]{1,0:T(8,128)} %param.15) | copy-start | bytes 868
  56.3 71.2 %all-to-all-start.1 = ((bf16[128,80,256]{2,1,0:T(8,128)(2,1)}), bf16[128,80,256]{2,1,0:T(8,128)(2,1)}, u32[]{:S(2)}, u32[]{:S(2)}) async-start(bf16[128,80,256]{2,1,0:T(8,128)(2,1)} %shard_map.118), calls=%async_computation.1 | async-start | bytes 10485760 | tf_op jit(solution)/shard_map/all_to_all | solution.py:570
  127.5 22.7 %copy-start = (bf16[1024,2048]{1,0:T(8,128)(2,1)S(1)}, bf16[1024,2048]{1,0:T(8,128)(2,1)}, u32[]{:S(2)}) copy-start(bf16[1024,2048]{1,0:T(8,128)(2,1)} %get-tuple-element.41.hot_ref) | copy-start | bytes 12582916

commit v5 on v4

--- a/solution.py
+++ b/solution.py
@@ -278,7 +278,7 @@
         curvature = next_row + p1 + pe + pw - 4.0 * p
         eta = e - 0.4 * up + 0.3 * across + plan_ref[24 + x : 25 + x, :] * curvature
         eta_tracks[x] = eta
-        stores.append(pltpu.make_async_copy(eta_tracks.at[x], eta_hbm.at[:, x, :], eta_sems.at[x]))
+        stores.append(pltpu.make_async_copy(eta_tracks.at[x], eta_hbm.at[x], eta_sems.at[x]))
         stores[x].start()
         values = p - 0.4 * phi_up + 0.3 * phi_across - 0.5 * eta
         lanes = pl.ds(x * 128, 128)
@@ -314,7 +314,7 @@
     return call(
         surface_kernel,
         (
-            jax.ShapeDtypeStruct((WAVES, 16, 128), F32),
+            jax.ShapeDtypeStruct((16, WAVES, 128), F32),
             jax.ShapeDtypeStruct((ROWS, 256), BF16),
         ),
         [VMEM] * 9,
@@ -430,9 +430,11 @@
     own_ref,
     after_ref,
     place_ref,
+    eta_tracks,
     blocks_ref,
     out_ref,
     hot_hbm,
+    eta_hbm,
     wide,
     hot,
     sems,
@@ -456,28 +458,33 @@
 
     @pl.when(c == 7)
     def _():
-        load([(hot, hot_hbm)], sems)
-
-
-def near_product(relative, before, own, after, place, near_blocks):
+        tracks = [(eta_tracks.at[x], eta_hbm.at[:, x, :]) for x in range(16)]
+        load([(hot, hot_hbm)] + tracks, sems)
+
+
+def near_product(relative, before, own, after, place, eta, near_blocks):
     matrix = jax.ShapeDtypeStruct((1024, PANELS), BF16)
     return pl.pallas_call(
         near_kernel,
-        out_shape=(jax.ShapeDtypeStruct((8, WAVES, CL), F32), matrix),
+        out_shape=(
+                jax.ShapeDtypeStruct((8, WAVES, CL), F32),
+                matrix,
+                jax.ShapeDtypeStruct((WAVES, 16, 128), F32),
+        ),
         grid_spec=pltpu.PrefetchScalarGridSpec(
             num_scalar_prefetch=1,
             grid=(8,),
-            in_specs=[VMEM] * 4 + [pl.BlockSpec((1, 9, CL, CL), lambda c, r: (c, 0, 0, 0))],
-            out_specs=(pl.BlockSpec((1, WAVES, CL), lambda c, r: (c, 0, 0)), HBM),
+            in_specs=[VMEM] * 4 + [HBM, pl.BlockSpec((1, 9, CL, CL), lambda c, r: (c, 0, 0, 0))],
+            out_specs=(pl.BlockSpec((1, WAVES, CL), lambda c, r: (c, 0, 0)), HBM, HBM),
             scratch_shapes=[
                 pltpu.VMEM((24, WAVES, CL), BF16),
                 pltpu.VMEM((1024, PANELS), BF16),
-                pltpu.SemaphoreType.DMA((1,)),
+                pltpu.SemaphoreType.DMA((17,)),
             ],
         ),
         compiler_params=pltpu.CompilerParams(vmem_limit_bytes=TIGHT * 2**20),
         cost_estimate=pl.CostEstimate(flops=0, bytes_accessed=512 * 2**20, transcendentals=0),
-    )(relative, before, own, after, place, near_blocks)
+    )(relative, before, own, after, place, eta, near_blocks)
 
 
 def total_kernel(big_ref, near_ref, info_ref, out_hbm, hot, acc, masked, grid, out, out_sems):
@@ -618,8 +625,8 @@
     big = exchange(big)
 
     relative = (near_cols - (me * per_owner - per_owner)) % clusters
-    near, hot = near_product(
-        relative.reshape(72), before, clustered, after, place, near_blocks
+    near, hot, eta = near_product(
+        relative.reshape(72), before, clustered, after, place, eta, near_blocks
     )
 
     home = total_home(big, near, info).reshape(OWNERS, 8, 128)

time: 153 us -> 157 us (1.026)
  starting transfers between devices: 24.6 us -> 30.1 us
  waiting for transfers between devices: 66.1 us -> 62.9 us
  Pallas kernels: 43.2 us -> 45.5 us
    all_to_all x2, starting transfers between devices: 17.2 us -> 21.1 us  [exchange(): return lax.all_to_all(x, BOTH, split_axis=0, concat_axis=0, tiled=True)]
    ppermute x1, waiting for transfers between devices: 3.45 us -> 0.46 us  [body(): before = lax.ppermute(clustered, BOTH, ring(BOTH, 1))]
    pallas_call x1, Pallas kernels: 4.84 us -> 7.04 us  [surface_payload(): call(surface_kernel, (jax.ShapeDtypeStruct((16, WAVES, 128), F32), jax.Sh...]
where the time goes in v5:
time: 157 us; the launch traced here: 156 us
  waiting for transfers between devices  62.9 us (40%)
  Pallas kernels  45.5 us (29%)
  starting transfers between devices  30.1 us (19%)
  blocking collectives  15.1 us (10%)
  local copies, waits for them, and re-layouts  2.03 us (1%)
    all_to_all x2, waiting for transfers between devices, exchange(): return lax.all_to_all(x, BOTH, split_axis=0, concat_axis=0, tiled=True)  62.5 us
    all_to_all x2, starting transfers between devices, exchange(): return lax.all_to_all(x, BOTH, split_axis=0, concat_axis=0, tiled=True)  21.1 us
    all_to_all x1, blocking collectives, exchange(): return lax.all_to_all(x, BOTH, split_axis=0, concat_axis=0, tiled=True)  15.1 us
    pallas_call x1, Pallas kernels, near_product(): pl.pallas_call(near_kernel, out_shape=(jax.ShapeDtypeStruct((8, WAVES, CL...  11.1 us
    pallas_call x1, Pallas kernels, total_home(): call(total_kernel, jax.ShapeDtypeStruct((ROWS, 128), BF16), [VMEM, VMEM,...  7.61 us
    pallas_call x1, Pallas kernels, surface_payload(): call(surface_kernel, (jax.ShapeDtypeStruct((16, WAVES, 128), F32), jax.Sh...  7.04 us
    pallas_call x1, Pallas kernels, add_coeff(): pl.pallas_call(coeff_kernel, out_shape=jax.ShapeDtypeStruct((OWNERS, 80,...  6.45 us
    pallas_call x1, Pallas kernels, far_bucket(): call(bucket_kernel, jax.ShapeDtypeStruct((OWNERS, 80, CL), BF16), [SMEM,...  5.06 us
  transfers between devices with their start and end apart: 8, of which 3 were waited for; matrix products, arithmetic and copies ran while one was open for 0% of the time, Pallas kernels for 16%

profile of v5, /device:TPU:1, one launch (start us, length us, event | category | flops | bytes accessed | tf_op | source)
XLA Modules:
  0.0 156.4 jit_solution(14779242571106557332)
XLA Ops:
  0.6 2.9 %shard_map.113 = (f32[32,64,128]{2,1,0:T(8,128)}, f32[40,128]{1,0:T(8,128)}, f32[4,64,128]{2,1,0:T(8,128)}, f32[4,64,128]{2,1,0:T(8,128)}, f32[64,128]{1,0:T(8,128)}, /*index=5*/f32[64,128]{1,0:T(8,128)}) custom-call(f32[64,16,128]{2,1,0:T(8,128)} %elevation_hbm.1, f32[64,16,128]{2,1,0:T(8,128)} %phi_hbm.1, s32[16,128]{1,0:T(8,128)} %slot_hbm.1, ...), custom_call_target="tpu_custom_call" | custom-call | tf_op jit(solution)/shard_map/pallas_call | solution.py:154
  3.6 1.5 collective-permute-start
  5.1 1.4 collective-permute-start.1
  6.4 1.2 collective-permute-start.2
  7.7 1.8 %collective-permute-start.3 = (f32[64,128]{1,0:T(8,128)}, f32[64,128]{1,0:T(8,128)S(1)}, u32[]{:S(2)}, u32[]{:S(2)}) collective-permute-start(f32[64,128]{1,0:T(8,128)} %get-tuple-element.28), channel_id=1, source_target_pairs={{1,2},{3,0},{2,1},{0,3},{5,6},{7,4},{6,5},{4,7},{9,10},{11,8},{10,... | collective-permute-start | bytes 98312 | tf_op jit(solution)/shard_map/ppermute | solution.py:611
  9.5 0.0 copy-start.2
  9.5 0.7 copy-done.2
  10.2 1.8 %shard_map.114 = (bf16[1024,2048]{1,0:T(8,128)(2,1)S(1)}, s32[8,2048]{1,0:T(8,128)S(1)}, s32[8,128]{1,0:T(8,128)S(1)}) custom-call(f32[40,128]{1,0:T(8,128)S(1)} %copy-done.2), custom_call_target="tpu_custom_call" | custom-call | tf_op jit(solution)/shard_map/pallas_call | solution.py:213
  12.0 0.0 collective-permute-done.2.across_a
  12.0 0.0 collective-permute-done.3.across_b
  12.0 0.0 collective-permute-done.along_a
  12.1 0.0 collective-permute-done.1.along_b
  12.1 0.0 copy-start.1
  12.1 1.2 copy-done.1
  13.3 7.0 %shard_map.115 = (f32[16,64,128]{2,1,0:T(8,128)S(1)}, bf16[1024,256]{1,0:T(8,128)(2,1)}) custom-call(f32[40,128]{1,0:T(8,128)S(1)} %copy-done.2, f32[32,64,128]{2,1,0:T(8,128)S(1)} %copy-done.1, f32[4,64,128]{2,1,0:T(8,128)S(1)} %collective-permute-done.along_a, f32[4,64,128]{2,1,0:T(8,128)S(1)} %collective-permute-done.1.along_b, ...), custom_call_target="tpu_custom_call" | custom-call | tf_op jit(solution)/shard_map/pallas_call | solution.py:314
  20.3 11.0 %all-to-all-start = ((bf16[128,8,256]{2,1,0:T(8,128)(2,1)}), bf16[128,8,256]{2,1,0:T(8,128)(2,1)S(1)}, u32[]{:S(2)}, u32[]{:S(2)}) async-start(bf16[128,8,256]{2,1,0:T(8,128)(2,1)} %bitcast.2), calls=%async_computation | async-start | bytes 1048576 | tf_op jit(solution)/shard_map/all_to_all | solution.py:577
  31.3 5.1 %shard_map.116.big_hbm = bf16[128,80,256]{2,1,0:T(8,128)(2,1)} custom-call(s32[1024]{0:T(1024)S(1)} %bitcast.10, bf16[128,32,256]{2,1,0:T(8,128)(2,1)} %u_hbm.1), custom_call_target="tpu_custom_call" | custom-call | bytes 9437184 | tf_op jit(solution)/shard_map/pallas_call | solution.py:71
  36.4 8.9 %all-to-all-done = bf16[128,8,256]{2,1,0:T(8,128)(2,1)S(1)} async-done(((bf16[128,8,256]{2,1,0:T(8,128)(2,1)}), bf16[128,8,256]{2,1,0:T(8,128)(2,1)S(1)}, u32[]{:S(2)}, u32[]{:S(2)}) %all-to-all-start) | async-done | bytes 524320 | tf_op jit(solution)/shard_map/all_to_all | solution.py:577
  45.3 1.7 %shard_map.117 = (bf16[1024,128]{1,0:T(8,128)(2,1)S(1)}, f32[8,1024]{1,0:T(8,128)S(1)}) custom-call(bf16[1024,256]{1,0:T(8,128)(2,1)S(1)} %bitcast.7), custom_call_target="tpu_custom_call" | custom-call | tf_op jit(solution)/shard_map/pallas_call | solution.py:357
  47.0 0.4 collective-permute-start.5
  47.4 2.7 %collective-permute-start.4 = (bf16[1024,128]{1,0:T(8,128)(2,1)S(1)}, bf16[1024,128]{1,0:T(8,128)(2,1)S(1)}, u32[]{:S(2)}, u32[]{:S(2)}) collective-permute-start(bf16[1024,128]{1,0:T(8,128)(2,1)S(1)} %get-tuple-element.34.clustered_ref.own_ref), channel_id=1, source_target_pairs={{0,127},{1,0},{2,1},{3,2},{4,3},{5,4},{6,5},{7,6},{8,7},{9,8},{10,... | collective-permute-start | bytes 786440 | tf_op jit(solution)/shard_map/ppermute | solution.py:622
  50.1 6.4 %shard_map.118 = bf16[128,80,256]{2,1,0:T(8,128)(2,1)} custom-call(s32[1024]{0:T(1024)S(1)} %bitcast.11, bf16[1024,128]{1,0:T(8,128)(2,1)S(1)} %get-tuple-element.34.clustered_ref.own_ref, bf16[128,32,256]{2,1,0:T(8,128)(2,1)} %v_hbm.1, bf16[128,80,256]{2,1,0:T(8,128)(2,1)} %shard_map.116.big_hbm), custom_call_target="tpu_custom_call", output_to_operand_aliasing={{}: (3, {})} | custom-call | bytes 33554432 | tf_op jit(solution)/shard_map/pallas_call | solution.py:410
  56.5 0.0 copy-start.3
  56.5 0.5 collective-permute-done.5.before_ref
  57.0 0.0 collective-permute-done.4.after_ref
  57.0 10.2 %all-to-all-start.1 = ((bf16[128,80,256]{2,1,0:T(8,128)(2,1)}), bf16[128,80,256]{2,1,0:T(8,128)(2,1)}, u32[]{:S(2)}, u32[]{:S(2)}) async-start(bf16[128,80,256]{2,1,0:T(8,128)(2,1)} %shard_map.118), calls=%async_computation.1 | async-start | bytes 10485760 | tf_op jit(solution)/shard_map/all_to_all | solution.py:577
  67.2 0.0 copy-done.3
  67.2 0.1 reshape.28.rel_ref
  67.3 11.1 %shard_map.119 = (f32[8,64,256]{2,1,0:T(8,128)S(1)}, bf16[1024,2048]{1,0:T(8,128)(2,1)}, f32[64,16,128]{2,1,0:T(8,128)}) custom-call(s32[72]{0:T(128)S(1)} %reshape.28.rel_ref, bf16[1024,128]{1,0:T(8,128)(2,1)S(1)} %collective-permute-done.5.before_ref, bf16[1024,128]{1,0:T(8,128)(2,1)S(1)} %get-tuple-element.34.clustered_ref.own_ref, ...), custom_call_target="tpu_custom_call" | custom-call | bytes 536870912 | tf_op jit(solution)/shard_map/pallas_call | solution.py:467
  78.4 53.6 %all-to-all-done.1.big_ref = bf16[128,80,256]{2,1,0:T(8,128)(2,1)} async-done(((bf16[128,80,256]{2,1,0:T(8,128)(2,1)}), bf16[128,80,256]{2,1,0:T(8,128)(2,1)}, u32[]{:S(2)}, u32[]{:S(2)}) %all-to-all-start.1) | async-done | bytes 5242912 | tf_op jit(solution)/shard_map/all_to_all | solution.py:577
  132.0 0.0 copy-start
  132.0 7.6 %shard_map.120 = bf16[1024,128]{1,0:T(8,128)(2,1)S(1)} custom-call(bf16[128,80,256]{2,1,0:T(8,128)(2,1)} %all-to-all-done.1.big_ref, f32[8,64,256]{2,1,0:T(8,128)S(1)} %get-tuple-element.41.near_ref, f32[8,1024]{1,0:T(8,128)S(1)} %get-tuple-element.42.info_ref), custom_call_target="tpu_custom_call" | custom-call | tf_op jit(solution)/shard_map/pallas_call | solution.py:537
  139.6 15.1 %all_to_all.15 = bf16[128,8,128]{2,1,0:T(8,128)(2,1)S(1)} all-to-all(bf16[128,8,128]{2,1,0:T(8,128)(2,1)S(1)} %bitcast.8), channel_id=1, replica_groups=mesh['along'=32,'across'=4] {'along','across'}, dimensions={0} | all-to-all | bytes 524288 | tf_op jit(solution)/shard_map/all_to_all | solution.py:577
  154.6 0.0 copy-done
  154.6 1.8 %shard_map.121 = bf16[64,16,128]{2,1,0:T(8,128)(2,1)} custom-call(bf16[1024,128]{1,0:T(8,128)(2,1)S(1)} %bitcast.9, bf16[1024,2048]{1,0:T(8,128)(2,1)S(1)} %copy-done, s32[8,2048]{1,0:T(8,128)S(1)} %get-tuple-element.30.place_ref), custom_call_target="tpu_custom_call" | custom-call | tf_op jit(solution)/shard_map/pallas_call | solution.py:567
  (1 shorter events, 0.0 us)
Async XLA Ops:
  3.6 8.5 %collective-permute-start = (f32[4,64,128]{2,1,0:T(8,128)}, f32[4,64,128]{2,1,0:T(8,128)S(1)}, u32[]{:S(2)}, u32[]{:S(2)}) collective-permute-start(f32[4,64,128]{2,1,0:T(8,128)} %get-tuple-element.25), channel_id=1, source_target_pairs={{0,4},{8,12},{16,20},{24,28},{32,36},{40,44},{48,52},{56,60},{64,6... | collective-permute-start | bytes 393224 | tf_op jit(solution)/shard_map/ppermute | solution.py:608
  5.1 7.0 %collective-permute-start.1 = (f32[4,64,128]{2,1,0:T(8,128)}, f32[4,64,128]{2,1,0:T(8,128)S(1)}, u32[]{:S(2)}, u32[]{:S(2)}) collective-permute-start(f32[4,64,128]{2,1,0:T(8,128)} %get-tuple-element.26), channel_id=1, source_target_pairs={{4,8},{12,16},{20,24},{28,32},{36,40},{44,48},{52,56},{60,64},{68,... | collective-permute-start | bytes 393224 | tf_op jit(solution)/shard_map/ppermute | solution.py:609
  6.4 5.6 %collective-permute-start.2 = (f32[64,128]{1,0:T(8,128)}, f32[64,128]{1,0:T(8,128)S(1)}, u32[]{:S(2)}, u32[]{:S(2)}) collective-permute-start(f32[64,128]{1,0:T(8,128)} %get-tuple-element.27), channel_id=1, source_target_pairs={{0,1},{2,3},{1,0},{3,2},{4,5},{6,7},{5,4},{7,6},{8,9},{10,11},{9,8... | collective-permute-start | bytes 98312 | tf_op jit(solution)/shard_map/ppermute | solution.py:610
  7.7 4.4 %collective-permute-start.3 = (f32[64,128]{1,0:T(8,128)}, f32[64,128]{1,0:T(8,128)S(1)}, u32[]{:S(2)}, u32[]{:S(2)}) collective-permute-start(f32[64,128]{1,0:T(8,128)} %get-tuple-element.28), channel_id=1, source_target_pairs={{1,2},{3,0},{2,1},{0,3},{5,6},{7,4},{6,5},{4,7},{9,10},{11,8},{10,... | collective-permute-start | bytes 98312 | tf_op jit(solution)/shard_map/ppermute | solution.py:611
  9.5 0.7 copy-start.2
  12.1 1.2 copy-start.1
  20.3 24.9 %all-to-all-start = ((bf16[128,8,256]{2,1,0:T(8,128)(2,1)}), bf16[128,8,256]{2,1,0:T(8,128)(2,1)S(1)}, u32[]{:S(2)}, u32[]{:S(2)}) async-start(bf16[128,8,256]{2,1,0:T(8,128)(2,1)} %bitcast.2), calls=%async_computation | async-start | bytes 1048576 | tf_op jit(solution)/shard_map/all_to_all | solution.py:577
  47.0 10.0 %collective-permute-start.5 = (bf16[1024,128]{1,0:T(8,128)(2,1)S(1)}, bf16[1024,128]{1,0:T(8,128)(2,1)S(1)}, u32[]{:S(2)}, u32[]{:S(2)}) collective-permute-start(bf16[1024,128]{1,0:T(8,128)(2,1)S(1)} %get-tuple-element.34.clustered_ref.own_ref), channel_id=1, source_target_pairs={{0,1},{1,2},{2,3},{3,4},{4,5},{5,6},{6,7},{7,8},{8,9},{9,10},{10,1... | collective-permute-start | bytes 786440 | tf_op jit(solution)/shard_map/ppermute | solution.py:621
  47.4 9.6 %collective-permute-start.4 = (bf16[1024,128]{1,0:T(8,128)(2,1)S(1)}, bf16[1024,128]{1,0:T(8,128)(2,1)S(1)}, u32[]{:S(2)}, u32[]{:S(2)}) collective-permute-start(bf16[1024,128]{1,0:T(8,128)(2,1)S(1)} %get-tuple-element.34.clustered_ref.own_ref), channel_id=1, source_target_pairs={{0,127},{1,0},{2,1},{3,2},{4,3},{5,4},{6,5},{7,6},{8,7},{9,8},{10,... | collective-permute-start | bytes 786440 | tf_op jit(solution)/shard_map/ppermute | solution.py:622
  56.5 10.7 %copy-start.3 = (s32[8,9]{1,0:T(8,128)S(1)}, s32[8,9]{1,0:T(8,128)}, u32[]{:S(2)}) copy-start(s32[8,9]{1,0:T(8,128)} %param.15) | copy-start | bytes 868
  57.0 75.0 %all-to-all-start.1 = ((bf16[128,80,256]{2,1,0:T(8,128)(2,1)}), bf16[128,80,256]{2,1,0:T(8,128)(2,1)}, u32[]{:S(2)}, u32[]{:S(2)}) async-start(bf16[128,80,256]{2,1,0:T(8,128)(2,1)} %shard_map.118), calls=%async_computation.1 | async-start | bytes 10485760 | tf_op jit(solution)/shard_map/all_to_all | solution.py:577
  132.0 22.7 %copy-start = (bf16[1024,2048]{1,0:T(8,128)(2,1)S(1)}, bf16[1024,2048]{1,0:T(8,128)(2,1)}, u32[]{:S(2)}) copy-start(bf16[1024,2048]{1,0:T(8,128)(2,1)} %get-tuple-element.43.hot_ref) | copy-start | bytes 12582916

commit v6 on v4

--- a/solution.py
+++ b/solution.py
@@ -498,8 +498,8 @@
                     values = turned[s * 64 : s * 64 + 64] * hit
                     masked[2 * s + part, pl.ds(cluster * 64, 64), at] = values
     basis = [big_ref[:, pl.ds(16 * n, 16), :].reshape(2048, CL) for n in range(4)]
-    for r in range(0, 512, 128):
-        at = pl.ds(r, 128)
+    for r in range(0, 512, 256):
+        at = pl.ds(r, 256)
         product = dot(masked[0, at, :], basis[0])
         for n in range(1, 4):
             product += dot(masked[n, at, :], basis[n])

time: 153 us -> 153 us (level)
  no operation moved by 1% of the time
where the time goes in v6:
time: 153 us; the launch traced here: 152 us
  waiting for transfers between devices  66.1 us (43%)
  Pallas kernels  43.3 us (28%)
  starting transfers between devices  24.6 us (16%)
  blocking collectives  15.1 us (10%)
  local copies, waits for them, and re-layouts  2.03 us (1%)
    all_to_all x2, waiting for transfers between devices, exchange(): return lax.all_to_all(x, BOTH, split_axis=0, concat_axis=0, tiled=True)  62.7 us
    all_to_all x2, starting transfers between devices, exchange(): return lax.all_to_all(x, BOTH, split_axis=0, concat_axis=0, tiled=True)  17.2 us
    all_to_all x1, blocking collectives, exchange(): return lax.all_to_all(x, BOTH, split_axis=0, concat_axis=0, tiled=True)  15.1 us
    pallas_call x1, Pallas kernels, near_product(): pl.pallas_call(near_kernel, out_shape=(jax.ShapeDtypeStruct((8, WAVES, CL...  11 us
    pallas_call x1, Pallas kernels, total_home(): call(total_kernel, jax.ShapeDtypeStruct((ROWS, 128), BF16), [VMEM, VMEM,...  7.63 us
    pallas_call x1, Pallas kernels, add_coeff(): pl.pallas_call(coeff_kernel, out_shape=jax.ShapeDtypeStruct((OWNERS, 80,...  6.44 us
    pallas_call x1, Pallas kernels, far_bucket(): call(bucket_kernel, jax.ShapeDtypeStruct((OWNERS, 80, CL), BF16), [SMEM,...  5.06 us
    pallas_call x1, Pallas kernels, surface_payload(): call(surface_kernel, (jax.ShapeDtypeStruct((WAVES, 16, 128), F32), jax.Sh...  4.84 us
  transfers between devices with their start and end apart: 8, of which 3 were waited for; matrix products, arithmetic and copies ran while one was open for 0% of the time, Pallas kernels for 16%

profile of v6, /device:TPU:1, one launch (start us, length us, event | category | flops | bytes accessed | tf_op | source)
XLA Modules:
  0.0 151.9 jit_solution(7776866005318231965)
XLA Ops:
  0.6 2.9 %shard_map.113 = (f32[32,64,128]{2,1,0:T(8,128)}, f32[40,128]{1,0:T(8,128)}, f32[4,64,128]{2,1,0:T(8,128)}, f32[4,64,128]{2,1,0:T(8,128)}, f32[64,128]{1,0:T(8,128)}, /*index=5*/f32[64,128]{1,0:T(8,128)}) custom-call(f32[64,16,128]{2,1,0:T(8,128)} %elevation_hbm.1, f32[64,16,128]{2,1,0:T(8,128)} %phi_hbm.1, s32[16,128]{1,0:T(8,128)} %slot_hbm.1, ...), custom_call_target="tpu_custom_call" | custom-call | tf_op jit(solution)/shard_map/pallas_call | solution.py:154
  3.6 1.5 collective-permute-start
  5.1 1.4 collective-permute-start.1
  6.4 1.2 collective-permute-start.2
  7.7 1.8 %collective-permute-start.3 = (f32[64,128]{1,0:T(8,128)}, f32[64,128]{1,0:T(8,128)S(1)}, u32[]{:S(2)}, u32[]{:S(2)}) collective-permute-start(f32[64,128]{1,0:T(8,128)} %get-tuple-element.27), channel_id=1, source_target_pairs={{1,2},{3,0},{2,1},{0,3},{5,6},{7,4},{6,5},{4,7},{9,10},{11,8},{10,... | collective-permute-start | bytes 98312 | tf_op jit(solution)/shard_map/ppermute | solution.py:604
  9.5 0.0 copy-start.2
  9.5 0.7 copy-done.2
  10.2 1.8 %shard_map.114 = (bf16[1024,2048]{1,0:T(8,128)(2,1)S(1)}, s32[8,2048]{1,0:T(8,128)S(1)}, s32[8,128]{1,0:T(8,128)S(1)}) custom-call(f32[40,128]{1,0:T(8,128)S(1)} %copy-done.2), custom_call_target="tpu_custom_call" | custom-call | tf_op jit(solution)/shard_map/pallas_call | solution.py:213
  12.0 0.0 collective-permute-done.2.across_a
  12.0 0.0 collective-permute-done.3.across_b
  12.0 0.0 collective-permute-done.along_a
  12.1 0.0 collective-permute-done.1.along_b
  12.1 0.0 copy-start.1
  12.1 1.2 copy-done.1
  13.3 4.8 %shard_map.115 = (f32[64,16,128]{2,1,0:T(8,128)}, bf16[1024,256]{1,0:T(8,128)(2,1)}) custom-call(f32[40,128]{1,0:T(8,128)S(1)} %copy-done.2, f32[32,64,128]{2,1,0:T(8,128)S(1)} %copy-done.1, f32[4,64,128]{2,1,0:T(8,128)S(1)} %collective-permute-done.along_a, f32[4,64,128]{2,1,0:T(8,128)S(1)} %collective-permute-done.1.along_b, ...), custom_call_target="tpu_custom_call" | custom-call | tf_op jit(solution)/shard_map/pallas_call | solution.py:314
  18.1 11.0 %all-to-all-start = ((bf16[128,8,256]{2,1,0:T(8,128)(2,1)}), bf16[128,8,256]{2,1,0:T(8,128)(2,1)S(1)}, u32[]{:S(2)}, u32[]{:S(2)}) async-start(bf16[128,8,256]{2,1,0:T(8,128)(2,1)} %bitcast.2), calls=%async_computation | async-start | bytes 1048576 | tf_op jit(solution)/shard_map/all_to_all | solution.py:570
  29.1 5.1 %shard_map.116.big_hbm = bf16[128,80,256]{2,1,0:T(8,128)(2,1)} custom-call(s32[1024]{0:T(1024)S(1)} %bitcast.10, bf16[128,32,256]{2,1,0:T(8,128)(2,1)} %u_hbm.1), custom_call_target="tpu_custom_call" | custom-call | bytes 9437184 | tf_op jit(solution)/shard_map/pallas_call | solution.py:71
  34.2 8.9 %all-to-all-done = bf16[128,8,256]{2,1,0:T(8,128)(2,1)S(1)} async-done(((bf16[128,8,256]{2,1,0:T(8,128)(2,1)}), bf16[128,8,256]{2,1,0:T(8,128)(2,1)S(1)}, u32[]{:S(2)}, u32[]{:S(2)}) %all-to-all-start) | async-done | bytes 524320 | tf_op jit(solution)/shard_map/all_to_all | solution.py:570
  43.1 1.7 %shard_map.117 = (bf16[1024,128]{1,0:T(8,128)(2,1)S(1)}, f32[8,1024]{1,0:T(8,128)S(1)}) custom-call(bf16[1024,256]{1,0:T(8,128)(2,1)S(1)} %bitcast.7), custom_call_target="tpu_custom_call" | custom-call | tf_op jit(solution)/shard_map/pallas_call | solution.py:357
  44.8 1.5 collective-permute-start.4
  46.3 0.1 collective-permute-start.5
  46.4 6.4 %shard_map.118 = bf16[128,80,256]{2,1,0:T(8,128)(2,1)} custom-call(s32[1024]{0:T(1024)S(1)} %bitcast.11, bf16[1024,128]{1,0:T(8,128)(2,1)S(1)} %get-tuple-element.34.clustered_ref.own_ref, bf16[128,32,256]{2,1,0:T(8,128)(2,1)} %v_hbm.1, bf16[128,80,256]{2,1,0:T(8,128)(2,1)} %shard_map.116.big_hbm), custom_call_target="tpu_custom_call", output_to_operand_aliasing={{}: (3, {})} | custom-call | bytes 33554432 | tf_op jit(solution)/shard_map/pallas_call | solution.py:410
  52.8 0.0 copy-start.3
  52.8 0.0 collective-permute-done.4.after_ref
  52.8 3.4 %collective-permute-done.5.before_ref = bf16[1024,128]{1,0:T(8,128)(2,1)S(1)} collective-permute-done((bf16[1024,128]{1,0:T(8,128)(2,1)S(1)}, bf16[1024,128]{1,0:T(8,128)(2,1)S(1)}, u32[]{:S(2)}, u32[]{:S(2)}) %collective-permute-start.5) | collective-permute-done | bytes 262176 | tf_op jit(solution)/shard_map/ppermute | solution.py:614
  56.3 6.2 %all-to-all-start.1 = ((bf16[128,80,256]{2,1,0:T(8,128)(2,1)}), bf16[128,80,256]{2,1,0:T(8,128)(2,1)}, u32[]{:S(2)}, u32[]{:S(2)}) async-start(bf16[128,80,256]{2,1,0:T(8,128)(2,1)} %shard_map.118), calls=%async_computation.1 | async-start | bytes 10485760 | tf_op jit(solution)/shard_map/all_to_all | solution.py:570
  62.5 0.0 copy-done.3
  62.6 0.1 reshape.33.rel_ref
  62.7 11.0 %shard_map.119 = (f32[8,64,256]{2,1,0:T(8,128)S(1)}, bf16[1024,2048]{1,0:T(8,128)(2,1)}) custom-call(s32[72]{0:T(128)S(1)} %reshape.33.rel_ref, bf16[1024,128]{1,0:T(8,128)(2,1)S(1)} %collective-permute-done.5.before_ref, bf16[1024,128]{1,0:T(8,128)(2,1)S(1)} %get-tuple-element.34.clustered_ref.own_ref, ...), custom_call_target="tpu_custom_call" | custom-call | bytes 536870912 | tf_op jit(solution)/shard_map/pallas_call | solution.py:464
  73.7 53.8 %all-to-all-done.1.big_ref = bf16[128,80,256]{2,1,0:T(8,128)(2,1)} async-done(((bf16[128,80,256]{2,1,0:T(8,128)(2,1)}), bf16[128,80,256]{2,1,0:T(8,128)(2,1)}, u32[]{:S(2)}, u32[]{:S(2)}) %all-to-all-start.1) | async-done | bytes 5242912 | tf_op jit(solution)/shard_map/all_to_all | solution.py:570
  127.5 0.0 copy-start
  127.5 7.6 %shard_map.120 = bf16[1024,128]{1,0:T(8,128)(2,1)S(1)} custom-call(bf16[128,80,256]{2,1,0:T(8,128)(2,1)} %all-to-all-done.1.big_ref, f32[8,64,256]{2,1,0:T(8,128)S(1)} %get-tuple-element.39.near_ref, f32[8,1024]{1,0:T(8,128)S(1)} %get-tuple-element.40.info_ref), custom_call_target="tpu_custom_call" | custom-call | tf_op jit(solution)/shard_map/pallas_call | solution.py:530
  135.1 15.1 %all_to_all.15 = bf16[128,8,128]{2,1,0:T(8,128)(2,1)S(1)} all-to-all(bf16[128,8,128]{2,1,0:T(8,128)(2,1)S(1)} %bitcast.9), channel_id=1, replica_groups=mesh['along'=32,'across'=4] {'along','across'}, dimensions={0} | all-to-all | bytes 524288 | tf_op jit(solution)/shard_map/all_to_all | solution.py:570
  150.2 0.0 copy-done
  150.2 1.8 %shard_map.121 = bf16[64,16,128]{2,1,0:T(8,128)(2,1)} custom-call(bf16[1024,128]{1,0:T(8,128)(2,1)S(1)} %bitcast.8, bf16[1024,2048]{1,0:T(8,128)(2,1)S(1)} %copy-done, s32[8,2048]{1,0:T(8,128)S(1)} %get-tuple-element.29.place_ref), custom_call_target="tpu_custom_call" | custom-call | tf_op jit(solution)/shard_map/pallas_call | solution.py:560
  (1 shorter events, 0.0 us)
Async XLA Ops:
  3.6 8.5 %collective-permute-start = (f32[4,64,128]{2,1,0:T(8,128)}, f32[4,64,128]{2,1,0:T(8,128)S(1)}, u32[]{:S(2)}, u32[]{:S(2)}) collective-permute-start(f32[4,64,128]{2,1,0:T(8,128)} %get-tuple-element.24), channel_id=1, source_target_pairs={{0,4},{8,12},{16,20},{24,28},{32,36},{40,44},{48,52},{56,60},{64,6... | collective-permute-start | bytes 393224 | tf_op jit(solution)/shard_map/ppermute | solution.py:601
  5.1 7.0 %collective-permute-start.1 = (f32[4,64,128]{2,1,0:T(8,128)}, f32[4,64,128]{2,1,0:T(8,128)S(1)}, u32[]{:S(2)}, u32[]{:S(2)}) collective-permute-start(f32[4,64,128]{2,1,0:T(8,128)} %get-tuple-element.25), channel_id=1, source_target_pairs={{4,8},{12,16},{20,24},{28,32},{36,40},{44,48},{52,56},{60,64},{68,... | collective-permute-start | bytes 393224 | tf_op jit(solution)/shard_map/ppermute | solution.py:602
  6.4 5.6 %collective-permute-start.2 = (f32[64,128]{1,0:T(8,128)}, f32[64,128]{1,0:T(8,128)S(1)}, u32[]{:S(2)}, u32[]{:S(2)}) collective-permute-start(f32[64,128]{1,0:T(8,128)} %get-tuple-element.26), channel_id=1, source_target_pairs={{0,1},{2,3},{1,0},{3,2},{4,5},{6,7},{5,4},{7,6},{8,9},{10,11},{9,8... | collective-permute-start | bytes 98312 | tf_op jit(solution)/shard_map/ppermute | solution.py:603
  7.7 4.4 %collective-permute-start.3 = (f32[64,128]{1,0:T(8,128)}, f32[64,128]{1,0:T(8,128)S(1)}, u32[]{:S(2)}, u32[]{:S(2)}) collective-permute-start(f32[64,128]{1,0:T(8,128)} %get-tuple-element.27), channel_id=1, source_target_pairs={{1,2},{3,0},{2,1},{0,3},{5,6},{7,4},{6,5},{4,7},{9,10},{11,8},{10,... | collective-permute-start | bytes 98312 | tf_op jit(solution)/shard_map/ppermute | solution.py:604
  9.5 0.7 copy-start.2
  12.1 1.2 copy-start.1
  18.1 24.9 %all-to-all-start = ((bf16[128,8,256]{2,1,0:T(8,128)(2,1)}), bf16[128,8,256]{2,1,0:T(8,128)(2,1)S(1)}, u32[]{:S(2)}, u32[]{:S(2)}) async-start(bf16[128,8,256]{2,1,0:T(8,128)(2,1)} %bitcast.2), calls=%async_computation | async-start | bytes 1048576 | tf_op jit(solution)/shard_map/all_to_all | solution.py:570
  44.8 8.0 %collective-permute-start.4 = (bf16[1024,128]{1,0:T(8,128)(2,1)S(1)}, bf16[1024,128]{1,0:T(8,128)(2,1)S(1)}, u32[]{:S(2)}, u32[]{:S(2)}) collective-permute-start(bf16[1024,128]{1,0:T(8,128)(2,1)S(1)} %get-tuple-element.34.clustered_ref.own_ref), channel_id=1, source_target_pairs={{0,127},{1,0},{2,1},{3,2},{4,3},{5,4},{6,5},{7,6},{8,7},{9,8},{10,... | collective-permute-start | bytes 786440 | tf_op jit(solution)/shard_map/ppermute | solution.py:615
  46.3 10.0 %collective-permute-start.5 = (bf16[1024,128]{1,0:T(8,128)(2,1)S(1)}, bf16[1024,128]{1,0:T(8,128)(2,1)S(1)}, u32[]{:S(2)}, u32[]{:S(2)}) collective-permute-start(bf16[1024,128]{1,0:T(8,128)(2,1)S(1)} %get-tuple-element.34.clustered_ref.own_ref), channel_id=1, source_target_pairs={{0,1},{1,2},{2,3},{3,4},{4,5},{5,6},{6,7},{7,8},{8,9},{9,10},{10,1... | collective-permute-start | bytes 786440 | tf_op jit(solution)/shard_map/ppermute | solution.py:614
  52.8 9.7 %copy-start.3 = (s32[8,9]{1,0:T(8,128)S(1)}, s32[8,9]{1,0:T(8,128)}, u32[]{:S(2)}) copy-start(s32[8,9]{1,0:T(8,128)} %param.15) | copy-start | bytes 868
  56.3 71.2 %all-to-all-start.1 = ((bf16[128,80,256]{2,1,0:T(8,128)(2,1)}), bf16[128,80,256]{2,1,0:T(8,128)(2,1)}, u32[]{:S(2)}, u32[]{:S(2)}) async-start(bf16[128,80,256]{2,1,0:T(8,128)(2,1)} %shard_map.118), calls=%async_computation.1 | async-start | bytes 10485760 | tf_op jit(solution)/shard_map/all_to_all | solution.py:570
  127.5 22.7 %copy-start = (bf16[1024,2048]{1,0:T(8,128)(2,1)S(1)}, bf16[1024,2048]{1,0:T(8,128)(2,1)}, u32[]{:S(2)}) copy-start(bf16[1024,2048]{1,0:T(8,128)(2,1)} %get-tuple-element.41.hot_ref) | copy-start | bytes 12582916
